TPU v7x, 32 devices: a whole 2x2x4 slice. The times are simulated.
32 devices in a mesh: parts: 2 (over y), req: 8 (over z, x), tp: 2 (over core).
Axes of the slice: x: 2, y: 2, z: 4, core: 2. Of those that a mesh axis runs over, the one named last changes fastest.
Arguments:
- counts: int32 [16], P('parts'), parts along dimension 0, may hold values from 1 to 2, as said below
- move_plan: int32 [32], P('parts'), parts along dimension 0, may hold values from 0 to 15, as said below
- ssm_state: float32 [32, 128, 4096], P(('parts', 'req'), 'tp'), parts along dimension 0, may hold values from -6 to 6
- conv_x_state: bfloat16 [32, 3, 8192], P(('parts', 'req'), None, 'tp'), parts along dimension 0, may hold values from -6 to 6
- conv_bc_state: bfloat16 [32, 3, 4, 128], P(('parts', 'req'), None, 'tp'), parts along dimension 0, may hold values from -6 to 6
- x_in: bfloat16 [32, 4, 8192], P(('parts', 'req'), None, 'tp'), parts along dimension 0, may hold values from -6 to 6
- bc_in: bfloat16 [32, 4, 4, 128], P(('parts', 'req'), None, 'tp'), parts along dimension 0, may hold values from -6 to 6
- z_in: bfloat16 [32, 4, 8192], P(('parts', 'req'), None, 'tp'), parts along dimension 0, may hold values from -6 to 6
- dt_in: float32 [32, 4, 128], P(('parts', 'req'), None, 'tp'), parts along dimension 0, may hold values from -1.5 to 1.5
- conv_w_x: float32 [4, 8192], P(None, 'tp'), may hold values from -3 to 3
- conv_b_x: float32 [8192], P('tp'), may hold values from -3 to 3
- conv_w_bc: float32 [4, 4, 128], P(None, 'tp'), may hold values from -3 to 3
- conv_b_bc: float32 [4, 128], P('tp'), may hold values from -3 to 3
- dt_bias: float32 [128], P('tp'), may hold values from -4 to -1
- a_log: float32 [128], P('tp'), may hold values from -2.5 to -0.5
- d_skip: float32 [128], P('tp'), may hold values from 0.3 to 1.5
- norm_w: float32 [8192], P('tp'), may hold values from 0.1 to 1.9
Outputs:
- y_out: bfloat16 [32, 4, 8192], P(('parts', 'req'), None, 'tp'), parts along dimension 0
- new_ssm: float32 [32, 128, 4096], P(('parts', 'req'), 'tp'), parts along dimension 0
- new_conv_x: bfloat16 [32, 3, 8192], P(('parts', 'req'), None, 'tp'), parts along dimension 0
- new_conv_bc: bfloat16 [32, 3, 4, 128], P(('parts', 'req'), None, 'tp'), parts along dimension 0
There are 2 independent parts, one for each index of `parts`. A program takes and returns all parts, laid end to end along the dimension named above; an argument that names none is the same for every part. Nothing has to cross between parts.
Inputs may be any that keep to these rules, and one draw needn't show every extreme that they name: `counts`: at least 1; every draw has owners with 2 live requests. `move_plan`: A destination slot is owner times 2 plus a local slot. Entries of slots that are not live are meaningless. Live requests have distinct destinations. An owner sends at most 1 live requests to other owners and receives at most 1 from other owners, and keeps at most 1 of its own; both bounds are reached in every draw, and some owner has all 2 destination slots taken.
All inputs are finite; a program needn't handle non-finite values.
Results may differ from a plain program's by a relative error of at most 0.001.
Values may be sent and summed in bfloat16 or wider, within the bound.
No kernel may reach another device: no remote copies, remote signals or barrier semaphores. Data moves between devices by JAX's collectives and lax.ppermute only.
A program may use at most 128 MiB of HBM per device.

v0:
```python
import jax
import jax.numpy as jnp
from jax import lax
from jax.sharding import PartitionSpec as P

H = 128
P_SIZE = 64


def on_device(
    counts,
    move_plan,
    ssm_state,
    conv_x_state,
    conv_bc_state,
    x_in,
    bc_in,
    z_in,
    dt_in,
    conv_w_x,
    conv_b_x,
    conv_w_bc,
    conv_b_bc,
    dt_bias,
    a_log,
    d_skip,
    norm_w,
):
    owners = lax.axis_size("req")
    owner = lax.axis_index("req")
    slots, heads_loc, columns = ssm_state.shape
    places, steps, channels = x_in.shape
    groups_loc = conv_bc_state.shape[2]
    pair = conv_bc_state.shape[3]
    state_size = pair // 2
    head_dim = channels // heads_loc
    reqs = move_plan.shape[0]
    ids = jnp.arange(reqs, dtype=jnp.int32)
    home = ids // slots
    live = ids % slots < jnp.take(counts, home)
    conv_flat = jnp.concatenate(
        [conv_x_state.reshape(slots, -1), conv_bc_state.reshape(slots, -1)], 1
    )
    conv_width = conv_flat.shape[1]
    zero_conv = jnp.zeros((), jnp.bfloat16)
    spread_state = lax.all_to_all(
        ssm_state.reshape(slots, owners, -1), "req", split_axis=1, concat_axis=0, tiled=True
    )
    spread_conv = lax.all_to_all(
        conv_flat.reshape(slots, owners, -1), "req", split_axis=1, concat_axis=0, tiled=True
    )
    targets = jnp.arange(owners * places, dtype=jnp.int32)
    match = live[None, :] & (move_plan[None, :] == targets[:, None])
    source = jnp.sum(jnp.where(match, ids[None, :], 0), axis=1)
    hit = jnp.any(match, axis=1)
    keep = hit.astype(jnp.float32)
    picked_state = jnp.take(spread_state, source, axis=0) * keep[:, None, None]
    picked_conv = jnp.where(hit[:, None, None], jnp.take(spread_conv, source, axis=0), zero_conv)
    arrived_state = lax.all_to_all(picked_state, "req", split_axis=0, concat_axis=1, tiled=True)
    arrived_conv = lax.all_to_all(picked_conv, "req", split_axis=0, concat_axis=1, tiled=True)
    state = arrived_state.reshape(places, heads_loc, columns)
    conv = arrived_conv.reshape(places, conv_width)
    mask = lax.dynamic_slice_in_dim(keep, owner * places, places)
    conv_x = conv[:, : 3 * channels].reshape(places, 3, channels)
    conv_bc = conv[:, 3 * channels :].reshape(places, 3, groups_loc, pair)
    per_group = heads_loc // groups_loc
    rate = jnp.exp(a_log)
    status = state.reshape(places, heads_loc, head_dim, state_size)
    scaling = 1.0 / (H * P_SIZE)
    outputs = []
    for step in range(steps):
        x_new = x_in[:, step]
        window = jnp.concatenate([conv_x, x_new[:, None]], 1).astype(jnp.float32)
        xconv = jax.nn.silu(jnp.sum(window * conv_w_x[None], axis=1) + conv_b_x)
        conv_x = jnp.concatenate([conv_x[:, 1:], x_new[:, None]], 1)
        bc_new = bc_in[:, step]
        bwindow = jnp.concatenate([conv_bc, bc_new[:, None]], 1).astype(jnp.float32)
        bconv = jax.nn.silu(jnp.sum(bwindow * conv_w_bc[None], axis=1) + conv_b_bc)
        conv_bc = jnp.concatenate([conv_bc[:, 1:], bc_new[:, None]], 1)
        b_head = jnp.repeat(bconv[..., :state_size], per_group, axis=1)
        c_head = jnp.repeat(bconv[..., state_size:], per_group, axis=1)
        delta = jax.nn.softplus(dt_in[:, step] + dt_bias)
        decay = jnp.exp(-delta * rate)
        heads_x = xconv.reshape(places, heads_loc, head_dim)
        status = (
            decay[:, :, None, None] * status
            + (delta[:, :, None] * heads_x)[..., None] * b_head[:, :, None, :]
        )
        mixed = jnp.sum(status * c_head[:, :, None, :], axis=-1) + d_skip[None, :, None] * heads_x
        gated = mixed.reshape(places, channels) * jax.nn.silu(z_in[:, step].astype(jnp.float32))
        total = lax.psum(jnp.sum(gated * gated, axis=-1), "tp")
        outputs.append(gated * lax.rsqrt(total * scaling + 1e-05)[:, None] * norm_w)
    normed = jnp.stack(outputs, 1)
    y_out = (normed * mask[:, None, None]).astype(jnp.bfloat16)
    new_ssm = status.reshape(places, heads_loc, columns) * mask[:, None, None]
    filled = mask > 0.5
    new_conv_x = jnp.where(filled[:, None, None], conv_x, jnp.zeros_like(conv_x))
    new_conv_bc = jnp.where(filled[:, None, None, None], conv_bc, jnp.zeros_like(conv_bc))
    return (y_out, new_ssm, new_conv_x, new_conv_bc)


def solution(mesh):
    in_specs = (
        P("parts"),
        P("parts"),
        P(("parts", "req"), "tp", None),
        P(("parts", "req"), None, "tp"),
        P(("parts", "req"), None, "tp", None),
        P(("parts", "req"), None, "tp"),
        P(("parts", "req"), None, "tp", None),
        P(("parts", "req"), None, "tp"),
        P(("parts", "req"), None, "tp"),
        P(None, "tp"),
        P("tp"),
        P(None, "tp", None),
        P("tp", None),
        P("tp"),
        P("tp"),
        P("tp"),
        P("tp"),
    )
    out_specs = (
        P(("parts", "req"), None, "tp"),
        P(("parts", "req"), "tp", None),
        P(("parts", "req"), None, "tp"),
        P(("parts", "req"), None, "tp", None),
    )
    return jax.shard_map(
        on_device, mesh=mesh, in_specs=in_specs, out_specs=out_specs, check_vma=False
    )
```

profile of v0, /device:TPU:0, one launch (start us, length us, event | category | flops | bytes accessed | tf_op | source)
XLA Modules:
  0.0 195.3 jit_solution(5956617972472375227)
XLA Ops:
  3.0 7.3 %all-to-all-start.2 = ((bf16[2,8,1632]{2,0,1:T(2,128)(2,1)}), bf16[2,8,1632]{2,0,1:T(2,128)(2,1)S(1)}, u32[]{:S(2)}, u32[]{:S(2)}) async-start(bf16[2,8,1632]{2,0,1:T(2,128)(2,1)} %copy.107), calls=%async_computation.2 | async-start | bytes 106496 | tf_op jit(solution)/shard_map/all_to_all | solution.py:49
  12.6 4.5 %all-to-all-done.2 = bf16[2,8,1632]{2,0,1:T(2,128)(2,1)S(1)} async-done(((bf16[2,8,1632]{2,0,1:T(2,128)(2,1)}), bf16[2,8,1632]{2,0,1:T(2,128)(2,1)S(1)}, u32[]{:S(2)}, u32[]{:S(2)}) %all-to-all-start.2) | async-done | bytes 52256 | tf_op jit(solution)/shard_map/all_to_all | solution.py:49
  19.7 3.3 %all-to-all-start.3 = ((bf16[8,2,1632]{2,1,0:T(2,128)(2,1)}), bf16[8,2,1632]{2,1,0:T(2,128)(2,1)S(1)}, u32[]{:S(2)}, u32[]{:S(2)}) async-start(bf16[8,2,1632]{2,1,0:T(2,128)(2,1)} %reshape.1103), calls=%async_computation.3 | async-start | bytes 106496 | tf_op jit(solution)/shard_map/all_to_all | solution.py:60
  23.0 1.8 reshape.1061
  24.8 2.9 %copy.104 = f32[2,8,32768]{2,0,1:T(2,128)} copy(f32[2,8,32768]{2,1,0:T(8,128)S(1)} %reshape.1061) | data formatting | bytes 4194304 | tf_op jit(solution)/shard_map/reshape | solution.py:47
  27.8 2.0 %all-to-all-done.3 = bf16[8,2,1632]{2,1,0:T(2,128)(2,1)S(1)} async-done(((bf16[8,2,1632]{2,1,0:T(2,128)(2,1)}), bf16[8,2,1632]{2,1,0:T(2,128)(2,1)S(1)}, u32[]{:S(2)}, u32[]{:S(2)}) %all-to-all-start.3) | async-done | bytes 52256 | tf_op jit(solution)/shard_map/all_to_all | solution.py:60
  29.8 4.1 %all-to-all-start = ((f32[2,8,32768]{2,0,1:T(2,128)}), f32[2,8,32768]{2,0,1:T(2,128)S(1)}, u32[]{:S(2)}, u32[]{:S(2)}) async-start(f32[2,8,32768]{2,0,1:T(2,128)} %copy.104), calls=%async_computation | async-start | bytes 4194304 | tf_op jit(solution)/shard_map/all_to_all | solution.py:46
  35.4 45.1 %all-to-all-done = f32[2,8,32768]{2,0,1:T(2,128)S(1)} async-done(((f32[2,8,32768]{2,0,1:T(2,128)}), f32[2,8,32768]{2,0,1:T(2,128)S(1)}, u32[]{:S(2)}, u32[]{:S(2)}) %all-to-all-start) | async-done | bytes 2097184 | tf_op jit(solution)/shard_map/all_to_all | solution.py:46
  81.9 2.7 %reshape.1080 = f32[16,32768]{1,0:T(8,128)S(1)} reshape(f32[8,2,1,32768]{3,1,0,2:T(2,128)} %bitcast.161) | data formatting | bytes 4194304 | tf_op jit(solution)/shard_map/all_to_all | solution.py:46
  84.6 2.4 %gather_fusion.1 = f32[16,32768]{1,0:T(8,128)} fusion(f32[16,32768]{1,0:T(8,128)S(1)} %reshape.1080, s32[1024]{0:T(1024)S(1)} %pad_clamp_fusion), kind=kCustom, calls=%fused_computation.1 | custom fusion | bytes 4194368 | tf_op jit(solution)/shard_map/jit(_take)/gather | solution.py:57
  87.0 1.8 fusion
  88.8 3.5 %copy.105 = f32[16,1,32768]{2,1,0:T(1,128)} copy(f32[16,1,32768]{2,0,1:T(8,128)S(1)} %fusion) | data formatting | bytes 4194304 | tf_op jit(solution)/shard_map/mul | solution.py:57
  92.3 3.9 %all-to-all-start.1 = ((f32[16,1,32768]{2,1,0:T(1,128)}), f32[16,1,32768]{2,1,0:T(1,128)S(1)}, u32[]{:S(2)}, u32[]{:S(2)}) async-start(f32[16,1,32768]{2,1,0:T(1,128)} %copy.105), calls=%async_computation.1 | async-start | bytes 4194304 | tf_op jit(solution)/shard_map/all_to_all | solution.py:59
  99.4 44.9 %all-to-all-done.1 = f32[16,1,32768]{2,1,0:T(1,128)S(1)} async-done(((f32[16,1,32768]{2,1,0:T(1,128)}), f32[16,1,32768]{2,1,0:T(1,128)S(1)}, u32[]{:S(2)}, u32[]{:S(2)}) %all-to-all-start.1) | async-done | bytes 2097184 | tf_op jit(solution)/shard_map/all_to_all | solution.py:59
  145.7 2.8 %copy.130 = f32[8,2,1,32768]{3,0,1,2:T(8,128)S(1)} copy(f32[8,2,1,32768]{3,2,1,0:T(1,128)} %bitcast.160) | data formatting | bytes 4194304 | tf_op jit(solution)/shard_map/all_to_all | solution.py:59
  148.5 3.0 %reshape_reshape.5 = f32[2,64,64,64]{3,2,1,0:T(8,128)} reshape(f32[2,8,1,32768]{3,1,0,2:T(8,128)S(1)} %bitcast.158) | data formatting | bytes 4194304 | tf_op jit(solution)/shard_map/reshape;reshape | solution.py:68
  151.6 13.2 %multiply_reduce_fusion.1 = (f32[2,64,64]{2,1,0:T(8,128)S(1)}, f32[2,64,64]{2,1,0:T(8,128)S(1)}, f32[2,64,64]{2,1,0:T(8,128)S(1)}, f32[2,64,64]{2,1,0:T(8,128)S(...) fusion(f32[2,64,64]{2,1,0:T(8,128)S(1)} %bitcast.162, ...), kind=kLoop, calls=%fused_computation.4 | loop fusion | flops 10452992 | bytes 11012096 | tf_op jit(solution)/shard_map/reduce_sum | solution.py:89
  165.7 1.6 reshape_reshape.6
  167.7 2.5 %all-reduce = (f32[2]{0:T(128)S(1)}, f32[2]{0:T(128)S(1)}, f32[2]{0:T(128)S(1)}, f32[2]{0:T(128)S(1)}) all-reduce(f32[2]{0:T(128)S(1)} %get-tuple-element.35, f32[2]{0:T(128)S(1)} %get-tuple-element.34, f32[2]{0:T(128)S(1)} %get-tuple-element.33, f32[2]{0:T(128)S(1)} %get-tuple-element.32), channel_id=1, replica_groups=mesh['parts'=2,'req'=8,'tp'=2] {'tp'}, use_global_device_ids=true, to_apply=%region_21.22 | all-reduce | flops 8 | bytes 64 | tf_op jit(solution)/shard_map/psum | solution.py:91
  171.3 3.5 %mul.869 = f32[2,64,4096]{2,1,0:T(8,128)S(1)} reshape(f32[2,64,64,64]{3,2,1,0:T(8,128)} %get-tuple-element.57) | data formatting | bytes 4194304 | tf_op jit(solution)/shard_map/mul | solution.py:87
  174.8 4.8 %mul.867 = f32[2,64,4096]{2,1,0:T(8,128)} reshape(f32[2,64,64,64]{3,2,1,0:T(8,128)} %get-tuple-element.56) | data formatting | bytes 4194304 | tf_op jit(solution)/shard_map/mul | solution.py:87
  179.6 4.8 %mul.865 = f32[2,64,4096]{2,1,0:T(8,128)} reshape(f32[2,64,64,64]{3,2,1,0:T(8,128)} %get-tuple-element.55) | data formatting | bytes 4194304 | tf_op jit(solution)/shard_map/mul | solution.py:87
  184.4 4.8 %mul.863 = f32[2,64,4096]{2,1,0:T(8,128)} reshape(f32[2,64,64,64]{3,2,1,0:T(8,128)} %get-tuple-element.54) | data formatting | bytes 4194304 | tf_op jit(solution)/shard_map/mul | solution.py:87
  189.1 6.1 %add_multiply_fusion = f32[2,64,4096]{2,1,0:T(8,128)} fusion(f32[2,64,4096]{2,1,0:T(8,128)S(1)} %mul.869, f32[2,64,4096]{2,1,0:T(8,128)} %mul.867, f32[2,64,4096]{2,1,0:T(8,128)} %mul.865, f32[2,64,4096]{2,1,0:T(8,128)} %mul.863, f32[2,64,4096]{2,1,0:T(8,128)} %reshape_reshape.6, f32[2]{0:T(128)S(1)} %get-tuple-element.45, ...), kind=kLoop, calls=%fused_computation.13 | loop fusion | flops 4718592 | bytes 12584968 | tf_op jit(solution)/shard_map/mul | solution.py:95
  (114 shorter events, 16.8 us)
Async XLA Ops:
  0.6 9.7 %copy-start = (s32[8]{0:T(128)S(1)}, s32[8]{0:T(128)}, u32[]{:S(2)}) copy-start(s32[8]{0:T(128)} %param.17) | copy-start | bytes 100
  3.0 14.1 %all-to-all-start.2 = ((bf16[2,8,1632]{2,0,1:T(2,128)(2,1)}), bf16[2,8,1632]{2,0,1:T(2,128)(2,1)S(1)}, u32[]{:S(2)}, u32[]{:S(2)}) async-start(bf16[2,8,1632]{2,0,1:T(2,128)(2,1)} %copy.107), calls=%async_computation.2 | async-start | bytes 106496 | tf_op jit(solution)/shard_map/all_to_all | solution.py:49
  19.7 10.1 %all-to-all-start.3 = ((bf16[8,2,1632]{2,1,0:T(2,128)(2,1)}), bf16[8,2,1632]{2,1,0:T(2,128)(2,1)S(1)}, u32[]{:S(2)}, u32[]{:S(2)}) async-start(bf16[8,2,1632]{2,1,0:T(2,128)(2,1)} %reshape.1103), calls=%async_computation.3 | async-start | bytes 106496 | tf_op jit(solution)/shard_map/all_to_all | solution.py:60
  27.7 6.2 %copy-start.14 = (f32[64]{0:T(128)S(1)}, f32[64]{0:T(128)}, u32[]{:S(2)}) copy-start(f32[64]{0:T(128)} %param.31) | copy-start | bytes 772
  27.7 6.2 %copy-start.5 = (f32[4096]{0:T(1024)S(1)}, f32[4096]{0:T(1024)}, u32[]{:S(2)}) copy-start(f32[4096]{0:T(1024)} %param.27) | copy-start | bytes 49156
  27.7 6.3 %copy-start.12 = (f32[64]{0:T(128)S(1)}, f32[64]{0:T(128)}, u32[]{:S(2)}) copy-start(f32[64]{0:T(128)} %param.32) | copy-start | bytes 772
  27.7 6.5 %copy-start.7 = (bf16[2,4,2,128]{3,2,1,0:T(2,128)(2,1)S(1)}, bf16[2,4,2,128]{3,2,1,0:T(2,128)(2,1)}, u32[]{:S(2)}) copy-start(bf16[2,4,2,128]{3,2,1,0:T(2,128)(2,1)} %param.23) | copy-start | bytes 12292
  27.7 6.5 %copy-start.10 = (f32[2,4,64]{2,1,0:T(4,128)S(1)}, f32[2,4,64]{2,1,0:T(4,128)}, u32[]{:S(2)}) copy-start(f32[2,4,64]{2,1,0:T(4,128)} %param.25) | copy-start | bytes 6148
  27.8 6.5 %copy-start.13 = (f32[64]{0:T(128)S(1)}, f32[64]{0:T(128)}, u32[]{:S(2)}) copy-start(f32[64]{0:T(128)} %param.30) | copy-start | bytes 772
  27.8 6.5 %copy-start.3 = (bf16[2,4,4096]{2,1,0:T(4,128)(2,1)S(1)}, bf16[2,4,4096]{2,1,0:T(4,128)(2,1)}, u32[]{:S(2)}) copy-start(bf16[2,4,4096]{2,1,0:T(4,128)(2,1)} %param.22) | copy-start | bytes 196612
  27.8 6.6 %copy-start.4 = (bf16[2,4,4096]{2,1,0:T(4,128)(2,1)S(1)}, bf16[2,4,4096]{2,1,0:T(4,128)(2,1)}, u32[]{:S(2)}) copy-start(bf16[2,4,4096]{2,1,0:T(4,128)(2,1)} %param.24) | copy-start | bytes 196612
  29.8 50.8 %all-to-all-start = ((f32[2,8,32768]{2,0,1:T(2,128)}), f32[2,8,32768]{2,0,1:T(2,128)S(1)}, u32[]{:S(2)}, u32[]{:S(2)}) async-start(f32[2,8,32768]{2,0,1:T(2,128)} %copy.104), calls=%async_computation | async-start | bytes 4194304 | tf_op jit(solution)/shard_map/all_to_all | solution.py:46
  80.5 1.3 copy-start.2
  92.3 4.1 %copy-start.6 = (f32[4,4096]{1,0:T(4,128)S(1)}, f32[4,4096]{1,0:T(4,128)}, u32[]{:S(2)}) copy-start(f32[4,4096]{1,0:T(4,128)} %param.26) | copy-start | bytes 196612
  92.3 6.0 %copy-start.9 = (f32[4,2,128]{2,1,0:T(2,128)S(1)}, f32[4,2,128]{2,1,0:T(2,128)}, u32[]{:S(2)}) copy-start(f32[4,2,128]{2,1,0:T(2,128)} %param.28) | copy-start | bytes 12292
  92.3 6.7 %copy-start.11 = (f32[2,128]{1,0:T(2,128)S(1)}, f32[2,128]{1,0:T(2,128)}, u32[]{:S(2)}) copy-start(f32[2,128]{1,0:T(2,128)} %param.29) | copy-start | bytes 3076
  92.3 52.1 %all-to-all-start.1 = ((f32[16,1,32768]{2,1,0:T(1,128)}), f32[16,1,32768]{2,1,0:T(1,128)S(1)}, u32[]{:S(2)}, u32[]{:S(2)}) async-start(f32[16,1,32768]{2,1,0:T(1,128)} %copy.105), calls=%async_computation.1 | async-start | bytes 4194304 | tf_op jit(solution)/shard_map/all_to_all | solution.py:59
  144.4 1.3 copy-start.1
  165.6 4.5 %copy-start.8 = (f32[4096]{0:T(1024)S(1)}, f32[4096]{0:T(1024)}, u32[]{:S(2)}) copy-start(f32[4096]{0:T(1024)} %param.33) | copy-start | bytes 49156
where the time goes:
time: 196 us; the launch traced here: 195 us
  waiting for transfers between devices  96.6 us (49%)
  local copies, waits for them, and re-layouts  48.9 us (25%)
  other arithmetic  27.6 us (14%)
  starting transfers between devices  18.6 us (9%)
  blocking collectives  2.46 us (1%)
    all_to_all x1, waiting for transfers between devices, on_device(): lax.all_to_all(ssm_state.reshape(slots, owners, -1), 'req', split_axis=1,...  45.1 us
    all_to_all x1, waiting for transfers between devices, on_device(): lax.all_to_all(picked_state, 'req', split_axis=0, concat_axis=1, tiled=True)  44.9 us
    mul x4, local copies, waits for them, and re-layouts, on_device(): (delta[:, :, None] * heads_x)[..., None] * b_head[:, :, None, :]  17.8 us
    reduce_sum x1, other arithmetic, on_device(): jnp.sum(status * c_head[:, :, None, :], axis=-1)  13.2 us
    all_to_all x1, starting transfers between devices, on_device(): lax.all_to_all(conv_flat.reshape(slots, owners, -1), 'req', split_axis=1,...  7.25 us
    mul x1, other arithmetic, on_device(): new_ssm = status.reshape(places, heads_loc, columns) * mask[:, None, None]  6.13 us
    unnamed x34, local copies, waits for them, and re-layouts  4.76 us
    reshape x2, local copies, waits for them, and re-layouts, on_device(): ssm_state.reshape(slots, owners, -1)  4.69 us
  transfers between devices with their start and end apart: 4, of which 4 were waited for; matrix products, arithmetic and copies ran while one was open for 6% of the time, Pallas kernels for 0%

commit v1 on v0

v1 whole, which is shorter than its diff:
```python
import jax
import jax.numpy as jnp
from jax import lax
from jax.experimental import pallas as pl
from jax.experimental.pallas import tpu as pltpu
from jax.sharding import PartitionSpec as P

H = 128
P_SIZE = 64
LANES = 128
AUX = 16
REACH = 6.0
LEVELS = 32767.0
VMEM_LIMIT = 48 * 1024 * 1024


def level_code(top):
    code = jnp.floor(-8.0 / jnp.log(2.0) * jnp.log(jnp.maximum(top, 1e-30) / REACH) - 0.01)
    return jnp.clip(code, 0.0, 800.0)


def level_scale(code):
    return REACH * jnp.exp(code * (-0.125 * jnp.log(2.0)))


def moving_slot(counts_ref, plan_ref, me_ref, slots):
    me = me_ref[0]
    slot = jnp.int32(0)
    for local in range(1, slots):
        live = local < counts_ref[me]
        away = plan_ref[me * slots + local] // slots != me
        slot = jnp.where(live & away, local, slot)
    return slot


def pack_kernel(counts_ref, plan_ref, me_ref, state_ref, cx_ref, cb_ref, out_ref, rows_ref):
    heads, columns = state_ref.shape[1:]
    owners, piece, _ = out_ref.shape
    share = piece - AUX
    top = jnp.abs(state_ref[0, :, :LANES])
    for j in range(1, columns // LANES):
        top = jnp.maximum(top, jnp.abs(state_ref[0, :, j * LANES : (j + 1) * LANES]))
    code = level_code(jnp.max(top, axis=1, keepdims=True))
    factor = LEVELS / level_scale(code)
    run = min(share, heads)
    for j in range(columns // LANES):
        tile = state_ref[0, :, j * LANES : (j + 1) * LANES] * factor
        tile = jnp.round(tile).astype(jnp.int32).astype(jnp.int16)
        for at in range(0, heads, run):
            flat = j * heads + at
            out_ref[flat // share, flat % share : flat % share + run, :] = tile[at : at + run]
    taps, channels = cx_ref.shape[1:]
    groups = cb_ref.shape[2]
    blocks = channels // LANES
    cx = cx_ref[0].astype(jnp.float32)
    cb = cb_ref[0].astype(jnp.float32)
    code_x = level_code(jnp.max(jnp.abs(cx)).reshape(1, 1))
    code_b = level_code(jnp.max(jnp.abs(cb)).reshape(1, 1))
    for b in range(blocks):
        rows_ref[pl.ds(b, taps, stride=blocks), :] = cx[:, b * LANES : (b + 1) * LANES]
    last = taps * blocks
    rows_ref[last:, :] = jnp.zeros((rows_ref.shape[0] - last, LANES), jnp.float32)
    for k in range(taps):
        rows_ref[last + k * groups : last + (k + 1) * groups, :] = cb[k]
    row = lax.broadcasted_iota(jnp.int32, (heads, LANES), 0)
    lane = lax.broadcasted_iota(jnp.int32, (heads, LANES), 1)
    codes = jnp.sum(jnp.where(row == lane, code, 0.0), axis=0, keepdims=True)
    codes = jnp.where(lane[:1] == heads, code_x, codes)
    codes = jnp.where(lane[:1] == heads + 1, code_b, codes)
    factor_x = LEVELS / level_scale(code_x)
    factor_b = LEVELS / level_scale(code_b)
    used = rows_ref.shape[0] // AUX
    line = lax.broadcasted_iota(jnp.int32, (AUX, LANES), 0)
    for m in range(owners):
        if m < used:
            values = rows_ref[m * AUX : (m + 1) * AUX, :]
            if m * AUX < last:
                values = values * factor_x
            else:
                values = jnp.where(line == taps * groups, codes, values * factor_b)
        else:
            values = jnp.zeros((AUX, LANES), jnp.float32)
        out_ref[m, share:, :] = jnp.round(values).astype(jnp.int32).astype(jnp.int16)


def silu(v):
    return v / (1.0 + jnp.exp(-v))


def split(v):
    high = v.astype(jnp.bfloat16)
    low = (v - high.astype(jnp.float32)).astype(jnp.bfloat16)
    return high, low


def small_steps(seq_x, seq_b, wx_ref, bx_ref, wb_ref, bb_ref, steps):
    taps = len(seq_x) - steps + 1
    xs, bs, cs = [], [], []
    for t in range(steps):
        total = bx_ref[...]
        pairs = bb_ref[...]
        for k in range(taps):
            total = total + wx_ref[k] * seq_x[t + k]
            pairs = pairs + wb_ref[k] * seq_b[t + k]
        xs.append(silu(total))
        pairs = silu(pairs)
        turned = jnp.concatenate([pairs[:, LANES // 2 :], pairs[:, : LANES // 2]], 1)
        lower = lax.broadcasted_iota(jnp.int32, pairs.shape, 1) < LANES // 2
        bs.append(jnp.where(lower, pairs, turned))
        cs.append(jnp.where(lower, turned, pairs))
    return xs, bs, cs


def by_group(rows, count):
    groups = rows.shape[0]
    run = count // groups
    return jnp.concatenate(
        [jnp.broadcast_to(rows[g : g + 1], (run, rows.shape[1])) for g in range(groups)], 0
    )


def slot_steps(
    tile, column, scale, xs, bs, cs, dec, dts, skip, gate, write, spread_ref, mixed_ref
):
    steps = len(xs)
    heads = column.shape[0]
    blocks = xs[0].shape[0]
    lane = lax.broadcasted_iota(jnp.int32, (blocks, LANES), 1)
    lower = lane < LANES // 2
    later = None
    for t in reversed(range(steps)):
        weighted = xs[t] * dts[t]
        if later is not None:
            weighted = weighted * later
        later = dec[t] if later is None else later * dec[t]
        spread_ref[pl.ds(t * heads, blocks, stride=2), :] = jnp.where(lower, weighted, 0.0)
        spread_ref[pl.ds(t * heads + 1, blocks, stride=2), :] = jnp.where(lower, 0.0, weighted)
    high, low = split(spread_ref[...])
    spread = jnp.concatenate([high, low], 1)
    b_rows = [by_group(b, heads) for b in bs]
    c_rows = [by_group(c, heads) for c in cs]
    at = lax.broadcasted_iota(jnp.int32, (2 * LANES, LANES), 0) // P_SIZE
    to = lax.broadcasted_iota(jnp.int32, (2 * LANES, LANES), 1) % P_SIZE
    place = to - at
    wide = jnp.broadcast_to(column, (heads, LANES))
    mixed = jnp.zeros((steps * heads, LANES), jnp.float32)
    count = P_SIZE * P_SIZE // (2 * LANES)
    for k in range(count):
        chosen = jnp.where(place == k * (2 * LANES // P_SIZE), 1.0, 0.0).astype(jnp.bfloat16)
        states = [tile(2 * k), tile(2 * k + 1)]
        highs, lows = [], []
        for t in range(steps):
            parts = [split(s * c_rows[t]) for s in states]
            highs.append(jnp.concatenate([p[0] for p in parts], 1))
            lows.append(jnp.concatenate([p[1] for p in parts], 1))
        mixed = mixed + jnp.dot(
            jnp.concatenate(highs, 0), chosen, preferred_element_type=jnp.float32
        )
        mixed = mixed + jnp.dot(
            jnp.concatenate(lows, 0), chosen, preferred_element_type=jnp.float32
        )
        both = jnp.concatenate([chosen, chosen], 1)
        grown = lax.dot_general(
            spread, both, (((1,), (1,)), ((), ())), preferred_element_type=jnp.float32
        )
        for half in range(2):
            new = wide * states[half]
            for t in range(steps):
                piece = grown[t * heads : (t + 1) * heads, half * LANES : (half + 1) * LANES]
                new = new + piece * b_rows[t]
            write(2 * k + half, new)
    for t in range(steps):
        part = mixed[t * heads : (t + 1) * heads]
        if scale is not None:
            part = part * scale
        mixed_ref[t * heads : (t + 1) * heads, :] = part
    gated, sums = [], []
    ahead = None
    weights = []
    for t in range(steps):
        weights = [w * dec[t] for w in weights] + [dts[t]]
        ahead = dec[t] if ahead is None else ahead * dec[t]
        even = mixed_ref[pl.ds(t * heads, blocks, stride=2), :]
        odd = mixed_ref[pl.ds(t * heads + 1, blocks, stride=2), :]
        out = ahead * jnp.where(lower, even, odd) + skip * xs[t]
        for s in range(t + 1):
            inner = 0.5 * jnp.sum(bs[s] * cs[t], axis=1, keepdims=True)
            inner = by_group(jnp.broadcast_to(inner, (inner.shape[0], LANES)), blocks)
            out = out + weights[s] * inner * xs[s]
        out = out * gate[t]
        gated.append(out)
        squares = jnp.sum(jnp.sum(out * out, axis=0, keepdims=True), axis=1, keepdims=True)
        sums.append(jnp.broadcast_to(squares, (1, LANES)))
    return gated, sums


def kept_kernel(
    info_ref, state_ref, cx_ref, cb_ref, x_ref, bc_ref, gate_ref, dec_ref, dt_ref, skip_ref,
    column_ref, wx_ref, bx_ref, wb_ref, bb_ref,
    new_ref, gated_ref, sums_ref, spread_ref, mixed_ref,
):
    steps = x_ref.shape[1]
    taps = cx_ref.shape[1]
    seq_x = [cx_ref[0, k] for k in range(taps)] + [x_ref[0, t] for t in range(steps)]
    seq_b = [cb_ref[0, k] for k in range(taps)] + [bc_ref[0, t] for t in range(steps)]
    xs, bs, cs = small_steps(seq_x, seq_b, wx_ref, bx_ref, wb_ref, bb_ref, steps)
    full = info_ref[2] > 0

    def write(j, new):
        new_ref[0, :, j * LANES : (j + 1) * LANES] = jnp.where(full, new, 0.0)

    gated, sums = slot_steps(
        lambda j: state_ref[0, :, j * LANES : (j + 1) * LANES],
        column_ref[0], None, xs, bs, cs,
        [dec_ref[0, t] for t in range(steps)], [dt_ref[0, t] for t in range(steps)],
        skip_ref[...], [gate_ref[0, t] for t in range(steps)], write, spread_ref, mixed_ref,
    )
    for t in range(steps):
        gated_ref[t] = gated[t]
    sums_ref[...] = jnp.concatenate(sums, 0)


def moved_kernel(
    info_ref, got_ref, held_ref, kept_sums_ref, x_ref, bc_ref, gate_ref, dec_ref, dt_ref, skip_ref,
    column_ref, wx_ref, bx_ref, wb_ref, bb_ref,
    new_ref, gated_ref, sums_ref, spread_ref, mixed_ref,
):
    del held_ref
    steps, blocks = x_ref.shape[1:3]
    groups = bc_ref.shape[2]
    taps = wx_ref.shape[0] - 1
    heads = column_ref.shape[1]
    share = got_ref.shape[1] - AUX

    def aux(m):
        return got_ref[m, share:, :].astype(jnp.int32).astype(jnp.float32)

    per = blocks // AUX
    last = aux(taps * per)
    codes = last[taps * groups : taps * groups + 1]
    row = lax.broadcasted_iota(jnp.int32, (heads, LANES), 0)
    lane = lax.broadcasted_iota(jnp.int32, (heads, LANES), 1)
    code = jnp.sum(jnp.where(row == lane, codes, 0.0), axis=1, keepdims=True)
    scale = level_scale(code) * (1.0 / LEVELS)
    scale_x = level_scale(codes[:, heads : heads + 1]) * (1.0 / LEVELS)
    scale_b = level_scale(codes[:, heads + 1 : heads + 2]) * (1.0 / LEVELS)
    seq_x = [
        jnp.concatenate([aux(k * per + m) for m in range(per)], 0) * scale_x for k in range(taps)
    ] + [x_ref[0, t] for t in range(steps)]
    seq_b = [last[k * groups : (k + 1) * groups] * scale_b for k in range(taps)] + [
        bc_ref[0, t] for t in range(steps)
    ]
    xs, bs, cs = small_steps(seq_x, seq_b, wx_ref, bx_ref, wb_ref, bb_ref, steps)
    full = info_ref[4] > 0
    run = min(share, heads)

    def tile(j):
        parts = []
        for at in range(0, heads, run):
            flat = j * heads + at
            part = got_ref[flat // share, flat % share : flat % share + run, :]
            parts.append(part.astype(jnp.int32).astype(jnp.float32))
        return jnp.concatenate(parts, 0)

    def write(j, new):
        new_ref[0, :, j * LANES : (j + 1) * LANES] = jnp.where(full, new, 0.0)

    gated, sums = slot_steps(
        tile, column_ref[0] * scale, scale, xs, bs, cs,
        [dec_ref[0, t] for t in range(steps)], [dt_ref[0, t] for t in range(steps)],
        skip_ref[...], [gate_ref[0, t] for t in range(steps)], write, spread_ref, mixed_ref,
    )
    for t in range(steps):
        gated_ref[t] = gated[t]
    sums_ref[...] = jnp.concatenate([kept_sums_ref[...]] + sums, 0)


def norm_kernel(info_ref, kept_ref, moved_ref, mine_ref, theirs_ref, norm_ref, out_ref, rows_ref):
    steps, blocks = kept_ref.shape[:2]
    factor = lax.rsqrt((mine_ref[...] + theirs_ref[...]) * (1.0 / (H * P_SIZE)) + 1e-05)
    for which, ref in enumerate((kept_ref, moved_ref)):
        slot = info_ref[3 * which]
        full = info_ref[2 + 2 * which] > 0
        for t in range(steps):
            at = which * steps + t
            rows_ref[t * blocks : (t + 1) * blocks, :] = jnp.where(
                full, ref[t] * factor[at : at + 1] * norm_ref[...], 0.0
            )
        for b in range(blocks):
            out_ref[slot, :, b * LANES : (b + 1) * LANES] = rows_ref[
                pl.ds(b, steps, stride=blocks), :
            ].astype(jnp.bfloat16)


def on_device(
    counts,
    move_plan,
    ssm_state,
    conv_x_state,
    conv_bc_state,
    x_in,
    bc_in,
    z_in,
    dt_in,
    conv_w_x,
    conv_b_x,
    conv_w_bc,
    conv_b_bc,
    dt_bias,
    a_log,
    d_skip,
    norm_w,
):
    owners = lax.axis_size("req")
    owner = lax.axis_index("req").astype(jnp.int32)
    slots, heads, columns = ssm_state.shape
    places, steps, channels = x_in.shape
    taps = conv_x_state.shape[1]
    groups, pair = conv_bc_state.shape[2:]
    blocks = channels // LANES
    rows = heads * columns // LANES
    share = rows // owners
    params = pltpu.CompilerParams(vmem_limit_bytes=VMEM_LIMIT)
    f32 = jnp.float32

    def moving(i, counts_ref, plan_ref, me_ref):
        return moving_slot(counts_ref, plan_ref, me_ref, slots)

    payload = pl.pallas_call(
        pack_kernel,
        grid_spec=pltpu.PrefetchScalarGridSpec(
            num_scalar_prefetch=3,
            grid=(1,),
            in_specs=[
                pl.BlockSpec((1, heads, columns), lambda *a: (moving(*a), 0, 0)),
                pl.BlockSpec((1, taps, channels), lambda *a: (moving(*a), 0, 0)),
                pl.BlockSpec((1, taps, groups, pair), lambda *a: (moving(*a), 0, 0, 0)),
            ],
            out_specs=pl.BlockSpec((owners, share + AUX, LANES), lambda *a: (0, 0, 0)),
            scratch_shapes=[pltpu.VMEM((taps * blocks + AUX, LANES), f32)],
        ),
        out_shape=jax.ShapeDtypeStruct((owners, share + AUX, LANES), jnp.int16),
        compiler_params=params,
        name="pack",
    )(counts, move_plan, owner.reshape(1), ssm_state, conv_x_state, conv_bc_state)
    spread = lax.all_to_all(payload, "req", split_axis=0, concat_axis=0, tiled=True)

    ids = jnp.arange(move_plan.shape[0], dtype=jnp.int32)
    home = ids // slots
    live = ids % slots < jnp.repeat(counts, slots)
    target = move_plan // places
    away = live & (target != home)
    own = live & (target == home) & (home == owner)
    every = jnp.arange(owners, dtype=jnp.int32)
    source = jnp.sum(jnp.where(away[None] & (target[None] == every[:, None]), home[None], 0), axis=1)
    into = away & (target == owner)
    has_moved = jnp.any(into).astype(jnp.int32)
    has_kept = jnp.any(own).astype(jnp.int32)
    moved_to = jnp.sum(jnp.where(into, move_plan % places, 0))
    kept_to = jnp.sum(jnp.where(own, move_plan % places, 0))
    kept_from = jnp.sum(jnp.where(own, ids % slots, 0))
    moved_to = jnp.where(has_moved > 0, moved_to, jnp.where(has_kept > 0, 1 - kept_to, 0))
    kept_to = 1 - moved_to
    info = jnp.stack([kept_to, kept_from, has_kept, moved_to, has_moved]).astype(jnp.int32)

    picked = jnp.take(spread, source, axis=0, mode="clip")
    got = lax.all_to_all(picked, "req", split_axis=0, concat_axis=0, tiled=True)

    def dense(v):
        return v.astype(f32).reshape(*v.shape[:-1], blocks, LANES)

    def per_channel(v):
        return dense(jnp.repeat(v, P_SIZE, axis=-1))

    x_dense = dense(x_in)
    gate = jax.nn.silu(dense(z_in))
    delta = jax.nn.softplus(dt_in + dt_bias)
    decay = jnp.exp(-delta * jnp.exp(a_log))
    dt_dense = per_channel(delta)
    dec_dense = per_channel(decay)
    column = jnp.prod(decay, axis=1)[..., None]
    bc = bc_in.astype(f32)
    common = [x_dense, bc, gate, dec_dense, dt_dense, per_channel(d_skip), column]
    common += [dense(conv_w_x), dense(conv_b_x), conv_w_bc, conv_b_bc]

    def common_specs(at):
        def slot(*shape):
            return pl.BlockSpec((1, *shape), lambda i, info: (info[at], *[0] * len(shape)))

        def whole(*shape):
            return pl.BlockSpec(shape, lambda i, info: tuple([0] * len(shape)))

        return [
            slot(steps, blocks, LANES), slot(steps, groups, pair), slot(steps, blocks, LANES),
            slot(steps, blocks, LANES), slot(steps, blocks, LANES), whole(blocks, LANES),
            slot(heads, 1), whole(taps + 1, blocks, LANES), whole(blocks, LANES),
            whole(taps + 1, groups, pair), whole(groups, pair),
        ]

    state_shape = jax.ShapeDtypeStruct((places, heads, columns), f32)
    gated_shape = jax.ShapeDtypeStruct((steps, blocks, LANES), f32)
    scratch = [pltpu.VMEM((steps * heads, LANES), f32)] * 2

    def out_specs(at, count):
        return [
            pl.BlockSpec((1, heads, columns), lambda i, info: (info[at], 0, 0)),
            pl.BlockSpec((steps, blocks, LANES), lambda i, info: (0, 0, 0)),
            pl.BlockSpec((count, LANES), lambda i, info: (0, 0)),
        ]

    held, kept_gated, kept_sums = pl.pallas_call(
        kept_kernel,
        grid_spec=pltpu.PrefetchScalarGridSpec(
            num_scalar_prefetch=1,
            grid=(1,),
            in_specs=[
                pl.BlockSpec((1, heads, columns), lambda i, info: (info[1], 0, 0)),
                pl.BlockSpec((1, taps, blocks, LANES), lambda i, info: (info[1], 0, 0, 0)),
                pl.BlockSpec((1, taps, groups, pair), lambda i, info: (info[1], 0, 0, 0)),
            ]
            + common_specs(0),
            out_specs=out_specs(0, steps),
            scratch_shapes=scratch,
        ),
        out_shape=[state_shape, gated_shape, jax.ShapeDtypeStruct((steps, LANES), f32)],
        compiler_params=params,
        name="kept",
    )(info, ssm_state, dense(conv_x_state), conv_bc_state.astype(f32), *common)

    new_ssm, moved_gated, sums = pl.pallas_call(
        moved_kernel,
        grid_spec=pltpu.PrefetchScalarGridSpec(
            num_scalar_prefetch=1,
            grid=(1,),
            in_specs=[
                pl.BlockSpec((owners, share + AUX, LANES), lambda i, info: (0, 0, 0)),
                pl.BlockSpec(memory_space=pl.ANY),
                pl.BlockSpec((steps, LANES), lambda i, info: (0, 0)),
            ]
            + common_specs(3),
            out_specs=out_specs(3, 2 * steps),
            scratch_shapes=scratch,
        ),
        out_shape=[state_shape, gated_shape, jax.ShapeDtypeStruct((2 * steps, LANES), f32)],
        input_output_aliases={2: 0},
        compiler_params=params,
        name="moved",
    )(info, got, held, kept_sums, *common)

    theirs = lax.ppermute(sums, "tp", [(0, 1), (1, 0)])
    y_out = pl.pallas_call(
        norm_kernel,
        grid_spec=pltpu.PrefetchScalarGridSpec(
            num_scalar_prefetch=1,
            grid=(1,),
            in_specs=[
                pl.BlockSpec((steps, blocks, LANES), lambda i, info: (0, 0, 0)),
                pl.BlockSpec((steps, blocks, LANES), lambda i, info: (0, 0, 0)),
                pl.BlockSpec((2 * steps, LANES), lambda i, info: (0, 0)),
                pl.BlockSpec((2 * steps, LANES), lambda i, info: (0, 0)),
                pl.BlockSpec((blocks, LANES), lambda i, info: (0, 0)),
            ],
            out_specs=pl.BlockSpec((places, steps, channels), lambda i, info: (0, 0, 0)),
            scratch_shapes=[pltpu.VMEM((steps * blocks, LANES), f32)],
        ),
        out_shape=jax.ShapeDtypeStruct((places, steps, channels), jnp.bfloat16),
        compiler_params=params,
        name="norm",
    )(info, kept_gated, moved_gated, sums, theirs, dense(norm_w))

    filled = jnp.where(jnp.arange(places) == kept_to, has_kept, has_moved) > 0
    last_x = x_in[:, steps - taps :]
    last_bc = bc_in[:, steps - taps :]
    new_conv_x = jnp.where(filled[:, None, None], last_x, jnp.zeros_like(last_x))
    new_conv_bc = jnp.where(filled[:, None, None, None], last_bc, jnp.zeros_like(last_bc))
    return (y_out, new_ssm, new_conv_x, new_conv_bc)


def solution(mesh):
    in_specs = (
        P("parts"),
        P("parts"),
        P(("parts", "req"), "tp", None),
        P(("parts", "req"), None, "tp"),
        P(("parts", "req"), None, "tp", None),
        P(("parts", "req"), None, "tp"),
        P(("parts", "req"), None, "tp", None),
        P(("parts", "req"), None, "tp"),
        P(("parts", "req"), None, "tp"),
        P(None, "tp"),
        P("tp"),
        P(None, "tp", None),
        P("tp", None),
        P("tp"),
        P("tp"),
        P("tp"),
        P("tp"),
    )
    out_specs = (
        P(("parts", "req"), None, "tp"),
        P(("parts", "req"), "tp", None),
        P(("parts", "req"), None, "tp"),
        P(("parts", "req"), None, "tp", None),
    )
    return jax.shard_map(
        on_device, mesh=mesh, in_specs=in_specs, out_specs=out_specs, check_vma=False
    )
```

time: 196 us -> 56.7 us (0.29)
  waiting for transfers between devices: 96.6 us -> 18.3 us
  local copies, waits for them, and re-layouts: 48.9 us -> 9.22 us
  other arithmetic: 27.6 us -> 3.81 us
  Pallas kernels: 0 us -> 10.2 us
  starting transfers between devices: 18.6 us -> 11.2 us
  blocking collectives: 2.46 us -> 0 us
  between operations: 1.11 us -> 3.46 us
    all_to_all x4 -> x2, waiting for transfers between devices: 96.6 us -> 17.8 us  [the longest x1 14.6 us: on_device(): got = lax.all_to_all(picked, 'req', split_axis=0, concat_axis=0, tiled=True)]
    mul x7 -> x0, local copies, waits for them, and re-layouts: 21.4 us -> none  [the longest x4 17.8 us: on_device(): (delta[:, :, None] * heads_x)[..., None] * b_head[:, :, None, :]]
    reduce_sum x5 -> x2, other arithmetic: 15.1 us -> 0.76 us  [the longest x1 0.64 us: on_device(): kept_from = jnp.sum(jnp.where(own, ids % slots, 0))]
    pallas_call x0 -> x4, Pallas kernels: none -> 10.2 us  [the longest x1 3.64 us: on_device(): pl.pallas_call(moved_kernel, grid_spec=pltpu.PrefetchScalarGridSpec(num_s...]
    mul x5 -> x1, other arithmetic: 8.43 us -> 0.95 us  [on_device(): gate = jax.nn.silu(dense(z_in))]
    all_to_all x4 -> x2, starting transfers between devices: 18.6 us -> 11.2 us  [the longest x1 7.4 us: on_device(): lax.all_to_all(payload, 'req', split_axis=0, concat_axis=0, tiled=True)]
    all_to_all x5 -> x0, local copies, waits for them, and re-layouts: 5.58 us -> none  [the longest x1 2.81 us: on_device(): lax.all_to_all(picked_state, 'req', split_axis=0, concat_axis=1, tiled=True)]
    reshape x8 -> x5, local copies, waits for them, and re-layouts: 6.45 us -> 0.9 us  [the longest x4 0.82 us: dense(): return v.astype(f32).reshape(*v.shape[:-1], blocks, LANES)]
  transfers between devices with their start and end apart: 4 -> 3, of which waited for: 4 -> 3; matrix products, arithmetic and copies ran while one was open for 6% -> 12% of each run, Pallas kernels for 0% -> 6%
where the time goes in v1:
time: 56.7 us; the launch traced here: 56.2 us
  waiting for transfers between devices  18.3 us (32%)
  starting transfers between devices  11.2 us (20%)
  Pallas kernels  10.2 us (18%)
  local copies, waits for them, and re-layouts  9.22 us (16%)
  other arithmetic  3.81 us (7%)
  between operations  3.46 us (6%)
    all_to_all x1, waiting for transfers between devices, on_device(): got = lax.all_to_all(picked, 'req', split_axis=0, concat_axis=0, tiled=True)  14.6 us
    all_to_all x1, starting transfers between devices, on_device(): lax.all_to_all(payload, 'req', split_axis=0, concat_axis=0, tiled=True)  7.4 us
    unnamed x46, local copies, waits for them, and re-layouts  4.55 us
    all_to_all x1, starting transfers between devices, on_device(): got = lax.all_to_all(picked, 'req', split_axis=0, concat_axis=0, tiled=True)  3.77 us
    pallas_call x1, Pallas kernels, on_device(): pl.pallas_call(moved_kernel, grid_spec=pltpu.PrefetchScalarGridSpec(num_s...  3.64 us
    pallas_call x1, Pallas kernels, on_device(): pl.pallas_call(kept_kernel, grid_spec=pltpu.PrefetchScalarGridSpec(num_sc...  3.62 us
    all_to_all x1, waiting for transfers between devices, on_device(): lax.all_to_all(payload, 'req', split_axis=0, concat_axis=0, tiled=True)  3.18 us
    pallas_call x1, Pallas kernels, on_device(): pl.pallas_call(pack_kernel, grid_spec=pltpu.PrefetchScalarGridSpec(num_sc...  1.66 us
  transfers between devices with their start and end apart: 3, of which 3 were waited for; matrix products, arithmetic and copies ran while one was open for 12% of the time, Pallas kernels for 6%

profile of v1, /device:TPU:0, one launch (start us, length us, event | category | flops | bytes accessed | tf_op | source)
XLA Modules:
  0.0 56.2 jit_solution(9082128296034143284)
XLA Ops:
  0.7 0.9 %copy.34.cx_ref = bf16[2,3,4096]{2,1,0:T(4,128)(2,1)S(1)} copy(bf16[2,3,4096]{2,0,1:T(2,128)(2,1)} %param.20) | data formatting | bytes 98304 | tf_op args[3]
  1.6 1.6 %copy-done = f32[2,64,4096]{2,1,0:T(8,128)S(1)} copy-done((f32[2,64,4096]{2,1,0:T(8,128)S(1)}, f32[2,64,4096]{2,1,0:T(8,128)}, u32[]{:S(2)}) %copy-start) | copy-done | bytes 2097176
  3.2 0.7 %copy-done.5 = bf16[2,3,2,128]{3,2,1,0:T(2,128)(2,1)S(1)} copy-done((bf16[2,3,2,128]{3,2,1,0:T(2,128)(2,1)S(1)}, bf16[2,3,2,128]{3,2,1,0:T(2,128)(2,1)}, u32[]{:S(2)}) %copy-start.5) | copy-done | bytes 3096
  3.9 0.7 %copy-done.8 = s32[8]{0:T(128)S(1)} copy-done((s32[8]{0:T(128)S(1)}, s32[8]{0:T(128)}, u32[]{:S(2)}) %copy-start.8) | copy-done | bytes 56
  4.5 0.7 %copy-done.10 = s32[16]{0:T(128)S(1)} copy-done((s32[16]{0:T(128)S(1)}, s32[16]{0:T(128)}, u32[]{:S(2)}) %copy-start.10) | copy-done | bytes 88
  5.2 1.7 %pack.1 = s16[8,272,128]{2,1,0:T(8,128)(2,1)} custom-call(s32[8]{0:T(128)S(1)} %copy-done.8, s32[16]{0:T(128)S(1)} %copy-done.10, s32[1]{0:T(128)} %bitcast.7.me_ref, f32[2,64,4096]{2,1,0:T(8,128)S(1)} %copy-done, bf16[2,3,4096]{2,1,0:T(4,128)(2,1)S(1)} %copy.34.cx_ref, bf16[2,3,2,128]{3,2,1,0:T(2,128)(2,1)S(1)} %copy-done.5), custom_call_target="tpu_custom_call" | custom-call | tf_op jit(solution)/shard_map/pack/pallas_call | solution.py:329
  6.9 7.4 %all-to-all-start = ((s16[8,272,128]{2,1,0:T(8,128)(2,1)}), s16[8,272,128]{2,1,0:T(8,128)(2,1)S(1)}, u32[]{:S(2)}, u32[]{:S(2)}) async-start(s16[8,272,128]{2,1,0:T(8,128)(2,1)} %pack.1), calls=%async_computation | async-start | bytes 1114112 | tf_op jit(solution)/shard_map/all_to_all | solution.py:346
  14.5 0.6 %fusion.5 = (pred[]{:T(512)}, pred[16]{0:T(512)(128)(4,1)S(1)}, pred[]{:T(512)}) fusion(s32[]{:T(128)} %axis_index.15, s32[16]{0:T(128)S(1)} %get-tuple-element.20, s32[16]{0:T(128)S(1)} %reshape.70), kind=kLoop, calls=%fused_computation.32 | loop fusion | flops 366 | bytes 150 | tf_op jit(solution)/shard_map/reduce_or | solution.py:358
  15.2 0.7 %slice.6 = bf16[2,3,4096]{2,1,0:T(4,128)(2,1)} slice(bf16[2,4,4096]{2,1,0:T(4,128)(2,1)S(1)} %copy-done.12), slice={[0:2], [1:4], [0:4096]} | slice | bytes 98304 | tf_op jit(solution)/shard_map/slice | solution.py:472
  17.2 0.6 %select_reduce_fusion.1 = (s32[]{:T(128)}, s32[]{:T(128)}, s32[]{:T(128)}) fusion(pred[16]{0:T(512)(128)(4,1)S(1)} %get-tuple-element.26, s32[16]{0:T(128)S(1)} %get-tuple-element.21, s32[16]{0:T(128)S(1)} %get-tuple-element.20, s32[]{:T(128)} %axis_index.15, s32[16]{0:T(128)S(1)} %reshape.70), kind=kLoop, calls=%fused_computation.25 | loop fusion | flops 445 | bytes 224 | tf_op jit(solution)/shard_map/reduce_sum | solution.py:361
  19.1 0.7 %reshape.86 = f32[2,4,32,128]{3,2,1,0:T(8,128)} reshape(bf16[2,4,4096]{2,1,0:T(4,128)(2,1)S(1)} %copy-done.15) | data formatting | bytes 196608 | tf_op jit(solution)/shard_map/reshape | solution.py:370
  19.9 0.1 broadcast_in_dim.78
  20.8 0.7 %stack.23.info_ref = s32[5]{0:T(128)S(1)} concatenate(s32[1]{0:T(128)} %bitcast, s32[1]{0:T(128)} %bitcast.1, s32[1]{0:T(128)} %bitcast.2, s32[1]{0:T(128)} %bitcast.3, s32[1]{0:T(128)} %bitcast.4), dimensions={0} | concatenate | bytes 40 | tf_op jit(solution)/shard_map/stack | solution.py:364
  21.5 0.9 %divide_multiply_fusion.gate_ref = f32[2,4,32,128]{3,2,1,0:T(8,128)S(1)} fusion(f32[2,4,32,128]{3,2,1,0:T(8,128)} %reshape.86), kind=kLoop, calls=%fused_computation.1 | loop fusion | flops 131072 | bytes 262144 | tf_op jit(solution)/shard_map/jit(silu)/mul | solution.py:376
  22.5 3.6 %kept.1 = (f32[2,64,4096]{2,1,0:T(8,128)}, f32[4,32,128]{2,1,0:T(8,128)S(1)}, f32[4,128]{1,0:T(4,128)S(1)}) custom-call(s32[5]{0:T(128)S(1)} %stack.23.info_ref, f32[2,64,4096]{2,1,0:T(8,128)S(1)} %copy-done.1, f32[2,3,32,128]{3,2,1,0:T(8,128)S(1)} %copy.32.cx_ref, f32[2,3,2,128]{3,2,1,0:T(2,128)S(1)} %convert_element_type.17.cb_ref, ...), custom_call_target="tpu_custom_call" | custom-call | tf_op jit(solution)/shard_map/kept/pallas_call | solution.py:411
  26.3 3.2 %all-to-all-done = s16[8,272,128]{2,1,0:T(8,128)(2,1)S(1)} async-done(((s16[8,272,128]{2,1,0:T(8,128)(2,1)}), s16[8,272,128]{2,1,0:T(8,128)(2,1)S(1)}, u32[]{:S(2)}, u32[]{:S(2)}) %all-to-all-start) | async-done | bytes 557088 | tf_op jit(solution)/shard_map/all_to_all | solution.py:346
  29.5 1.5 %gather_fusion = s16[8,272,128]{2,1,0:T(8,128)(2,1)} fusion(s16[8,272,128]{2,1,0:T(8,128)(2,1)S(1)} %all-to-all-done, s32[1024]{0:T(1024)S(1)} %pad_clamp_fusion), kind=kCustom, calls=%fused_computation | custom fusion | bytes 1114144 | tf_op jit(solution)/shard_map/jit(_take)/gather | solution.py:366
  30.9 3.8 %all-to-all-start.1 = ((s16[8,272,128]{2,1,0:T(8,128)(2,1)}), s16[8,272,128]{2,1,0:T(8,128)(2,1)S(1)}, u32[]{:S(2)}, u32[]{:S(2)}) async-start(s16[8,272,128]{2,1,0:T(8,128)(2,1)} %gather_fusion), calls=%async_computation.1 | async-start | bytes 1114112 | tf_op jit(solution)/shard_map/all_to_all | solution.py:367
  34.7 0.7 %broadcast_select_fusion = bf16[2,3,4096]{2,0,1:T(2,128)(2,1)} fusion(pred[2]{0:T(512)(128)(4,1)S(1)} %fusion.1, bf16[2,3,4096]{2,1,0:T(4,128)(2,1)S(1)} %copy-done.13), kind=kLoop, calls=%fused_computation.2 | loop fusion | flops 24576 | bytes 98306 | tf_op jit(solution)/shard_map/jit(_where)/select_n | solution.py:474
  35.5 14.6 %all-to-all-done.1.got_ref = s16[8,272,128]{2,1,0:T(8,128)(2,1)S(1)} async-done(((s16[8,272,128]{2,1,0:T(8,128)(2,1)}), s16[8,272,128]{2,1,0:T(8,128)(2,1)S(1)}, u32[]{:S(2)}, u32[]{:S(2)}) %all-to-all-start.1) | async-done | bytes 557088 | tf_op jit(solution)/shard_map/all_to_all | solution.py:367
  50.1 3.6 %moved.1 = (f32[2,64,4096]{2,1,0:T(8,128)}, f32[4,32,128]{2,1,0:T(8,128)S(1)}, f32[8,128]{1,0:T(8,128)S(1)}) custom-call(s32[5]{0:T(128)S(1)} %stack.23.info_ref, s16[8,272,128]{2,1,0:T(8,128)(2,1)S(1)} %all-to-all-done.1.got_ref, f32[2,64,4096]{2,1,0:T(8,128)} %get-tuple-element.11.held_ref, ...), custom_call_target="tpu_custom_call", output_to_operand_aliasing={{0}: (2, {})} | custom-call | tf_op jit(solution)/shard_map/moved/pallas_call | solution.py:430
  53.7 0.7 %broadcast_select_fusion.1 = bf16[2,3,2,128]{3,2,1,0:T(2,128)(2,1)} fusion(pred[2]{0:T(512)(128)(4,1)S(1)} %fusion.1, bf16[2,4,2,128]{3,2,1,0:T(2,128)(2,1)S(1)} %copy-done.17), kind=kLoop, calls=%fused_computation.5 | loop fusion | flops 1536 | bytes 6146 | tf_op jit(solution)/shard_map/jit(_where)/select_n | solution.py:475
  54.4 0.5 collective-permute-done.theirs_ref
  54.9 1.3 %norm.1 = bf16[2,4,4096]{2,1,0:T(4,128)(2,1)} custom-call(s32[5]{0:T(128)S(1)} %stack.23.info_ref, f32[4,32,128]{2,1,0:T(8,128)S(1)} %get-tuple-element.10.kept_ref, f32[4,32,128]{2,1,0:T(8,128)S(1)} %get-tuple-element.13.moved_ref, f32[8,128]{1,0:T(8,128)S(1)} %get-tuple-element.14.mine_ref, f32[8,128]{1,0:T(8,128)S(1)} %collective-permute-done.theirs_ref, ...), custom_call_target="tpu_custom_call" | custom-call | tf_op jit(solution)/shard_map/norm/pallas_call | solution.py:451
  (63 shorter events, 1.3 us)
Async XLA Ops:
  0.6 14.5 %copy-start.14 = (bf16[2,3,4096]{2,0,1:T(2,128)(2,1)S(1)}, bf16[2,3,4096]{2,0,1:T(2,128)(2,1)}, u32[]{:S(2)}) copy-start(bf16[2,3,4096]{2,0,1:T(2,128)(2,1)} %param.20) | copy-start | bytes 147460
  0.6 13.6 %copy-start.9 = (s32[8]{0:T(128)S(1)}, s32[8]{0:T(128)}, u32[]{:S(2)}) copy-start(s32[8]{0:T(128)} %counts_ref.1) | copy-start | bytes 100
  0.7 13.8 %copy-start.11 = (s32[16]{0:T(128)S(1)}, s32[16]{0:T(128)}, u32[]{:S(2)}) copy-start(s32[16]{0:T(128)} %plan_ref.1) | copy-start | bytes 196
  0.7 14.5 %copy-start.6 = (bf16[2,3,2,128]{3,2,1,0:T(2,128)(2,1)S(1)}, bf16[2,3,2,128]{3,2,1,0:T(2,128)(2,1)}, u32[]{:S(2)}) copy-start(bf16[2,3,2,128]{3,2,1,0:T(2,128)(2,1)} %cb_ref.1) | copy-start | bytes 9220
  0.7 14.5 %copy-start.12 = (bf16[2,4,4096]{2,1,0:T(4,128)(2,1)S(1)}, bf16[2,4,4096]{2,1,0:T(4,128)(2,1)}, u32[]{:S(2)}) copy-start(bf16[2,4,4096]{2,1,0:T(4,128)(2,1)} %param.22) | copy-start | bytes 196612
  1.6 1.6 %copy-start = (f32[2,64,4096]{2,1,0:T(8,128)S(1)}, f32[2,64,4096]{2,1,0:T(8,128)}, u32[]{:S(2)}) copy-start(f32[2,64,4096]{2,1,0:T(8,128)} %state_ref.3) | copy-start | bytes 6291460
  3.2 0.7 %copy-start.5 = (bf16[2,3,2,128]{3,2,1,0:T(2,128)(2,1)S(1)}, bf16[2,3,2,128]{3,2,1,0:T(2,128)(2,1)}, u32[]{:S(2)}) copy-start(bf16[2,3,2,128]{3,2,1,0:T(2,128)(2,1)} %cb_ref.1) | copy-start | bytes 9220
  3.9 0.7 %copy-start.8 = (s32[8]{0:T(128)S(1)}, s32[8]{0:T(128)}, u32[]{:S(2)}) copy-start(s32[8]{0:T(128)} %counts_ref.1) | copy-start | bytes 100
  5.2 13.9 %copy-start.17 = (bf16[2,4,2,128]{3,2,1,0:T(2,128)(2,1)S(1)}, bf16[2,4,2,128]{3,2,1,0:T(2,128)(2,1)}, u32[]{:S(2)}) copy-start(bf16[2,4,2,128]{3,2,1,0:T(2,128)(2,1)} %param.23) | copy-start | bytes 12292
  5.2 13.9 %copy-start.15 = (bf16[2,4,4096]{2,1,0:T(4,128)(2,1)S(1)}, bf16[2,4,4096]{2,1,0:T(4,128)(2,1)}, u32[]{:S(2)}) copy-start(bf16[2,4,4096]{2,1,0:T(4,128)(2,1)} %param.24) | copy-start | bytes 196612
  5.2 14.7 %copy-start.21 = (f32[64]{0:T(128)S(1)}, f32[64]{0:T(128)}, u32[]{:S(2)}) copy-start(f32[64]{0:T(128)} %param.31) | copy-start | bytes 772
  5.2 14.7 %copy-start.18 = (f32[2,4,64]{2,1,0:T(4,128)S(1)}, f32[2,4,64]{2,1,0:T(4,128)}, u32[]{:S(2)}) copy-start(f32[2,4,64]{2,1,0:T(4,128)} %param.25) | copy-start | bytes 6148
  5.2 14.7 %copy-start.19 = (f32[64]{0:T(128)S(1)}, f32[64]{0:T(128)}, u32[]{:S(2)}) copy-start(f32[64]{0:T(128)} %param.30) | copy-start | bytes 772
  6.8 13.5 %copy-start.20 = (f32[64]{0:T(128)S(1)}, f32[64]{0:T(128)}, u32[]{:S(2)}) copy-start(f32[64]{0:T(128)} %param.32) | copy-start | bytes 772
  6.9 13.9 %copy-start.16 = (f32[4,4096]{1,0:T(4,128)S(1)}, f32[4,4096]{1,0:T(4,128)}, u32[]{:S(2)}) copy-start(f32[4,4096]{1,0:T(4,128)} %param.26) | copy-start | bytes 196612
  6.9 15.6 %copy-start.1 = (f32[2,64,4096]{2,1,0:T(8,128)S(1)}, f32[2,64,4096]{2,1,0:T(8,128)}, u32[]{:S(2)}) copy-start(f32[2,64,4096]{2,1,0:T(8,128)} %state_ref.3) | copy-start | bytes 6291460
  6.9 15.7 %copy-start.2 = (f32[4096]{0:T(1024)S(1)}, f32[4096]{0:T(1024)}, u32[]{:S(2)}) copy-start(f32[4096]{0:T(1024)} %param.27) | copy-start | bytes 49156
  6.9 15.7 %copy-start.3 = (f32[4,2,128]{2,1,0:T(2,128)S(1)}, f32[4,2,128]{2,1,0:T(2,128)}, u32[]{:S(2)}) copy-start(f32[4,2,128]{2,1,0:T(2,128)} %wb_ref.3) | copy-start | bytes 12292
  6.9 15.7 %copy-start.7 = (f32[2,128]{1,0:T(2,128)S(1)}, f32[2,128]{1,0:T(2,128)}, u32[]{:S(2)}) copy-start(f32[2,128]{1,0:T(2,128)} %bb_ref.3) | copy-start | bytes 3076
  6.9 22.6 %all-to-all-start = ((s16[8,272,128]{2,1,0:T(8,128)(2,1)}), s16[8,272,128]{2,1,0:T(8,128)(2,1)S(1)}, u32[]{:S(2)}, u32[]{:S(2)}) async-start(s16[8,272,128]{2,1,0:T(8,128)(2,1)} %pack.1), calls=%async_computation | async-start | bytes 1114112 | tf_op jit(solution)/shard_map/all_to_all | solution.py:346
  26.2 8.6 %copy-start.13 = (bf16[2,3,4096]{2,1,0:T(4,128)(2,1)S(1)}, bf16[2,3,4096]{2,1,0:T(4,128)(2,1)}, u32[]{:S(2)}) copy-start(bf16[2,3,4096]{2,1,0:T(4,128)(2,1)} %slice.6) | copy-start | bytes 147460
  30.9 23.9 %copy-start.4 = (f32[4096]{0:T(1024)S(1)}, f32[4096]{0:T(1024)}, u32[]{:S(2)}) copy-start(f32[4096]{0:T(1024)} %param.33) | copy-start | bytes 49156
  30.9 19.1 %all-to-all-start.1 = ((s16[8,272,128]{2,1,0:T(8,128)(2,1)}), s16[8,272,128]{2,1,0:T(8,128)(2,1)S(1)}, u32[]{:S(2)}, u32[]{:S(2)}) async-start(s16[8,272,128]{2,1,0:T(8,128)(2,1)} %gather_fusion), calls=%async_computation.1 | async-start | bytes 1114112 | tf_op jit(solution)/shard_map/all_to_all | solution.py:367
  53.7 1.2 %collective-permute-start = (f32[8,128]{1,0:T(8,128)S(1)}, f32[8,128]{1,0:T(8,128)S(1)}, u32[]{:S(2)}, u32[]{:S(2)}) collective-permute-start(f32[8,128]{1,0:T(8,128)S(1)} %get-tuple-element.14.mine_ref), channel_id=1, source_target_pairs={{0,1},{1,0},{2,3},{3,2},{4,5},{5,4},{6,7},{7,6},{8,9},{9,8},{10,11... | collective-permute-start | bytes 12296 | tf_op jit(solution)/shard_map/ppermute | solution.py:450
  (1 other events, 0.7 us)

commit v2 on v1

v2 whole, which is shorter than its diff:
```python
import functools

import jax
import jax.numpy as jnp
from jax import lax
from jax.experimental import pallas as pl
from jax.experimental.pallas import tpu as pltpu
from jax.sharding import PartitionSpec as P

H = 128
P_SIZE = 64
LANES = 128
AUX = 16
BLOCK = 16
INFO = 8
REACH = 6.0
LEVELS = 32767.0
VMEM_LIMIT = 48 * 1024 * 1024


def level_code(top):
    code = jnp.floor(-8.0 / jnp.log(2.0) * jnp.log(jnp.maximum(top, 1e-30) / REACH) - 0.01)
    return jnp.clip(code, 0.0, 800.0)


def level_scale(code):
    return REACH * jnp.exp(code * (-0.125 * jnp.log(2.0)))


def moving_slot(counts_ref, plan_ref, me, slots):
    slot = jnp.int32(0)
    for local in range(1, slots):
        live = local < counts_ref[me]
        away = plan_ref[me * slots + local] // slots != me
        slot = jnp.where(live & away, local, slot)
    return slot


def dense_rows(rows_ref, at, values):
    count, channels = values.shape
    blocks = channels // LANES
    for b in range(blocks):
        part = values[:, b * LANES : (b + 1) * LANES]
        if count == 1:
            rows_ref[at + b : at + b + 1, :] = part
        else:
            rows_ref[pl.ds(at + b, count, stride=blocks), :] = part


def of_slot(values, slot):
    return jnp.where(slot == 0, values[0], values[1])


def pack_kernel(me_ref, counts_hbm, plan_hbm, state_hbm, cx_hbm, cb_hbm, *refs):
    *out_refs, counts_ref, plan_ref, state_ref, cx_ref, cb_ref, rows_ref, sems = refs
    direct = len(out_refs) > 1
    slots, heads, columns = state_ref.shape
    owners = len(out_refs) if direct else out_refs[0].shape[0]
    share = out_refs[0].shape[-2] - AUX
    run = min(share, BLOCK)
    each = share // heads
    me = me_ref[0]
    small = [
        pltpu.make_async_copy(src, dst, sems.at[i])
        for i, (src, dst) in enumerate(
            ((counts_hbm, counts_ref), (plan_hbm, plan_ref), (cx_hbm, cx_ref), (cb_hbm, cb_ref))
        )
    ]
    for copy in small:
        copy.start()
    large = []
    for at in range(0, heads, BLOCK):
        for slot in range(slots):
            part = (slot, pl.ds(at, BLOCK))
            copy = pltpu.make_async_copy(
                state_hbm.at[part], state_ref.at[part], sems.at[len(small) + len(large)]
            )
            copy.start()
            large.append(copy)
    small[0].wait()
    small[1].wait()
    slot = moving_slot(counts_ref, plan_ref, me, slots)
    small[2].wait()
    small[3].wait()
    taps, _, channels = cx_ref.shape
    groups = cb_ref.shape[2]
    blocks = channels // LANES
    cx = cx_ref[...].astype(jnp.float32)
    cx = jnp.where(slot == 0, cx[:, 0], cx[:, 1])
    cb = of_slot(cb_ref[...].astype(jnp.float32), slot)
    code_x = level_code(jnp.max(jnp.abs(cx)).reshape(1, 1))
    code_b = level_code(jnp.max(jnp.abs(cb)).reshape(1, 1))
    dense_rows(rows_ref, 0, cx)
    last = taps * blocks
    rows_ref[last:, :] = jnp.zeros((rows_ref.shape[0] - last, LANES), jnp.float32)
    for k in range(taps):
        rows_ref[last + k * groups : last + (k + 1) * groups, :] = cb[k]
    lane = lax.broadcasted_iota(jnp.int32, (BLOCK, LANES), 1)
    row = lax.broadcasted_iota(jnp.int32, (BLOCK, LANES), 0)
    codes = jnp.where(lane[:1] == heads, code_x, 0.0)
    codes = jnp.where(lane[:1] == heads + 1, code_b, codes)
    for q in range(heads // BLOCK):
        for copy in large[q * slots : (q + 1) * slots]:
            copy.wait()
        at = q * BLOCK
        top = jnp.abs(state_ref[slot, at : at + BLOCK, :LANES])
        for j in range(1, columns // LANES):
            tile = state_ref[slot, at : at + BLOCK, j * LANES : (j + 1) * LANES]
            top = jnp.maximum(top, jnp.abs(tile))
        code = level_code(jnp.max(top, axis=1, keepdims=True))
        codes = codes + jnp.sum(jnp.where(row + at == lane, code, 0.0), axis=0, keepdims=True)
        factor = jnp.broadcast_to(LEVELS / level_scale(code), (BLOCK, LANES))
        for j in range(columns // LANES):
            place = (me ^ (j // each)) * each + j % each if direct else j
            lanes = pl.ds(pl.multiple_of(place * LANES, LANES), LANES)
            tile = state_ref[slot, at : at + BLOCK, lanes] * factor
            tile = jnp.round(tile).astype(jnp.int32).astype(jnp.int16)
            for part in range(0, BLOCK, run):
                flat = j * heads + at + part
                rows = pl.ds(flat % share, run)
                if direct:
                    out_refs[flat // share][rows, :] = tile[part : part + run]
                else:
                    out_refs[0][flat // share, rows, :] = tile[part : part + run]
    factor_x = LEVELS / level_scale(code_x)
    factor_b = LEVELS / level_scale(code_b)
    line = lax.broadcasted_iota(jnp.int32, (AUX, LANES), 0)
    rows_ref[:last, :] = rows_ref[:last, :] * factor_x
    values = rows_ref[last : last + AUX, :] * factor_b
    rows_ref[last : last + AUX, :] = jnp.where(line == taps * groups, codes, values)
    for m in range(owners):
        if direct:
            values = rows_ref[pl.ds(pl.multiple_of((me ^ m) * AUX, AUX), AUX), :]
        elif m * AUX < last + AUX:
            values = rows_ref[m * AUX : (m + 1) * AUX, :]
        else:
            values = jnp.zeros((AUX, LANES), jnp.float32)
        values = jnp.round(values).astype(jnp.int32).astype(jnp.int16)
        if direct:
            out_refs[m][share:, :] = values
        else:
            out_refs[0][m, share:, :] = values


def pick_kernel(info_ref, *refs):
    if len(refs) == 2:
        in_ref, out_ref = refs
        for m in range(out_ref.shape[0]):
            out_ref[m] = in_ref[info_ref[INFO + m]]
        return
    owners = len(refs) // 2
    *in_refs, all_ref = refs[:owners] + refs[-1:]
    out_refs = refs[owners:-1]
    me = info_ref[5]
    for k in range(owners):
        all_ref[k] = in_refs[k][...]
    for k in range(owners):
        out_refs[k][...] = all_ref[info_ref[INFO + (me ^ k)] ^ me]


def silu(v):
    return v / (1.0 + jnp.exp(-v))


def split(v):
    high = v.astype(jnp.bfloat16)
    low = (v - high.astype(jnp.float32)).astype(jnp.bfloat16)
    return high, low


def small_steps(seq_x, seq_b, wx_ref, bx_ref, wb_ref, bb_ref, steps):
    taps = len(seq_x) - steps + 1
    blocks = bx_ref.shape[0]
    xs, bs, cs = [], [], []
    for t in range(steps):
        total = bx_ref[...]
        pairs = bb_ref[...]
        for k in range(taps):
            total = total + wx_ref[k * blocks : (k + 1) * blocks, :] * seq_x[t + k]
            pairs = pairs + wb_ref[k] * seq_b[t + k]
        xs.append(silu(total))
        pairs = silu(pairs)
        turned = jnp.concatenate([pairs[:, LANES // 2 :], pairs[:, : LANES // 2]], 1)
        lower = lax.broadcasted_iota(jnp.int32, pairs.shape, 1) < LANES // 2
        bs.append(jnp.where(lower, pairs, turned))
        cs.append(jnp.where(lower, turned, pairs))
    return xs, bs, cs


def by_group(rows, count):
    groups = rows.shape[0]
    run = count // groups
    return jnp.concatenate(
        [jnp.broadcast_to(rows[g : g + 1], (run, rows.shape[1])) for g in range(groups)], 0
    )


def slot_steps(
    tile, first, wide, scale, xs, bs, cs, dec, dts, skip, gate, write, spread_ref, mixed_ref
):
    steps = len(xs)
    heads = wide.shape[0]
    blocks = xs[0].shape[0]
    lane = lax.broadcasted_iota(jnp.int32, (blocks, LANES), 1)
    lower = lane < LANES // 2
    later = None
    for t in reversed(range(steps)):
        weighted = xs[t] * dts[t]
        if later is not None:
            weighted = weighted * later
        later = dec[t] if later is None else later * dec[t]
        spread_ref[pl.ds(t * heads, blocks, stride=2), :] = jnp.where(lower, weighted, 0.0)
        spread_ref[pl.ds(t * heads + 1, blocks, stride=2), :] = jnp.where(lower, 0.0, weighted)
    high, low = split(spread_ref[...])
    spread = jnp.concatenate([high, low], 1)
    b_rows = [by_group(b, heads) for b in bs]
    c_rows = [by_group(c, heads) for c in cs]
    at = lax.broadcasted_iota(jnp.int32, (2 * LANES, LANES), 0) // P_SIZE
    to = lax.broadcasted_iota(jnp.int32, (2 * LANES, LANES), 1) % P_SIZE
    place = to - at
    mixed = jnp.zeros((steps * heads, LANES), jnp.float32)
    count = P_SIZE * P_SIZE // (2 * LANES)
    for k in range(count):
        chosen = jnp.where(place == first(2 * k) * (LANES // P_SIZE), 1.0, 0.0)
        chosen = chosen.astype(jnp.bfloat16)
        states = [tile(2 * k), tile(2 * k + 1)]
        highs, lows = [], []
        for t in range(steps):
            parts = [split(s * c_rows[t]) for s in states]
            highs.append(jnp.concatenate([p[0] for p in parts], 1))
            lows.append(jnp.concatenate([p[1] for p in parts], 1))
        mixed = mixed + jnp.dot(
            jnp.concatenate(highs, 0), chosen, preferred_element_type=jnp.float32
        )
        mixed = mixed + jnp.dot(
            jnp.concatenate(lows, 0), chosen, preferred_element_type=jnp.float32
        )
        both = jnp.concatenate([chosen, chosen], 1)
        grown = lax.dot_general(
            spread, both, (((1,), (1,)), ((), ())), preferred_element_type=jnp.float32
        )
        for half in range(2):
            new = wide * states[half]
            for t in range(steps):
                piece = grown[t * heads : (t + 1) * heads, half * LANES : (half + 1) * LANES]
                new = new + piece * b_rows[t]
            write(2 * k + half, new)
    for t in range(steps):
        part = mixed[t * heads : (t + 1) * heads]
        if scale is not None:
            part = part * scale
        mixed_ref[t * heads : (t + 1) * heads, :] = part
    gated, sums = [], []
    ahead = None
    weights = []
    for t in range(steps):
        weights = [w * dec[t] for w in weights] + [dts[t]]
        ahead = dec[t] if ahead is None else ahead * dec[t]
        even = mixed_ref[pl.ds(t * heads, blocks, stride=2), :]
        odd = mixed_ref[pl.ds(t * heads + 1, blocks, stride=2), :]
        out = ahead * jnp.where(lower, even, odd) + skip * xs[t]
        for s in range(t + 1):
            inner = 0.5 * jnp.sum(bs[s] * cs[t], axis=1, keepdims=True)
            inner = by_group(jnp.broadcast_to(inner, (inner.shape[0], LANES)), blocks)
            out = out + weights[s] * inner * xs[s]
        out = out * gate[t]
        gated.append(out)
        squares = jnp.sum(jnp.sum(out * out, axis=0, keepdims=True), axis=1, keepdims=True)
        sums.append(jnp.broadcast_to(squares, (1, LANES)))
    return gated, sums


def prep_kernel(
    me_ref, counts_hbm, plan_hbm, x_ref, z_ref, bc_ref, dt_ref, bias_ref, rate_ref, skip_ref,
    wx_ref,
    info_ref, xd_ref, gate_ref, dec_ref, dtd_ref, wide_ref, skipd_ref, wxd_ref, cx_ref, cb_ref,
    counts_ref, plan_ref, sems,
):
    slots, steps, channels = x_ref.shape
    heads = dt_ref.shape[2]
    blocks = channels // LANES
    taps = cx_ref.shape[0]
    me = me_ref[0]
    copies = [
        pltpu.make_async_copy(counts_hbm, counts_ref, sems.at[0]),
        pltpu.make_async_copy(plan_hbm, plan_ref, sems.at[1]),
    ]
    for copy in copies:
        copy.start()
    x = [x_ref[s].astype(jnp.float32) for s in range(slots)]
    for s in range(slots):
        dense_rows(xd_ref.at[s], 0, x[s])
        dense_rows(gate_ref.at[s], 0, z_ref[s].astype(jnp.float32))
    dense_rows(wxd_ref, 0, wx_ref[...])
    gate_ref[...] = silu(gate_ref[...])
    rate = jnp.exp(rate_ref[...])
    raw = [dt_ref[s] + bias_ref[...] for s in range(slots)]
    delta = [jnp.maximum(v, 0.0) + jnp.log1p(jnp.exp(-jnp.abs(v))) for v in raw]
    decay = [jnp.exp(-v * rate) for v in delta]
    at = lax.broadcasted_iota(jnp.int32, (blocks, heads), 0)
    of = lax.broadcasted_iota(jnp.int32, (blocks, heads), 1)
    lines = [v[t : t + 1] for v in delta + decay for t in range(steps)] + [skip_ref[...]]
    spread = jnp.concatenate([jnp.where(of // 2 == at, line, 0.0) for line in lines], 0)
    high = spread.astype(jnp.bfloat16)
    rest = spread - high.astype(jnp.float32)
    middle = rest.astype(jnp.bfloat16)
    low = (rest - middle.astype(jnp.float32)).astype(jnp.bfloat16)
    head = lax.broadcasted_iota(jnp.int32, (heads, LANES), 0)
    lane = lax.broadcasted_iota(jnp.int32, (heads, LANES), 1)
    chosen = jnp.where(head % 2 == lane // (LANES // 2), 1.0, 0.0).astype(jnp.bfloat16)
    out = jnp.dot(high, chosen, preferred_element_type=jnp.float32)
    out = out + jnp.dot(middle, chosen, preferred_element_type=jnp.float32)
    out = out + jnp.dot(low, chosen, preferred_element_type=jnp.float32)
    run = steps * blocks
    for s in range(slots):
        dtd_ref[s] = out[s * run : (s + 1) * run]
        dec_ref[s] = out[(slots + s) * run : (slots + s + 1) * run]
        total = decay[s][:1]
        for t in range(1, steps):
            total = total * decay[s][t : t + 1]
        total = jnp.concatenate([total, total], 1)
        wide = jnp.sum(jnp.where(head == lane, total, 0.0), axis=1, keepdims=True)
        wide_ref[s] = jnp.broadcast_to(wide, (heads, LANES))
    skipd_ref[...] = out[2 * slots * run :]
    for copy in copies:
        copy.wait()
    reqs = plan_ref.shape[0]
    owners = counts_ref.shape[0]
    for d in range(owners):
        info_ref[INFO + d] = 0

    def look(r, carry):
        kept_to, kept_from, has_kept, moved_to, has_moved = carry
        home, local = r // slots, r % slots
        goal = plan_ref[r]
        live = local < counts_ref[home]
        owner, place = goal // slots, goal % slots
        mine = live & (owner == me)
        own = mine & (home == me)
        into = mine & (home != me)

        @pl.when(live & (owner != home))
        def _():
            info_ref[INFO + owner] = home

        return (
            jnp.where(own, place, kept_to), jnp.where(own, local, kept_from),
            jnp.where(own, 1, has_kept), jnp.where(into, place, moved_to),
            jnp.where(into, 1, has_moved),
        )

    carry = (jnp.int32(0),) * 5
    if reqs <= 32:
        for r in range(reqs):
            carry = look(r, carry)
    else:
        carry = lax.fori_loop(0, reqs, look, carry)
    kept_to, kept_from, has_kept, moved_to, has_moved = carry
    moved_to = jnp.where(has_moved > 0, moved_to, jnp.where(has_kept > 0, 1 - kept_to, 0))
    kept_to = 1 - moved_to
    for i, v in enumerate((kept_to, kept_from, has_kept, moved_to, has_moved, me)):
        info_ref[i] = v
    full = [jnp.where(kept_to == s, has_kept, has_moved) > 0 for s in range(slots)]
    for k in range(taps):
        t = steps - taps + k
        rows = [jnp.where(full[s], x[s][t : t + 1], 0.0) for s in range(slots)]
        cx_ref[k] = jnp.concatenate(rows, 0).astype(jnp.bfloat16)
        for s in range(slots):
            pairs = bc_ref[s, t].astype(jnp.float32)
            cb_ref[s, k] = jnp.where(full[s], pairs, 0.0).astype(jnp.bfloat16)


def slot_inputs(slot, steps, x_ref, bc_ref, gate_ref, dec_ref, dt_ref):
    blocks = x_ref.shape[1] // steps
    rows = [pl.ds(t * blocks, blocks) for t in range(steps)]
    return [[ref[slot, r, :] for r in rows] for ref in (x_ref, gate_ref, dec_ref, dt_ref)] + [
        [bc_ref[slot, t].astype(jnp.float32) for t in range(steps)]
    ]


def kept_kernel(
    info_ref, state_ref, cx_ref, cb_ref, x_ref, bc_ref, gate_ref, dec_ref, dt_ref, skip_ref,
    wide_ref, wx_ref, bx_ref, wb_ref, bb_ref,
    out_hbm, gated_ref, sums_ref, spread_ref, mixed_ref, rows_ref, new_ref, sem,
):
    steps = bc_ref.shape[1]
    blocks = bx_ref.shape[0]
    taps = cx_ref.shape[0]
    slot, origin, full = info_ref[0], info_ref[1], info_ref[2] > 0
    cx = cx_ref[...].astype(jnp.float32)
    dense_rows(rows_ref, 0, jnp.where(origin == 0, cx[:, 0], cx[:, 1]))
    cb = of_slot(cb_ref[...].astype(jnp.float32), origin)
    new_x, gate, dec, dts, new_b = slot_inputs(
        slot, steps, x_ref, bc_ref, gate_ref, dec_ref, dt_ref
    )
    seq_x = [rows_ref[k * blocks : (k + 1) * blocks, :] for k in range(taps)] + new_x
    seq_b = [cb[k] for k in range(taps)] + new_b
    xs, bs, cs = small_steps(seq_x, seq_b, wx_ref, bx_ref, wb_ref, bb_ref, steps)

    def write(j, new):
        new_ref[:, j * LANES : (j + 1) * LANES] = jnp.where(full, new, 0.0)

    gated, sums = slot_steps(
        lambda j: state_ref[origin, :, j * LANES : (j + 1) * LANES],
        lambda j: j, wide_ref[slot], None, xs, bs, cs, dec, dts,
        skip_ref[...], gate, write, spread_ref, mixed_ref,
    )
    copy = pltpu.make_async_copy(new_ref, out_hbm.at[slot], sem)
    copy.start()
    for t in range(steps):
        gated_ref[t] = gated[t]
    sums_ref[...] = jnp.concatenate(sums, 0)
    copy.wait()


def moved_kernel(pieces, info_ref, *refs):
    got_refs = refs[:pieces]
    (
        held_hbm, kept_sums_ref, x_ref, bc_ref, gate_ref, dec_ref, dt_ref, skip_ref,
        wide_ref, wx_ref, bx_ref, wb_ref, bb_ref,
        out_hbm, gated_ref, sums_ref, spread_ref, mixed_ref, aux_ref, new_ref, sems,
    ) = refs[pieces:]
    del held_hbm
    direct = pieces > 1
    steps, groups = bc_ref.shape[1:3]
    blocks = bx_ref.shape[0]
    taps = wx_ref.shape[0] // blocks - 1
    heads = wide_ref.shape[1]
    share = got_refs[0].shape[-2] - AUX
    slot, full, me = info_ref[3], info_ref[4] > 0, info_ref[5]
    new_x, gate, dec, dts, new_b = slot_inputs(
        slot, steps, x_ref, bc_ref, gate_ref, dec_ref, dt_ref
    )

    def load(m, rows):
        part = got_refs[m][rows, :] if direct else got_refs[0][m, rows, :]
        return part.astype(jnp.int32).astype(jnp.float32)

    for m in range(pieces if direct else got_refs[0].shape[0]):
        if direct:
            at = pl.ds(pl.multiple_of((me ^ m) * AUX, AUX), AUX)
            aux_ref[at, :] = load(m, pl.ds(share, AUX))
        elif m * AUX < aux_ref.shape[0]:
            aux_ref[m * AUX : (m + 1) * AUX, :] = load(m, pl.ds(share, AUX))

    last = aux_ref[taps * blocks : taps * blocks + AUX, :]
    codes = last[taps * groups : taps * groups + 1]
    row = lax.broadcasted_iota(jnp.int32, (heads, LANES), 0)
    lane = lax.broadcasted_iota(jnp.int32, (heads, LANES), 1)
    code = jnp.sum(jnp.where(row == lane, codes, 0.0), axis=1, keepdims=True)
    scale = level_scale(code) * (1.0 / LEVELS)
    scale_x = level_scale(codes[:, heads : heads + 1]) * (1.0 / LEVELS)
    scale_b = level_scale(codes[:, heads + 1 : heads + 2]) * (1.0 / LEVELS)
    seq_x = [aux_ref[k * blocks : (k + 1) * blocks, :] * scale_x for k in range(taps)] + new_x
    seq_b = [last[k * groups : (k + 1) * groups] * scale_b for k in range(taps)] + new_b
    xs, bs, cs = small_steps(seq_x, seq_b, wx_ref, bx_ref, wb_ref, bb_ref, steps)
    run = min(share, heads)
    each = share // heads
    copies = []

    def tile(j):
        if direct:
            return load(j // each, pl.ds(j % each * heads, heads))
        flats = range(j * heads, (j + 1) * heads, run)
        return jnp.concatenate([load(f // share, pl.ds(f % share, run)) for f in flats], 0)

    def first(j):
        return (me ^ (j // each)) * each + j % each if direct else j

    def write(j, new):
        at = pl.ds(pl.multiple_of(first(j) * LANES, LANES), LANES)
        new_ref[:, at] = jnp.where(full, new, 0.0)
        if direct and j % each == each - 1:
            span = pl.ds(pl.multiple_of(first(j - each + 1) * LANES, LANES), each * LANES)
            copy = pltpu.make_async_copy(
                new_ref.at[:, span], out_hbm.at[slot, :, span], sems.at[j // each]
            )
            copy.start()
            copies.append(copy)

    gated, sums = slot_steps(
        tile, first, wide_ref[slot] * scale, scale, xs, bs, cs, dec, dts,
        skip_ref[...], gate, write, spread_ref, mixed_ref,
    )
    for t in range(steps):
        gated_ref[t] = gated[t]
    sums_ref[...] = jnp.concatenate([kept_sums_ref[...]] + sums, 0)
    if not direct:
        copies.append(pltpu.make_async_copy(new_ref, out_hbm.at[slot], sems.at[0]))
        copies[0].start()
    for copy in copies:
        copy.wait()


def norm_kernel(info_ref, kept_ref, moved_ref, mine_ref, theirs_ref, norm_ref, out_ref, rows_ref):
    steps, blocks = kept_ref.shape[:2]
    factor = lax.rsqrt((mine_ref[...] + theirs_ref[...]) * (1.0 / (H * P_SIZE)) + 1e-05)
    for which, ref in enumerate((kept_ref, moved_ref)):
        slot = info_ref[3 * which]
        full = info_ref[2 + 2 * which] > 0
        for t in range(steps):
            at = which * steps + t
            rows_ref[t * blocks : (t + 1) * blocks, :] = jnp.where(
                full, ref[t] * factor[at : at + 1] * norm_ref[...], 0.0
            )
        for b in range(blocks):
            out_ref[slot, :, b * LANES : (b + 1) * LANES] = rows_ref[
                pl.ds(b, steps, stride=blocks), :
            ].astype(jnp.bfloat16)


def on_device(
    counts,
    move_plan,
    ssm_state,
    conv_x_state,
    conv_bc_state,
    x_in,
    bc_in,
    z_in,
    dt_in,
    conv_w_x,
    conv_b_x,
    conv_w_bc,
    conv_b_bc,
    dt_bias,
    a_log,
    d_skip,
    norm_w,
):
    owners = lax.axis_size("req")
    owner = lax.axis_index("req").astype(jnp.int32)
    slots, heads, columns = ssm_state.shape
    places, steps, channels = x_in.shape
    taps = conv_x_state.shape[1]
    groups, pair = conv_bc_state.shape[2:]
    blocks = channels // LANES
    share = heads * columns // LANES // owners
    aux_rows = taps * blocks + AUX
    f32 = jnp.float32
    direct = owners <= 16 and owners & (owners - 1) == 0 and share % heads == 0
    pieces = owners if direct else 1
    smem = pl.BlockSpec(memory_space=pltpu.SMEM)
    vmem = pl.BlockSpec(memory_space=pltpu.VMEM)
    anywhere = pl.BlockSpec(memory_space=pl.ANY)

    def shaped(*shape, dtype=f32):
        return jax.ShapeDtypeStruct(shape, dtype)

    def call(kernel, name, in_specs, out_specs, out_shape, scratch=(), **more):
        return pl.pallas_call(
            kernel,
            in_specs=in_specs,
            out_specs=out_specs,
            out_shape=out_shape,
            scratch_shapes=scratch,
            compiler_params=pltpu.CompilerParams(vmem_limit_bytes=VMEM_LIMIT),
            name=name,
            **more,
        )

    def in_hbm(*values):
        return [pltpu.with_memory_space_constraint(v, pltpu.MemorySpace.HBM) for v in values]

    me = owner.reshape(1)
    conv_x_taps = jnp.transpose(conv_x_state, (1, 0, 2))
    piece = (share + AUX, LANES) if direct else (owners, share + AUX, LANES)
    sent = [shaped(*piece, dtype=jnp.int16)] * pieces
    payload = call(
        pack_kernel, "pack", [smem] + [anywhere] * 5, [vmem] * pieces, sent,
        [
            pltpu.SMEM(counts.shape, jnp.int32),
            pltpu.SMEM(move_plan.shape, jnp.int32),
            pltpu.VMEM(ssm_state.shape, f32),
            pltpu.VMEM(conv_x_taps.shape, jnp.bfloat16),
            pltpu.VMEM(conv_bc_state.shape, jnp.bfloat16),
            pltpu.VMEM((max(aux_rows, pieces * AUX), LANES), f32),
            pltpu.SemaphoreType.DMA((4 + slots * heads // BLOCK,)),
        ],
    )(me, *in_hbm(counts, move_plan, ssm_state, conv_x_taps, conv_bc_state))

    def exchange(values):
        if not direct:
            return [lax.all_to_all(values[0], "req", split_axis=0, concat_axis=0, tiled=True)]
        out = list(values)
        for k in reversed(range(1, pieces)):
            out[k] = lax.ppermute(values[k], "req", [(i, i ^ k) for i in range(owners)])
        return out

    spread = exchange(payload)

    _, x_late = lax.optimization_barrier((payload[0], x_in))
    rows = (places, steps * blocks, LANES)
    info, x_dense, gate, dec, dt_dense, wide, skip, wx, new_conv_x, new_conv_bc = call(
        prep_kernel, "prep", [smem] + [anywhere] * 2 + [vmem] * 8, [smem] + [vmem] * 9,
        [
            shaped(INFO + owners, dtype=jnp.int32), shaped(*rows), shaped(*rows), shaped(*rows),
            shaped(*rows), shaped(places, heads, LANES), shaped(blocks, LANES),
            shaped((taps + 1) * blocks, LANES),
            shaped(taps, places, channels, dtype=jnp.bfloat16),
            shaped(*conv_bc_state.shape, dtype=jnp.bfloat16),
        ],
        [
            pltpu.SMEM(counts.shape, jnp.int32),
            pltpu.SMEM(move_plan.shape, jnp.int32),
            pltpu.SemaphoreType.DMA((2,)),
        ],
    )(
        me, *in_hbm(counts, move_plan), x_late, z_in, bc_in, dt_in, dt_bias.reshape(1, -1),
        a_log.reshape(1, -1), d_skip.reshape(1, -1), conv_w_x,
    )

    picked = call(
        pick_kernel, "pick", [smem] + [vmem] * pieces, [vmem] * pieces, sent,
        [pltpu.VMEM((owners, *piece), jnp.int16)] if direct else [],
    )(info, *spread)
    got = exchange(picked)

    _, info = lax.optimization_barrier((picked[0], info))
    common = [x_dense, bc_in, gate, dec, dt_dense, skip, wide, wx]
    common += [conv_b_x.reshape(blocks, LANES), conv_w_bc, conv_b_bc]
    scratch = [pltpu.VMEM((steps * heads, LANES), f32)] * 2
    held, kept_gated, kept_sums = call(
        kept_kernel, "kept", [smem] + [vmem] * (3 + len(common)), [anywhere, vmem, vmem],
        [shaped(places, heads, columns), shaped(steps, blocks, LANES), shaped(steps, LANES)],
        scratch
        + [
            pltpu.VMEM((taps * blocks, LANES), f32),
            pltpu.VMEM((heads, columns), f32),
            pltpu.SemaphoreType.DMA,
        ],
    )(info, ssm_state, conv_x_taps, conv_bc_state, *common)
    new_ssm, moved_gated, sums = call(
        functools.partial(moved_kernel, pieces), "moved",
        [smem] + [vmem] * pieces + [anywhere] + [vmem] * (1 + len(common)),
        [anywhere, vmem, vmem],
        [shaped(places, heads, columns), shaped(steps, blocks, LANES), shaped(2 * steps, LANES)],
        scratch
        + [
            pltpu.VMEM((max(aux_rows, pieces * AUX), LANES), f32),
            pltpu.VMEM((heads, columns), f32),
            pltpu.SemaphoreType.DMA((pieces,)),
        ],
        input_output_aliases={1 + pieces: 0},
    )(info, *got, held, kept_sums, *common)

    theirs = lax.ppermute(sums, "tp", [(0, 1), (1, 0)])
    y_out = call(
        norm_kernel, "norm", [smem] + [vmem] * 5, vmem,
        shaped(places, steps, channels, dtype=jnp.bfloat16),
        [pltpu.VMEM((steps * blocks, LANES), f32)],
    )(info, kept_gated, moved_gated, sums, theirs, norm_w.reshape(blocks, LANES))
    return (y_out, new_ssm, jnp.transpose(new_conv_x, (1, 0, 2)), new_conv_bc)


def solution(mesh):
    in_specs = (
        P("parts"),
        P("parts"),
        P(("parts", "req"), "tp", None),
        P(("parts", "req"), None, "tp"),
        P(("parts", "req"), None, "tp", None),
        P(("parts", "req"), None, "tp"),
        P(("parts", "req"), None, "tp", None),
        P(("parts", "req"), None, "tp"),
        P(("parts", "req"), None, "tp"),
        P(None, "tp"),
        P("tp"),
        P(None, "tp", None),
        P("tp", None),
        P("tp"),
        P("tp"),
        P("tp"),
        P("tp"),
    )
    out_specs = (
        P(("parts", "req"), None, "tp"),
        P(("parts", "req"), "tp", None),
        P(("parts", "req"), None, "tp"),
        P(("parts", "req"), None, "tp", None),
    )
    return jax.shard_map(
        on_device, mesh=mesh, in_specs=in_specs, out_specs=out_specs, check_vma=False
    )
```

time: 56.7 us -> 46.4 us (0.82)
  starting transfers between devices: 11.2 us -> 24.2 us
  waiting for transfers between devices: 18.3 us -> 5.39 us
  local copies, waits for them, and re-layouts: 9.22 us -> 2.57 us
  other arithmetic: 3.81 us -> 0 us
  between operations: 3.46 us -> 0.87 us
  Pallas kernels: 10.2 us -> 12.6 us
    ppermute x0 -> x14, starting transfers between devices: none -> 24.2 us  [exchange(): out[k] = lax.ppermute(values[k], 'req', [(i, i ^ k) for i in range(owners)])]
    all_to_all x2 -> x0, waiting for transfers between devices: 17.8 us -> none  [the longest x1 14.6 us: on_device(): got = lax.all_to_all(picked, 'req', split_axis=0, concat_axis=0, tiled=True)]
    all_to_all x2 -> x0, starting transfers between devices: 11.2 us -> none  [the longest x1 7.4 us: on_device(): lax.all_to_all(payload, 'req', split_axis=0, concat_axis=0, tiled=True)]
    ppermute x0 -> x14, waiting for transfers between devices: none -> 4.24 us  [exchange(): out[k] = lax.ppermute(values[k], 'req', [(i, i ^ k) for i in range(owners)])]
    pallas_call x4 -> x6, Pallas kernels: 10.2 us -> 12.6 us  [the longest x1 3.63 us: on_device(): call(kept_kernel, 'kept', [smem] + [vmem] * (3 + len(common)), [anywhere,...]
    unnamed x46 -> x30, local copies, waits for them, and re-layouts: 4.55 us -> 2.57 us
    gather x1 -> x0, local copies, waits for them, and re-layouts: 1.47 us -> none  [on_device(): picked = jnp.take(spread, source, axis=0, mode='clip')]
    select_n x3 -> x0, other arithmetic: 1.38 us -> none  [the longest x1 0.73 us: on_device(): jnp.where(filled[:, None, None], last_x, jnp.zeros_like(last_x))]
  transfers between devices with their start and end apart: 3 -> 15, of which waited for: 3 -> 4; matrix products, arithmetic and copies ran while one was open for 12% -> 0% of each run, Pallas kernels for 6% -> 12%
where the time goes in v2:
time: 46.4 us; the launch traced here: 45.7 us
  starting transfers between devices  24.2 us (52%)
  Pallas kernels  12.6 us (27%)
  waiting for transfers between devices  5.39 us (12%)
  local copies, waits for them, and re-layouts  2.57 us (6%)
  between operations  0.87 us (2%)
    ppermute x14, starting transfers between devices, exchange(): out[k] = lax.ppermute(values[k], 'req', [(i, i ^ k) for i in range(owners)])  24.2 us
    ppermute x14, waiting for transfers between devices, exchange(): out[k] = lax.ppermute(values[k], 'req', [(i, i ^ k) for i in range(owners)])  4.24 us
    pallas_call x1, Pallas kernels, on_device(): call(kept_kernel, 'kept', [smem] + [vmem] * (3 + len(common)), [anywhere,...  3.63 us
    pallas_call x1, Pallas kernels, on_device(): call(functools.partial(moved_kernel, pieces), 'moved', [smem] + [vmem] *...  3.4 us
    unnamed x30, local copies, waits for them, and re-layouts  2.57 us
    pallas_call x1, Pallas kernels, on_device(): call(pack_kernel, 'pack', [smem] + [anywhere] * 5, [vmem] * pieces, sent,...  1.93 us
    pallas_call x1, Pallas kernels, on_device(): call(prep_kernel, 'prep', [smem] + [anywhere] * 2 + [vmem] * 8, [smem] +...  1.76 us
    pallas_call x1, Pallas kernels, on_device(): call(norm_kernel, 'norm', [smem] + [vmem] * 5, vmem, shaped(places, steps...  1.29 us
  transfers between devices with their start and end apart: 15, of which 4 were waited for; matrix products, arithmetic and copies ran while one was open for 0% of the time, Pallas kernels for 12%

profile of v2, /device:TPU:0, one launch (start us, length us, event | category | flops | bytes accessed | tf_op | source)
XLA Modules:
  0.0 45.7 jit_solution(6856976159260222750)
XLA Ops:
  0.7 1.9 %pack.1 = (s16[272,128]{1,0:T(8,128)(2,1)S(1)}, s16[272,128]{1,0:T(8,128)(2,1)S(1)}, s16[272,128]{1,0:T(8,128)(2,1)S(1)}, s16[272,128]{1,0:T(8,128)(2,1)S(1)}, s...) custom-call(s32[1]{0:T(128)} %bitcast.me_ref, ...), custom_call_target="tpu_custom_call" | custom-call | tf_op jit(solution)/shard_map/pack/pallas_call | solution.py:569
  2.7 3.0 %collective-permute-start = (s16[272,128]{1,0:T(8,128)(2,1)S(1)}, s16[272,128]{1,0:T(8,128)(2,1)S(1)}, u32[]{:S(2)}, u32[]{:S(2)}) collective-permute-start(s16[272,128]{1,0:T(8,128)(2,1)S(1)} %get-tuple-element.41), channel_id=1, source_target_pairs={{0,2},{2,0},{4,6},{6,4},{8,10},{10,8},{12,14},{14,12},{1,3},{3,1},... | collective-permute-start | bytes 208904 | tf_op jit(solution)/shard_map/ppermute | solution.py:587
  5.7 1.6 %collective-permute-start.1 = (s16[272,128]{1,0:T(8,128)(2,1)S(1)}, s16[272,128]{1,0:T(8,128)(2,1)S(1)}, u32[]{:S(2)}, u32[]{:S(2)}) collective-permute-start(s16[272,128]{1,0:T(8,128)(2,1)S(1)} %get-tuple-element.42), channel_id=1, source_target_pairs={{0,4},{2,6},{4,0},{6,2},{8,12},{10,14},{12,8},{14,10},{1,5},{3,7},... | collective-permute-start | bytes 208904 | tf_op jit(solution)/shard_map/ppermute | solution.py:587
  7.3 3.0 %collective-permute-start.3 = (s16[272,128]{1,0:T(8,128)(2,1)S(1)}, s16[272,128]{1,0:T(8,128)(2,1)S(1)}, u32[]{:S(2)}, u32[]{:S(2)}) collective-permute-start(s16[272,128]{1,0:T(8,128)(2,1)S(1)} %get-tuple-element.44), channel_id=1, source_target_pairs={{0,8},{2,10},{4,12},{6,14},{8,0},{10,2},{12,4},{14,6},{1,9},{3,11}... | collective-permute-start | bytes 208904 | tf_op jit(solution)/shard_map/ppermute | solution.py:587
  10.3 1.3 %collective-permute-start.4 = (s16[272,128]{1,0:T(8,128)(2,1)S(1)}, s16[272,128]{1,0:T(8,128)(2,1)S(1)}, u32[]{:S(2)}, u32[]{:S(2)}) collective-permute-start(s16[272,128]{1,0:T(8,128)(2,1)S(1)} %get-tuple-element.45), channel_id=1, source_target_pairs={{0,10},{2,8},{4,14},{6,12},{8,2},{10,0},{12,6},{14,4},{1,11},{3,9}... | collective-permute-start | bytes 208904 | tf_op jit(solution)/shard_map/ppermute | solution.py:587
  11.5 3.6 %collective-permute-start.5 = (s16[272,128]{1,0:T(8,128)(2,1)S(1)}, s16[272,128]{1,0:T(8,128)(2,1)S(1)}, u32[]{:S(2)}, u32[]{:S(2)}) collective-permute-start(s16[272,128]{1,0:T(8,128)(2,1)S(1)} %get-tuple-element.46), channel_id=1, source_target_pairs={{0,12},{2,14},{4,8},{6,10},{8,4},{10,6},{12,0},{14,2},{1,13},{3,15... | collective-permute-start | bytes 208904 | tf_op jit(solution)/shard_map/ppermute | solution.py:587
  15.2 0.8 %copy-done.3 = bf16[2,4,4096]{2,1,0:T(4,128)(2,1)S(1)} copy-done((bf16[2,4,4096]{2,1,0:T(4,128)(2,1)S(1)}, bf16[2,4,4096]{2,1,0:T(4,128)(2,1)}, u32[]{:S(2)}) %copy-start.3) | copy-done | bytes 65560
  16.1 0.8 %copy-done.4 = bf16[2,4,4096]{2,1,0:T(4,128)(2,1)S(1)} copy-done((bf16[2,4,4096]{2,1,0:T(4,128)(2,1)S(1)}, bf16[2,4,4096]{2,1,0:T(4,128)(2,1)}, u32[]{:S(2)}) %copy-start.4) | copy-done | bytes 65560
  16.9 0.8 %copy-done.5 = f32[4,4096]{1,0:T(4,128)S(1)} copy-done((f32[4,4096]{1,0:T(4,128)S(1)}, f32[4,4096]{1,0:T(4,128)}, u32[]{:S(2)}) %copy-start.5) | copy-done | bytes 65560
  17.7 1.8 %prep.1 = (s32[16]{0:T(128)S(1)}, f32[2,128,128]{2,1,0:T(8,128)S(1)}, f32[2,128,128]{2,1,0:T(8,128)S(1)}, f32[2,128,128]{2,1,0:T(8,128)S(1)}, f32[2,128,128]{2,1...) custom-call(s32[1]{0:T(128)} %bitcast.me_ref, ...), custom_call_target="tpu_custom_call" | custom-call | tf_op jit(solution)/shard_map/prep/pallas_call | solution.py:594
  19.5 1.5 %collective-permute-done.4.refs_5_ = s16[272,128]{1,0:T(8,128)(2,1)S(1)} collective-permute-done((s16[272,128]{1,0:T(8,128)(2,1)S(1)}, s16[272,128]{1,0:T(8,128)(2,1)S(1)}, u32[]{:S(2)}, u32[]{:S(2)}) %collective-permute-start.4) | collective-permute-done | bytes 69664 | tf_op jit(solution)/shard_map/ppermute | solution.py:587
  21.0 1.3 %collective-permute-done.6.refs_7_ = s16[272,128]{1,0:T(8,128)(2,1)S(1)} collective-permute-done((s16[272,128]{1,0:T(8,128)(2,1)S(1)}, s16[272,128]{1,0:T(8,128)(2,1)S(1)}, u32[]{:S(2)}, u32[]{:S(2)}) %collective-permute-start.6) | collective-permute-done | bytes 69664 | tf_op jit(solution)/shard_map/ppermute | solution.py:587
  22.3 0.6 %pick.1 = (s16[272,128]{1,0:T(8,128)(2,1)S(1)}, s16[272,128]{1,0:T(8,128)(2,1)S(1)}, s16[272,128]{1,0:T(8,128)(2,1)S(1)}, s16[272,128]{1,0:T(8,128)(2,1)S(1)}, s...) custom-call(s32[16]{0:T(128)S(1)} %get-tuple-element.49.info_ref, ...), custom_call_target="tpu_custom_call" | custom-call | tf_op jit(solution)/shard_map/pick/pallas_call | solution.py:613
  22.9 0.6 %collective-permute-start.7 = (s16[272,128]{1,0:T(8,128)(2,1)S(1)}, s16[272,128]{1,0:T(8,128)(2,1)S(1)}, u32[]{:S(2)}, u32[]{:S(2)}) collective-permute-start(s16[272,128]{1,0:T(8,128)(2,1)S(1)} %get-tuple-element.58), channel_id=1, source_target_pairs={{0,2},{2,0},{4,6},{6,4},{8,10},{10,8},{12,14},{14,12},{1,3},{3,1},... | collective-permute-start | bytes 208904 | tf_op jit(solution)/shard_map/ppermute | solution.py:587
  23.5 2.6 %collective-permute-start.8 = (s16[272,128]{1,0:T(8,128)(2,1)S(1)}, s16[272,128]{1,0:T(8,128)(2,1)S(1)}, u32[]{:S(2)}, u32[]{:S(2)}) collective-permute-start(s16[272,128]{1,0:T(8,128)(2,1)S(1)} %get-tuple-element.59), channel_id=1, source_target_pairs={{0,4},{2,6},{4,0},{6,2},{8,12},{10,14},{12,8},{14,10},{1,5},{3,7},... | collective-permute-start | bytes 208904 | tf_op jit(solution)/shard_map/ppermute | solution.py:587
  26.0 0.7 %collective-permute-start.9 = (s16[272,128]{1,0:T(8,128)(2,1)S(1)}, s16[272,128]{1,0:T(8,128)(2,1)S(1)}, u32[]{:S(2)}, u32[]{:S(2)}) collective-permute-start(s16[272,128]{1,0:T(8,128)(2,1)S(1)} %get-tuple-element.60), channel_id=1, source_target_pairs={{0,6},{2,4},{4,2},{6,0},{8,14},{10,12},{12,10},{14,8},{1,7},{3,5},... | collective-permute-start | bytes 208904 | tf_op jit(solution)/shard_map/ppermute | solution.py:587
  26.7 3.1 %collective-permute-start.10 = (s16[272,128]{1,0:T(8,128)(2,1)S(1)}, s16[272,128]{1,0:T(8,128)(2,1)S(1)}, u32[]{:S(2)}, u32[]{:S(2)}) collective-permute-start(s16[272,128]{1,0:T(8,128)(2,1)S(1)} %get-tuple-element.61), channel_id=1, source_target_pairs={{0,8},{2,10},{4,12},{6,14},{8,0},{10,2},{12,4},{14,6},{1,9},{3,11}... | collective-permute-start | bytes 208904 | tf_op jit(solution)/shard_map/ppermute | solution.py:587
  29.9 2.3 %collective-permute-start.12 = (s16[272,128]{1,0:T(8,128)(2,1)S(1)}, s16[272,128]{1,0:T(8,128)(2,1)S(1)}, u32[]{:S(2)}, u32[]{:S(2)}) collective-permute-start(s16[272,128]{1,0:T(8,128)(2,1)S(1)} %get-tuple-element.63), channel_id=1, source_target_pairs={{0,12},{2,14},{4,8},{6,10},{8,4},{10,6},{12,0},{14,2},{1,13},{3,15... | collective-permute-start | bytes 208904 | tf_op jit(solution)/shard_map/ppermute | solution.py:587
  32.2 2.4 %collective-permute-start.13 = (s16[272,128]{1,0:T(8,128)(2,1)S(1)}, s16[272,128]{1,0:T(8,128)(2,1)S(1)}, u32[]{:S(2)}, u32[]{:S(2)}) collective-permute-start(s16[272,128]{1,0:T(8,128)(2,1)S(1)} %get-tuple-element.64), channel_id=1, source_target_pairs={{0,14},{2,12},{4,10},{6,8},{8,6},{10,4},{12,2},{14,0},{1,15},{3,13... | collective-permute-start | bytes 208904 | tf_op jit(solution)/shard_map/ppermute | solution.py:587
  34.6 3.6 %kept.1 = (f32[2,64,4096]{2,1,0:T(8,128)}, f32[4,32,128]{2,1,0:T(8,128)S(1)}, f32[4,128]{1,0:T(4,128)S(1)}) custom-call(s32[16]{0:T(128)S(1)} %get-tuple-element.49.info_ref, f32[2,64,4096]{2,1,0:T(8,128)S(1)} %copy-done, bf16[3,2,4096]{2,1,0:T(2,128)(2,1)S(1)} %bitcast.9, bf16[2,3,2,128]{3,2,1,0:T(2,128)(2,1)S(1)} %copy-done.9, ...), custom_call_target="tpu_custom_call" | custom-call | tf_op jit(solution)/shard_map/kept/pallas_call | solution.py:623
  38.3 1.5 %collective-permute-done.11.refs_5_ = s16[272,128]{1,0:T(8,128)(2,1)S(1)} collective-permute-done((s16[272,128]{1,0:T(8,128)(2,1)S(1)}, s16[272,128]{1,0:T(8,128)(2,1)S(1)}, u32[]{:S(2)}, u32[]{:S(2)}) %collective-permute-start.11) | collective-permute-done | bytes 69664 | tf_op jit(solution)/shard_map/ppermute | solution.py:587
  39.8 3.4 %moved.1 = (f32[2,64,4096]{2,1,0:T(8,128)}, f32[4,32,128]{2,1,0:T(8,128)S(1)}, f32[8,128]{1,0:T(8,128)S(1)}) custom-call(s32[16]{0:T(128)S(1)} %get-tuple-element.49.info_ref, s16[272,128]{1,0:T(8,128)(2,1)S(1)} %get-tuple-element.48.refs_0_, s16[272,128]{1,0:T(8,128)(2,1)S(1)} %collective-permute-done.7.refs_1_, ...), custom_call_target="tpu_custom_call", output_to_operand_aliasing={{0}: (9, {})} | custom-call | tf_op jit(solution)/shard_map/moved/pallas_call | solution.py:633
  43.2 1.2 %collective-permute-done.14.theirs_ref = f32[8,128]{1,0:T(8,128)S(1)} collective-permute-done((f32[8,128]{1,0:T(8,128)S(1)}, f32[8,128]{1,0:T(8,128)S(1)}, u32[]{:S(2)}, u32[]{:S(2)}) %collective-permute-start.14) | collective-permute-done | bytes 4128 | tf_op jit(solution)/shard_map/ppermute | solution.py:647
  44.4 1.3 %norm.1 = bf16[2,4,4096]{2,1,0:T(4,128)(2,1)} custom-call(s32[16]{0:T(128)S(1)} %get-tuple-element.49.info_ref, f32[4,32,128]{2,1,0:T(8,128)S(1)} %get-tuple-element.57.kept_ref, f32[4,32,128]{2,1,0:T(8,128)S(1)} %get-tuple-element.67.moved_ref, f32[8,128]{1,0:T(8,128)S(1)} %get-tuple-element.68.mine_ref, f32[8,128]{1,0:T(8,128)S(1)} %collective-permute-done.14.theirs_ref, ...), custom_call_target="tpu_custom_call" | custom-call | tf_op jit(solution)/shard_map/norm/pallas_call | solution.py:648
  (42 shorter events, 0.2 us)
Async XLA Ops:
  0.6 33.9 %copy-start.9 = (bf16[2,3,2,128]{3,2,1,0:T(2,128)(2,1)S(1)}, bf16[2,3,2,128]{3,2,1,0:T(2,128)(2,1)}, u32[]{:S(2)}) copy-start(bf16[2,3,2,128]{3,2,1,0:T(2,128)(2,1)} %cb_ref.1) | copy-start | bytes 9220
  0.6 33.9 %copy-start = (f32[2,64,4096]{2,1,0:T(8,128)S(1)}, f32[2,64,4096]{2,1,0:T(8,128)}, u32[]{:S(2)}) copy-start(f32[2,64,4096]{2,1,0:T(8,128)} %state_ref.1) | copy-start | bytes 6291460
  0.7 33.9 %copy-start.1 = (bf16[2,3,4096]{2,0,1:T(2,128)(2,1)S(1)}, bf16[2,3,4096]{2,0,1:T(2,128)(2,1)}, u32[]{:S(2)}) copy-start(bf16[2,3,4096]{2,0,1:T(2,128)(2,1)} %param.20) | copy-start | bytes 147460
  0.7 14.5 %copy-start.6 = (bf16[2,4,2,128]{3,2,1,0:T(2,128)(2,1)S(1)}, bf16[2,4,2,128]{3,2,1,0:T(2,128)(2,1)}, u32[]{:S(2)}) copy-start(bf16[2,4,2,128]{3,2,1,0:T(2,128)(2,1)} %refs_11_.1) | copy-start | bytes 12292
  0.7 14.5 %copy-start.14 = (f32[64]{0:T(128)S(1)}, f32[64]{0:T(128)}, u32[]{:S(2)}) copy-start(f32[64]{0:T(128)} %param.32) | copy-start | bytes 772
  0.7 14.5 %copy-start.13 = (f32[64]{0:T(128)S(1)}, f32[64]{0:T(128)}, u32[]{:S(2)}) copy-start(f32[64]{0:T(128)} %param.31) | copy-start | bytes 772
  0.7 33.9 %copy-start.10 = (f32[2,128]{1,0:T(2,128)S(1)}, f32[2,128]{1,0:T(2,128)}, u32[]{:S(2)}) copy-start(f32[2,128]{1,0:T(2,128)} %refs_20_.1) | copy-start | bytes 3076
  0.7 33.9 %copy-start.7 = (f32[4,2,128]{2,1,0:T(2,128)S(1)}, f32[4,2,128]{2,1,0:T(2,128)}, u32[]{:S(2)}) copy-start(f32[4,2,128]{2,1,0:T(2,128)} %refs_19_.1) | copy-start | bytes 12292
  0.7 33.9 %copy-start.2 = (f32[4096]{0:T(1024)S(1)}, f32[4096]{0:T(1024)}, u32[]{:S(2)}) copy-start(f32[4096]{0:T(1024)} %param.27) | copy-start | bytes 49156
  2.7 8.9 %collective-permute-start = (s16[272,128]{1,0:T(8,128)(2,1)S(1)}, s16[272,128]{1,0:T(8,128)(2,1)S(1)}, u32[]{:S(2)}, u32[]{:S(2)}) collective-permute-start(s16[272,128]{1,0:T(8,128)(2,1)S(1)} %get-tuple-element.41), channel_id=1, source_target_pairs={{0,2},{2,0},{4,6},{6,4},{8,10},{10,8},{12,14},{14,12},{1,3},{3,1},... | collective-permute-start | bytes 208904 | tf_op jit(solution)/shard_map/ppermute | solution.py:587
  5.7 9.5 %collective-permute-start.1 = (s16[272,128]{1,0:T(8,128)(2,1)S(1)}, s16[272,128]{1,0:T(8,128)(2,1)S(1)}, u32[]{:S(2)}, u32[]{:S(2)}) collective-permute-start(s16[272,128]{1,0:T(8,128)(2,1)S(1)} %get-tuple-element.42), channel_id=1, source_target_pairs={{0,4},{2,6},{4,0},{6,2},{8,12},{10,14},{12,8},{14,10},{1,5},{3,7},... | collective-permute-start | bytes 208904 | tf_op jit(solution)/shard_map/ppermute | solution.py:587
  7.3 12.2 %collective-permute-start.2 = (s16[272,128]{1,0:T(8,128)(2,1)S(1)}, s16[272,128]{1,0:T(8,128)(2,1)S(1)}, u32[]{:S(2)}, u32[]{:S(2)}) collective-permute-start(s16[272,128]{1,0:T(8,128)(2,1)S(1)} %get-tuple-element.43), channel_id=1, source_target_pairs={{0,6},{2,4},{4,2},{6,0},{8,14},{10,12},{12,10},{14,8},{1,7},{3,5},... | collective-permute-start | bytes 208904 | tf_op jit(solution)/shard_map/ppermute | solution.py:587
  7.3 12.3 %collective-permute-start.3 = (s16[272,128]{1,0:T(8,128)(2,1)S(1)}, s16[272,128]{1,0:T(8,128)(2,1)S(1)}, u32[]{:S(2)}, u32[]{:S(2)}) collective-permute-start(s16[272,128]{1,0:T(8,128)(2,1)S(1)} %get-tuple-element.44), channel_id=1, source_target_pairs={{0,8},{2,10},{4,12},{6,14},{8,0},{10,2},{12,4},{14,6},{1,9},{3,11}... | collective-permute-start | bytes 208904 | tf_op jit(solution)/shard_map/ppermute | solution.py:587
  10.3 10.7 %collective-permute-start.4 = (s16[272,128]{1,0:T(8,128)(2,1)S(1)}, s16[272,128]{1,0:T(8,128)(2,1)S(1)}, u32[]{:S(2)}, u32[]{:S(2)}) collective-permute-start(s16[272,128]{1,0:T(8,128)(2,1)S(1)} %get-tuple-element.45), channel_id=1, source_target_pairs={{0,10},{2,8},{4,14},{6,12},{8,2},{10,0},{12,6},{14,4},{1,11},{3,9}... | collective-permute-start | bytes 208904 | tf_op jit(solution)/shard_map/ppermute | solution.py:587
  11.5 9.4 %collective-permute-start.5 = (s16[272,128]{1,0:T(8,128)(2,1)S(1)}, s16[272,128]{1,0:T(8,128)(2,1)S(1)}, u32[]{:S(2)}, u32[]{:S(2)}) collective-permute-start(s16[272,128]{1,0:T(8,128)(2,1)S(1)} %get-tuple-element.46), channel_id=1, source_target_pairs={{0,12},{2,14},{4,8},{6,10},{8,4},{10,6},{12,0},{14,2},{1,13},{3,15... | collective-permute-start | bytes 208904 | tf_op jit(solution)/shard_map/ppermute | solution.py:587
  15.1 7.1 %collective-permute-start.6 = (s16[272,128]{1,0:T(8,128)(2,1)S(1)}, s16[272,128]{1,0:T(8,128)(2,1)S(1)}, u32[]{:S(2)}, u32[]{:S(2)}) collective-permute-start(s16[272,128]{1,0:T(8,128)(2,1)S(1)} %get-tuple-element.47), channel_id=1, source_target_pairs={{0,14},{2,12},{4,10},{6,8},{8,6},{10,4},{12,2},{14,0},{1,15},{3,13... | collective-permute-start | bytes 208904 | tf_op jit(solution)/shard_map/ppermute | solution.py:587
  22.9 7.0 %collective-permute-start.7 = (s16[272,128]{1,0:T(8,128)(2,1)S(1)}, s16[272,128]{1,0:T(8,128)(2,1)S(1)}, u32[]{:S(2)}, u32[]{:S(2)}) collective-permute-start(s16[272,128]{1,0:T(8,128)(2,1)S(1)} %get-tuple-element.58), channel_id=1, source_target_pairs={{0,2},{2,0},{4,6},{6,4},{8,10},{10,8},{12,14},{14,12},{1,3},{3,1},... | collective-permute-start | bytes 208904 | tf_op jit(solution)/shard_map/ppermute | solution.py:587
  23.5 8.7 %collective-permute-start.8 = (s16[272,128]{1,0:T(8,128)(2,1)S(1)}, s16[272,128]{1,0:T(8,128)(2,1)S(1)}, u32[]{:S(2)}, u32[]{:S(2)}) collective-permute-start(s16[272,128]{1,0:T(8,128)(2,1)S(1)} %get-tuple-element.59), channel_id=1, source_target_pairs={{0,4},{2,6},{4,0},{6,2},{8,12},{10,14},{12,8},{14,10},{1,5},{3,7},... | collective-permute-start | bytes 208904 | tf_op jit(solution)/shard_map/ppermute | solution.py:587
  26.0 12.2 %collective-permute-start.9 = (s16[272,128]{1,0:T(8,128)(2,1)S(1)}, s16[272,128]{1,0:T(8,128)(2,1)S(1)}, u32[]{:S(2)}, u32[]{:S(2)}) collective-permute-start(s16[272,128]{1,0:T(8,128)(2,1)S(1)} %get-tuple-element.60), channel_id=1, source_target_pairs={{0,6},{2,4},{4,2},{6,0},{8,14},{10,12},{12,10},{14,8},{1,7},{3,5},... | collective-permute-start | bytes 208904 | tf_op jit(solution)/shard_map/ppermute | solution.py:587
  26.7 11.5 %collective-permute-start.10 = (s16[272,128]{1,0:T(8,128)(2,1)S(1)}, s16[272,128]{1,0:T(8,128)(2,1)S(1)}, u32[]{:S(2)}, u32[]{:S(2)}) collective-permute-start(s16[272,128]{1,0:T(8,128)(2,1)S(1)} %get-tuple-element.61), channel_id=1, source_target_pairs={{0,8},{2,10},{4,12},{6,14},{8,0},{10,2},{12,4},{14,6},{1,9},{3,11}... | collective-permute-start | bytes 208904 | tf_op jit(solution)/shard_map/ppermute | solution.py:587
  29.8 9.9 %collective-permute-start.11 = (s16[272,128]{1,0:T(8,128)(2,1)S(1)}, s16[272,128]{1,0:T(8,128)(2,1)S(1)}, u32[]{:S(2)}, u32[]{:S(2)}) collective-permute-start(s16[272,128]{1,0:T(8,128)(2,1)S(1)} %get-tuple-element.62), channel_id=1, source_target_pairs={{0,10},{2,8},{4,14},{6,12},{8,2},{10,0},{12,6},{14,4},{1,11},{3,9}... | collective-permute-start | bytes 208904 | tf_op jit(solution)/shard_map/ppermute | solution.py:587
  29.9 9.9 %collective-permute-start.12 = (s16[272,128]{1,0:T(8,128)(2,1)S(1)}, s16[272,128]{1,0:T(8,128)(2,1)S(1)}, u32[]{:S(2)}, u32[]{:S(2)}) collective-permute-start(s16[272,128]{1,0:T(8,128)(2,1)S(1)} %get-tuple-element.63), channel_id=1, source_target_pairs={{0,12},{2,14},{4,8},{6,10},{8,4},{10,6},{12,0},{14,2},{1,13},{3,15... | collective-permute-start | bytes 208904 | tf_op jit(solution)/shard_map/ppermute | solution.py:587
  32.2 7.5 %collective-permute-start.13 = (s16[272,128]{1,0:T(8,128)(2,1)S(1)}, s16[272,128]{1,0:T(8,128)(2,1)S(1)}, u32[]{:S(2)}, u32[]{:S(2)}) collective-permute-start(s16[272,128]{1,0:T(8,128)(2,1)S(1)} %get-tuple-element.64), channel_id=1, source_target_pairs={{0,14},{2,12},{4,10},{6,8},{8,6},{10,4},{12,2},{14,0},{1,15},{3,13... | collective-permute-start | bytes 208904 | tf_op jit(solution)/shard_map/ppermute | solution.py:587
  43.2 1.2 %collective-permute-start.14 = (f32[8,128]{1,0:T(8,128)S(1)}, f32[8,128]{1,0:T(8,128)S(1)}, u32[]{:S(2)}, u32[]{:S(2)}) collective-permute-start(f32[8,128]{1,0:T(8,128)S(1)} %get-tuple-element.68.mine_ref), channel_id=1, source_target_pairs={{0,1},{1,0},{2,3},{3,2},{4,5},{5,4},{6,7},{7,6},{8,9},{9,8},{10,11... | collective-permute-start | bytes 12296 | tf_op jit(solution)/shard_map/ppermute | solution.py:647
  (6 other events, 37.7 us)

commit v3 on v2

--- a/solution.py
+++ b/solution.py
@@ -12,6 +12,7 @@
 LANES = 128
 AUX = 16
 BLOCK = 16
+QUAD = 4
 INFO = 8
 REACH = 6.0
 LEVELS = 32767.0
@@ -51,7 +52,7 @@
     return jnp.where(slot == 0, values[0], values[1])
 
 
-def pack_kernel(me_ref, counts_hbm, plan_hbm, state_hbm, cx_hbm, cb_hbm, *refs):
+def pack_kernel(masks, me_ref, counts_hbm, plan_hbm, state_hbm, cx_hbm, cb_hbm, *refs):
     *out_refs, counts_ref, plan_ref, state_ref, cx_ref, cb_ref, rows_ref, sems = refs
     direct = len(out_refs) > 1
     slots, heads, columns = state_ref.shape
@@ -111,7 +112,7 @@
         codes = codes + jnp.sum(jnp.where(row + at == lane, code, 0.0), axis=0, keepdims=True)
         factor = jnp.broadcast_to(LEVELS / level_scale(code), (BLOCK, LANES))
         for j in range(columns // LANES):
-            place = (me ^ (j // each)) * each + j % each if direct else j
+            place = (me ^ masks[j // each]) * each + j % each if direct else j
             lanes = pl.ds(pl.multiple_of(place * LANES, LANES), LANES)
             tile = state_ref[slot, at : at + BLOCK, lanes] * factor
             tile = jnp.round(tile).astype(jnp.int32).astype(jnp.int16)
@@ -130,7 +131,7 @@
     rows_ref[last : last + AUX, :] = jnp.where(line == taps * groups, codes, values)
     for m in range(owners):
         if direct:
-            values = rows_ref[pl.ds(pl.multiple_of((me ^ m) * AUX, AUX), AUX), :]
+            values = rows_ref[pl.ds(pl.multiple_of((me ^ masks[m]) * AUX, AUX), AUX), :]
         elif m * AUX < last + AUX:
             values = rows_ref[m * AUX : (m + 1) * AUX, :]
         else:
@@ -142,7 +143,7 @@
             out_refs[0][m, share:, :] = values
 
 
-def pick_kernel(info_ref, *refs):
+def pick_kernel(masks, info_ref, *refs):
     if len(refs) == 2:
         in_ref, out_ref = refs
         for m in range(out_ref.shape[0]):
@@ -152,10 +153,10 @@
     *in_refs, all_ref = refs[:owners] + refs[-1:]
     out_refs = refs[owners:-1]
     me = info_ref[5]
-    for k in range(owners):
-        all_ref[k] = in_refs[k][...]
-    for k in range(owners):
-        out_refs[k][...] = all_ref[info_ref[INFO + (me ^ k)] ^ me]
+    for i, k in enumerate(masks):
+        all_ref[k] = in_refs[i][...]
+    for i, k in enumerate(masks):
+        out_refs[i][...] = all_ref[info_ref[INFO + (me ^ k)] ^ me]
 
 
 def silu(v):
@@ -195,61 +196,97 @@
     )
 
 
-def slot_steps(
-    tile, first, wide, scale, xs, bs, cs, dec, dts, skip, gate, write, spread_ref, mixed_ref
-):
-    steps = len(xs)
-    heads = wide.shape[0]
+def spread_x(xs, dec, dts, spread_ref):
     blocks = xs[0].shape[0]
-    lane = lax.broadcasted_iota(jnp.int32, (blocks, LANES), 1)
-    lower = lane < LANES // 2
+    heads = 2 * blocks
+    lower = lax.broadcasted_iota(jnp.int32, (blocks, LANES), 1) < LANES // 2
     later = None
-    for t in reversed(range(steps)):
+    for t in reversed(range(len(xs))):
         weighted = xs[t] * dts[t]
         if later is not None:
             weighted = weighted * later
         later = dec[t] if later is None else later * dec[t]
         spread_ref[pl.ds(t * heads, blocks, stride=2), :] = jnp.where(lower, weighted, 0.0)
         spread_ref[pl.ds(t * heads + 1, blocks, stride=2), :] = jnp.where(lower, 0.0, weighted)
-    high, low = split(spread_ref[...])
-    spread = jnp.concatenate([high, low], 1)
+    return jnp.concatenate(split(spread_ref[...]), 1)
+
+
+def new_state(tile, first, wide, spread, bs, write):
+    steps = len(bs)
+    heads = wide.shape[0]
     b_rows = [by_group(b, heads) for b in bs]
-    c_rows = [by_group(c, heads) for c in cs]
     at = lax.broadcasted_iota(jnp.int32, (2 * LANES, LANES), 0) // P_SIZE
     to = lax.broadcasted_iota(jnp.int32, (2 * LANES, LANES), 1) % P_SIZE
     place = to - at
-    mixed = jnp.zeros((steps * heads, LANES), jnp.float32)
-    count = P_SIZE * P_SIZE // (2 * LANES)
-    for k in range(count):
+    for k in range(P_SIZE * P_SIZE // (2 * LANES)):
         chosen = jnp.where(place == first(2 * k) * (LANES // P_SIZE), 1.0, 0.0)
         chosen = chosen.astype(jnp.bfloat16)
-        states = [tile(2 * k), tile(2 * k + 1)]
-        highs, lows = [], []
-        for t in range(steps):
-            parts = [split(s * c_rows[t]) for s in states]
-            highs.append(jnp.concatenate([p[0] for p in parts], 1))
-            lows.append(jnp.concatenate([p[1] for p in parts], 1))
-        mixed = mixed + jnp.dot(
-            jnp.concatenate(highs, 0), chosen, preferred_element_type=jnp.float32
-        )
-        mixed = mixed + jnp.dot(
-            jnp.concatenate(lows, 0), chosen, preferred_element_type=jnp.float32
-        )
         both = jnp.concatenate([chosen, chosen], 1)
         grown = lax.dot_general(
             spread, both, (((1,), (1,)), ((), ())), preferred_element_type=jnp.float32
         )
         for half in range(2):
-            new = wide * states[half]
+            new = wide * tile(2 * k + half)
             for t in range(steps):
                 piece = grown[t * heads : (t + 1) * heads, half * LANES : (half + 1) * LANES]
                 new = new + piece * b_rows[t]
             write(2 * k + half, new)
+
+
+def against_c(tile, first, cs, perm_ref, rows_ref):
+    steps = len(cs)
+    groups = cs[0].shape[0]
+    lower = lax.broadcasted_iota(jnp.int32, (steps, LANES), 1) < LANES // 2
+    lefts = []
+    for g in range(groups):
+        rows = jnp.concatenate([c[g : g + 1] for c in cs], 0)
+        rows = jnp.concatenate([jnp.where(lower, rows, 0.0), jnp.where(lower, 0.0, rows)], 0)
+        lefts.append(jnp.concatenate([jnp.concatenate([v, v], 1) for v in split(rows)], 0))
+    count = P_SIZE * P_SIZE // LANES
+    line = 2 * steps
+    run = LANES // QUAD
+    for u in range(0, count, 2 * QUAD):
+        parts = [jnp.concatenate(split(tile(j)), 1) for j in range(u, u + 2 * QUAD)]
+        for g in range(groups):
+            right = jnp.concatenate([p[g * run : (g + 1) * run] for p in parts], 0)
+            out = lax.dot_general(
+                lefts[g], right, (((1,), (1,)), ((), ())), preferred_element_type=jnp.float32
+            )
+            out = out[:line] + out[line:]
+            for w in range(2):
+                quad = first(u + w * QUAD) // QUAD
+                at = pl.ds(pl.multiple_of(g * (count // QUAD) * line + quad * line, 8), line)
+                rows_ref[at, :] = out[:, w * LANES : (w + 1) * LANES]
+    turned = jnp.transpose(rows_ref[...])
+    lower = lax.broadcasted_iota(jnp.int32, (run, LANES), 1) < LANES // 2
+    straight = [turned[i * run : (i + 1) * run] for i in range(QUAD)]
+    rolled = [
+        jnp.concatenate([v[:, LANES // 2 :], v[:, : LANES // 2]], 1) for v in straight
+    ]
+    low_group = [jnp.where(lower, straight[i], rolled[i + 1]) for i in range(0, QUAD, 2)]
+    high_group = [jnp.where(lower, rolled[i], straight[i + 1]) for i in range(0, QUAD, 2)]
+    values = jnp.concatenate(
+        [jnp.concatenate(low_group, 1), jnp.concatenate(high_group, 1)], 0
+    )
+    high = values.astype(jnp.bfloat16)
+    rest = values - high.astype(jnp.float32)
+    middle = rest.astype(jnp.bfloat16)
+    low = (rest - middle.astype(jnp.float32)).astype(jnp.bfloat16)
+    heads = values.shape[0]
+    out = jnp.dot(
+        jnp.concatenate([high, middle, low], 0), perm_ref[...], preferred_element_type=jnp.float32
+    )
+    return out[:heads] + out[heads : 2 * heads] + out[2 * heads :]
+
+
+def gated_steps(mixed, scale, xs, bs, cs, dec, dts, skip, gate, mixed_ref):
+    steps = len(xs)
+    heads = mixed.shape[0]
+    blocks = heads // 2
+    lower = lax.broadcasted_iota(jnp.int32, (blocks, LANES), 1) < LANES // 2
     for t in range(steps):
-        part = mixed[t * heads : (t + 1) * heads]
-        if scale is not None:
-            part = part * scale
-        mixed_ref[t * heads : (t + 1) * heads, :] = part
+        part = mixed[:, t * LANES : (t + 1) * LANES]
+        mixed_ref[t * heads : (t + 1) * heads, :] = part if scale is None else part * scale
     gated, sums = [], []
     ahead = None
     weights = []
@@ -273,7 +310,8 @@
 def prep_kernel(
     me_ref, counts_hbm, plan_hbm, x_ref, z_ref, bc_ref, dt_ref, bias_ref, rate_ref, skip_ref,
     wx_ref,
-    info_ref, xd_ref, gate_ref, dec_ref, dtd_ref, wide_ref, skipd_ref, wxd_ref, cx_ref, cb_ref,
+    info_ref, xd_ref, gate_ref, dec_ref, dtd_ref, wide_ref, skipd_ref, wxd_ref, perm_ref, cx_ref,
+    cb_ref,
     counts_ref, plan_ref, sems,
 ):
     slots, steps, channels = x_ref.shape
@@ -322,6 +360,13 @@
         wide = jnp.sum(jnp.where(head == lane, total, 0.0), axis=1, keepdims=True)
         wide_ref[s] = jnp.broadcast_to(wide, (heads, LANES))
     skipd_ref[...] = out[2 * slots * run :]
+    shape = perm_ref.shape
+    line = lax.broadcasted_iota(jnp.int32, shape, 0)
+    lane = lax.broadcasted_iota(jnp.int32, shape, 1)
+    span = shape[0] // QUAD
+    p = (line % span // (2 * steps) * QUAD + line // span) * 2 + line % (2 * steps) // steps
+    hit = (lane // LANES == line % steps) & (lane % P_SIZE == p)
+    perm_ref[...] = jnp.where(hit, 1.0, 0.0).astype(jnp.bfloat16)
     for copy in copies:
         copy.wait()
     reqs = plan_ref.shape[0]
@@ -380,8 +425,8 @@
 
 def kept_kernel(
     info_ref, state_ref, cx_ref, cb_ref, x_ref, bc_ref, gate_ref, dec_ref, dt_ref, skip_ref,
-    wide_ref, wx_ref, bx_ref, wb_ref, bb_ref,
-    out_hbm, gated_ref, sums_ref, spread_ref, mixed_ref, rows_ref, new_ref, sem,
+    wx_ref, bx_ref, wb_ref, bb_ref, perm_ref, wide_ref,
+    out_hbm, gated_ref, sums_ref, spread_ref, mixed_ref, turn_ref, rows_ref, new_ref, sem,
 ):
     steps = bc_ref.shape[1]
     blocks = bx_ref.shape[0]
@@ -400,11 +445,15 @@
     def write(j, new):
         new_ref[:, j * LANES : (j + 1) * LANES] = jnp.where(full, new, 0.0)
 
-    gated, sums = slot_steps(
-        lambda j: state_ref[origin, :, j * LANES : (j + 1) * LANES],
-        lambda j: j, wide_ref[slot], None, xs, bs, cs, dec, dts,
-        skip_ref[...], gate, write, spread_ref, mixed_ref,
-    )
+    def tile(j):
+        return state_ref[origin, :, j * LANES : (j + 1) * LANES]
+
+    mixed = against_c(tile, lambda j: j, cs, perm_ref, turn_ref)
+    gated, sums = gated_steps(
+        mixed, None, xs, bs, cs, dec, dts, skip_ref[...], gate, mixed_ref
+    )
+    spread = spread_x(xs, dec, dts, spread_ref)
+    new_state(tile, lambda j: j, wide_ref[slot], spread, bs, write)
     copy = pltpu.make_async_copy(new_ref, out_hbm.at[slot], sem)
     copy.start()
     for t in range(steps):
@@ -413,32 +462,50 @@
     copy.wait()
 
 
-def moved_kernel(pieces, info_ref, *refs):
+def piece_tiles(masks, me, got_refs, heads):
+    direct = len(masks) > 1
+    share = got_refs[0].shape[-2] - AUX
+    run = min(share, heads)
+    each = share // heads
+
+    def load(m, rows):
+        part = got_refs[m][rows, :] if direct else got_refs[0][m, rows, :]
+        return part.astype(jnp.int32).astype(jnp.float32)
+
+    def tile(j):
+        if direct:
+            return load(j // each, pl.ds(j % each * heads, heads))
+        flats = range(j * heads, (j + 1) * heads, run)
+        return jnp.concatenate([load(f // share, pl.ds(f % share, run)) for f in flats], 0)
+
+    def first(j):
+        return (me ^ masks[j // each]) * each + j % each if direct else j
+
+    return load, tile, first
+
+
+def moved_kernel(masks, info_ref, *refs):
+    pieces = len(masks)
     got_refs = refs[:pieces]
     (
-        held_hbm, kept_sums_ref, x_ref, bc_ref, gate_ref, dec_ref, dt_ref, skip_ref,
-        wide_ref, wx_ref, bx_ref, wb_ref, bb_ref,
-        out_hbm, gated_ref, sums_ref, spread_ref, mixed_ref, aux_ref, new_ref, sems,
+        kept_sums_ref, x_ref, bc_ref, gate_ref, dec_ref, dt_ref, skip_ref,
+        wx_ref, bx_ref, wb_ref, bb_ref, perm_ref, wide_ref,
+        gated_ref, sums_ref, spread_ref, b_ref, wide_out_ref, rows_ref, mixed_ref, turn_ref, aux_ref,
     ) = refs[pieces:]
-    del held_hbm
     direct = pieces > 1
     steps, groups = bc_ref.shape[1:3]
     blocks = bx_ref.shape[0]
     taps = wx_ref.shape[0] // blocks - 1
     heads = wide_ref.shape[1]
     share = got_refs[0].shape[-2] - AUX
-    slot, full, me = info_ref[3], info_ref[4] > 0, info_ref[5]
+    slot, me = info_ref[3], info_ref[5]
     new_x, gate, dec, dts, new_b = slot_inputs(
         slot, steps, x_ref, bc_ref, gate_ref, dec_ref, dt_ref
     )
-
-    def load(m, rows):
-        part = got_refs[m][rows, :] if direct else got_refs[0][m, rows, :]
-        return part.astype(jnp.int32).astype(jnp.float32)
-
+    load, tile, first = piece_tiles(masks, me, got_refs, heads)
     for m in range(pieces if direct else got_refs[0].shape[0]):
         if direct:
-            at = pl.ds(pl.multiple_of((me ^ m) * AUX, AUX), AUX)
+            at = pl.ds(pl.multiple_of((me ^ masks[m]) * AUX, AUX), AUX)
             aux_ref[at, :] = load(m, pl.ds(share, AUX))
         elif m * AUX < aux_ref.shape[0]:
             aux_ref[m * AUX : (m + 1) * AUX, :] = load(m, pl.ds(share, AUX))
@@ -454,18 +521,33 @@
     seq_x = [aux_ref[k * blocks : (k + 1) * blocks, :] * scale_x for k in range(taps)] + new_x
     seq_b = [last[k * groups : (k + 1) * groups] * scale_b for k in range(taps)] + new_b
     xs, bs, cs = small_steps(seq_x, seq_b, wx_ref, bx_ref, wb_ref, bb_ref, steps)
-    run = min(share, heads)
-    each = share // heads
+    mixed = against_c(tile, first, cs, perm_ref, turn_ref)
+    gated, sums = gated_steps(
+        mixed, scale, xs, bs, cs, dec, dts, skip_ref[...], gate, mixed_ref
+    )
+    for t in range(steps):
+        gated_ref[t] = gated[t]
+        b_ref[t] = bs[t]
+    sums_ref[...] = jnp.concatenate([kept_sums_ref[...]] + sums, 0)
+    spread_ref[...] = spread_x(xs, dec, dts, rows_ref)
+    wide_out_ref[...] = wide_ref[slot] * scale
+
+
+def state_kernel(masks, info_ref, *refs):
+    pieces = len(masks)
+    got_refs = refs[:pieces]
+    (
+        held_hbm, kept_ref, moved_ref, norm_ref, spread_ref, b_ref, wide_ref,
+        out_hbm, ready_ref, rows_ref, new_ref, sems,
+    ) = refs[pieces:]
+    del held_hbm
+    direct = pieces > 1
+    steps, blocks = kept_ref.shape[:2]
+    heads = wide_ref.shape[0]
+    each = (got_refs[0].shape[-2] - AUX) // heads
+    slot, full, me = info_ref[3], info_ref[4] > 0, info_ref[5]
+    _, tile, first = piece_tiles(masks, me, got_refs, heads)
     copies = []
-
-    def tile(j):
-        if direct:
-            return load(j // each, pl.ds(j % each * heads, heads))
-        flats = range(j * heads, (j + 1) * heads, run)
-        return jnp.concatenate([load(f // share, pl.ds(f % share, run)) for f in flats], 0)
-
-    def first(j):
-        return (me ^ (j // each)) * each + j % each if direct else j
 
     def write(j, new):
         at = pl.ds(pl.multiple_of(first(j) * LANES, LANES), LANES)
@@ -478,35 +560,40 @@
             copy.start()
             copies.append(copy)
 
-    gated, sums = slot_steps(
-        tile, first, wide_ref[slot] * scale, scale, xs, bs, cs, dec, dts,
-        skip_ref[...], gate, write, spread_ref, mixed_ref,
-    )
-    for t in range(steps):
-        gated_ref[t] = gated[t]
-    sums_ref[...] = jnp.concatenate([kept_sums_ref[...]] + sums, 0)
+    bs = [b_ref[t] for t in range(steps)]
+    new_state(tile, first, wide_ref[...], spread_ref[...], bs, write)
     if not direct:
         copies.append(pltpu.make_async_copy(new_ref, out_hbm.at[slot], sems.at[0]))
         copies[0].start()
+    for which, ref in enumerate((kept_ref, moved_ref)):
+        for t in range(steps):
+            rows_ref[t * blocks : (t + 1) * blocks, :] = ref[t] * norm_ref[...]
+        for b in range(blocks):
+            ready_ref[which, :, b * LANES : (b + 1) * LANES] = rows_ref[
+                pl.ds(b, steps, stride=blocks), :
+            ]
     for copy in copies:
         copy.wait()
 
 
-def norm_kernel(info_ref, kept_ref, moved_ref, mine_ref, theirs_ref, norm_ref, out_ref, rows_ref):
-    steps, blocks = kept_ref.shape[:2]
+def norm_kernel(info_ref, ready_ref, mine_ref, theirs_ref, out_ref):
+    steps = ready_ref.shape[1]
     factor = lax.rsqrt((mine_ref[...] + theirs_ref[...]) * (1.0 / (H * P_SIZE)) + 1e-05)
-    for which, ref in enumerate((kept_ref, moved_ref)):
-        slot = info_ref[3 * which]
+    for which in range(ready_ref.shape[0]):
         full = info_ref[2 + 2 * which] > 0
-        for t in range(steps):
-            at = which * steps + t
-            rows_ref[t * blocks : (t + 1) * blocks, :] = jnp.where(
-                full, ref[t] * factor[at : at + 1] * norm_ref[...], 0.0
-            )
-        for b in range(blocks):
-            out_ref[slot, :, b * LANES : (b + 1) * LANES] = rows_ref[
-                pl.ds(b, steps, stride=blocks), :
-            ].astype(jnp.bfloat16)
+        rows = factor[which * steps : (which + 1) * steps]
+        for b in range(0, ready_ref.shape[2], LANES):
+            values = jnp.where(full, ready_ref[which, :, b : b + LANES] * rows, 0.0)
+            out_ref[info_ref[3 * which], :, b : b + LANES] = values.astype(jnp.bfloat16)
+
+
+def partner_masks(owners):
+    gray = [i ^ (i >> 1) for i in range(owners)]
+    near, far = gray[1 : owners // 2], gray[owners // 2 :]
+    order = [0]
+    for i, k in enumerate(far):
+        order += [k, *near[i : i + 1]]
+    return tuple(order)
 
 
 def on_device(
@@ -538,8 +625,9 @@
     share = heads * columns // LANES // owners
     aux_rows = taps * blocks + AUX
     f32 = jnp.float32
-    direct = owners <= 16 and owners & (owners - 1) == 0 and share % heads == 0
-    pieces = owners if direct else 1
+    direct = owners <= 16 and owners & (owners - 1) == 0 and share % (QUAD * heads) == 0
+    masks = partner_masks(owners) if direct else (0,)
+    pieces = len(masks)
     smem = pl.BlockSpec(memory_space=pltpu.SMEM)
     vmem = pl.BlockSpec(memory_space=pltpu.VMEM)
     anywhere = pl.BlockSpec(memory_space=pl.ANY)
@@ -567,7 +655,7 @@
     piece = (share + AUX, LANES) if direct else (owners, share + AUX, LANES)
     sent = [shaped(*piece, dtype=jnp.int16)] * pieces
     payload = call(
-        pack_kernel, "pack", [smem] + [anywhere] * 5, [vmem] * pieces, sent,
+        functools.partial(pack_kernel, masks), "pack", [smem] + [anywhere] * 5, [vmem] * pieces, sent,
         [
             pltpu.SMEM(counts.shape, jnp.int32),
             pltpu.SMEM(move_plan.shape, jnp.int32),
@@ -583,20 +671,22 @@
         if not direct:
             return [lax.all_to_all(values[0], "req", split_axis=0, concat_axis=0, tiled=True)]
         out = list(values)
-        for k in reversed(range(1, pieces)):
-            out[k] = lax.ppermute(values[k], "req", [(i, i ^ k) for i in range(owners)])
+        for i, k in enumerate(masks):
+            if k:
+                out[i] = lax.ppermute(values[i], "req", [(o, o ^ k) for o in range(owners)])
         return out
 
     spread = exchange(payload)
 
     _, x_late = lax.optimization_barrier((payload[0], x_in))
     rows = (places, steps * blocks, LANES)
-    info, x_dense, gate, dec, dt_dense, wide, skip, wx, new_conv_x, new_conv_bc = call(
-        prep_kernel, "prep", [smem] + [anywhere] * 2 + [vmem] * 8, [smem] + [vmem] * 9,
+    info, x_dense, gate, dec, dt_dense, wide, skip, wx, perm, new_conv_x, new_conv_bc = call(
+        prep_kernel, "prep", [smem] + [anywhere] * 2 + [vmem] * 8, [smem] + [vmem] * 10,
         [
             shaped(INFO + owners, dtype=jnp.int32), shaped(*rows), shaped(*rows), shaped(*rows),
             shaped(*rows), shaped(places, heads, LANES), shaped(blocks, LANES),
             shaped((taps + 1) * blocks, LANES),
+            shaped(QUAD * P_SIZE, 2 * steps * P_SIZE, dtype=jnp.bfloat16),
             shaped(taps, places, channels, dtype=jnp.bfloat16),
             shaped(*conv_bc_state.shape, dtype=jnp.bfloat16),
         ],
@@ -611,15 +701,15 @@
     )
 
     picked = call(
-        pick_kernel, "pick", [smem] + [vmem] * pieces, [vmem] * pieces, sent,
+        functools.partial(pick_kernel, masks), "pick", [smem] + [vmem] * pieces, [vmem] * pieces, sent,
         [pltpu.VMEM((owners, *piece), jnp.int16)] if direct else [],
     )(info, *spread)
     got = exchange(picked)
 
     _, info = lax.optimization_barrier((picked[0], info))
-    common = [x_dense, bc_in, gate, dec, dt_dense, skip, wide, wx]
-    common += [conv_b_x.reshape(blocks, LANES), conv_w_bc, conv_b_bc]
-    scratch = [pltpu.VMEM((steps * heads, LANES), f32)] * 2
+    common = [x_dense, bc_in, gate, dec, dt_dense, skip, wx]
+    common += [conv_b_x.reshape(blocks, LANES), conv_w_bc, conv_b_bc, perm, wide]
+    scratch = [pltpu.VMEM((steps * heads, LANES), f32)] * 2 + [pltpu.VMEM((LANES, LANES), f32)]
     held, kept_gated, kept_sums = call(
         kept_kernel, "kept", [smem] + [vmem] * (3 + len(common)), [anywhere, vmem, vmem],
         [shaped(places, heads, columns), shaped(steps, blocks, LANES), shaped(steps, LANES)],
@@ -630,26 +720,35 @@
             pltpu.SemaphoreType.DMA,
         ],
     )(info, ssm_state, conv_x_taps, conv_bc_state, *common)
-    new_ssm, moved_gated, sums = call(
-        functools.partial(moved_kernel, pieces), "moved",
-        [smem] + [vmem] * pieces + [anywhere] + [vmem] * (1 + len(common)),
-        [anywhere, vmem, vmem],
-        [shaped(places, heads, columns), shaped(steps, blocks, LANES), shaped(2 * steps, LANES)],
-        scratch
-        + [
-            pltpu.VMEM((max(aux_rows, pieces * AUX), LANES), f32),
+    moved_gated, sums, spread_rows, b_steps, wide_scaled = call(
+        functools.partial(moved_kernel, masks), "moved",
+        [smem] + [vmem] * (pieces + 1 + len(common)), [vmem] * 5,
+        [
+            shaped(steps, blocks, LANES), shaped(2 * steps, LANES),
+            shaped(steps * heads, 2 * LANES, dtype=jnp.bfloat16),
+            shaped(steps, groups, pair), shaped(heads, LANES),
+        ],
+        scratch + [pltpu.VMEM((max(aux_rows, pieces * AUX), LANES), f32)],
+    )(info, *got, kept_sums, *common)
+    theirs = lax.ppermute(sums, "tp", [(0, 1), (1, 0)])
+    new_ssm, ready = call(
+        functools.partial(state_kernel, masks), "state",
+        [smem] + [vmem] * pieces + [anywhere] + [vmem] * 6, [anywhere, vmem],
+        [shaped(places, heads, columns), shaped(places, steps, channels)],
+        [
+            pltpu.VMEM((steps * blocks, LANES), f32),
             pltpu.VMEM((heads, columns), f32),
             pltpu.SemaphoreType.DMA((pieces,)),
         ],
         input_output_aliases={1 + pieces: 0},
-    )(info, *got, held, kept_sums, *common)
-
-    theirs = lax.ppermute(sums, "tp", [(0, 1), (1, 0)])
+    )(
+        info, *got, held, kept_gated, moved_gated, norm_w.reshape(blocks, LANES), spread_rows,
+        b_steps, wide_scaled,
+    )
     y_out = call(
-        norm_kernel, "norm", [smem] + [vmem] * 5, vmem,
+        norm_kernel, "norm", [smem] + [vmem] * 3, vmem,
         shaped(places, steps, channels, dtype=jnp.bfloat16),
-        [pltpu.VMEM((steps * blocks, LANES), f32)],
-    )(info, kept_gated, moved_gated, sums, theirs, norm_w.reshape(blocks, LANES))
+    )(info, ready, sums, theirs)
     return (y_out, new_ssm, jnp.transpose(new_conv_x, (1, 0, 2)), new_conv_bc)
 
 

time: 46.4 us -> 41.4 us (0.89)
  waiting for transfers between devices: 5.39 us -> 1.71 us
  starting transfers between devices: 24.2 us -> 23.7 us
    ppermute x14, waiting for transfers between devices: 4.24 us -> 1.71 us  [exchange(): out[i] = lax.ppermute(values[i], 'req', [(o, o ^ k) for o in range(owners)])]
    ppermute x1, waiting for transfers between devices: 1.15 us -> 0.01 us  [on_device(): theirs = lax.ppermute(sums, 'tp', [(0, 1), (1, 0)])]
    pallas_call x1, Pallas kernels: 3.63 us -> 2.89 us  [on_device(): call(kept_kernel, 'kept', [smem] + [vmem] * (3 + len(common)), [anywhere,...]
    ppermute x14, starting transfers between devices: 24.2 us -> 23.7 us  [exchange(): out[i] = lax.ppermute(values[i], 'req', [(o, o ^ k) for o in range(owners)])]
    pallas_call x4 -> x5, Pallas kernels: 7.23 us -> 7.39 us  [the longest x1 2.08 us: on_device(): call(functools.partial(state_kernel, masks), 'state', [smem] + [vmem] * p...]
  transfers between devices with their start and end apart: 15 -> 15, of which waited for: 4 -> 3; matrix products, arithmetic and copies ran while one was open for 0% -> 0% of each run, Pallas kernels for 12% -> 17%
where the time goes in v3:
time: 41.4 us; the launch traced here: 41.1 us
  starting transfers between devices  23.7 us (57%)
  Pallas kernels  12.2 us (29%)
  local copies, waits for them, and re-layouts  2.57 us (6%)
  waiting for transfers between devices  1.71 us (4%)
  between operations  0.9 us (2%)
    ppermute x14, starting transfers between devices, exchange(): out[i] = lax.ppermute(values[i], 'req', [(o, o ^ k) for o in range(owners)])  23.7 us
    pallas_call x1, Pallas kernels, on_device(): call(kept_kernel, 'kept', [smem] + [vmem] * (3 + len(common)), [anywhere,...  2.89 us
    unnamed x30, local copies, waits for them, and re-layouts  2.57 us
    pallas_call x1, Pallas kernels, on_device(): call(functools.partial(state_kernel, masks), 'state', [smem] + [vmem] * p...  2.08 us
    pallas_call x1, Pallas kernels, on_device(): call(prep_kernel, 'prep', [smem] + [anywhere] * 2 + [vmem] * 8, [smem] +...  1.93 us
    pallas_call x1, Pallas kernels, on_device(): call(functools.partial(pack_kernel, masks), 'pack', [smem] + [anywhere] *...  1.93 us
    ppermute x14, waiting for transfers between devices, exchange(): out[i] = lax.ppermute(values[i], 'req', [(o, o ^ k) for o in range(owners)])  1.71 us
    pallas_call x1, Pallas kernels, on_device(): call(functools.partial(moved_kernel, masks), 'moved', [smem] + [vmem] * (...  1.56 us
  transfers between devices with their start and end apart: 15, of which 3 were waited for; matrix products, arithmetic and copies ran while one was open for 0% of the time, Pallas kernels for 17%

profile of v3, /device:TPU:0, one launch (start us, length us, event | category | flops | bytes accessed | tf_op | source)
XLA Modules:
  0.0 41.1 jit_solution(3547094590559732766)
XLA Ops:
  0.7 1.9 %pack.1 = (s16[272,128]{1,0:T(8,128)(2,1)S(1)}, s16[272,128]{1,0:T(8,128)(2,1)S(1)}, s16[272,128]{1,0:T(8,128)(2,1)S(1)}, s16[272,128]{1,0:T(8,128)(2,1)S(1)}, s...) custom-call(s32[1]{0:T(128)} %bitcast.me_ref, ...), custom_call_target="tpu_custom_call" | custom-call | tf_op jit(solution)/shard_map/pack/pallas_call | solution.py:657
  2.7 5.1 %collective-permute-start = (s16[272,128]{1,0:T(8,128)(2,1)S(1)}, s16[272,128]{1,0:T(8,128)(2,1)S(1)}, u32[]{:S(2)}, u32[]{:S(2)}) collective-permute-start(s16[272,128]{1,0:T(8,128)(2,1)S(1)} %get-tuple-element.46), channel_id=1, source_target_pairs={{0,12},{2,14},{4,8},{6,10},{8,4},{10,6},{12,0},{14,2},{1,13},{3,15... | collective-permute-start | bytes 208904 | tf_op jit(solution)/shard_map/ppermute | solution.py:676
  7.8 1.5 %collective-permute-start.1 = (s16[272,128]{1,0:T(8,128)(2,1)S(1)}, s16[272,128]{1,0:T(8,128)(2,1)S(1)}, u32[]{:S(2)}, u32[]{:S(2)}) collective-permute-start(s16[272,128]{1,0:T(8,128)(2,1)S(1)} %get-tuple-element.47), channel_id=1, source_target_pairs={{0,2},{2,0},{4,6},{6,4},{8,10},{10,8},{12,14},{14,12},{1,3},{3,1},... | collective-permute-start | bytes 208904 | tf_op jit(solution)/shard_map/ppermute | solution.py:676
  9.3 0.8 %collective-permute-start.3 = (s16[272,128]{1,0:T(8,128)(2,1)S(1)}, s16[272,128]{1,0:T(8,128)(2,1)S(1)}, u32[]{:S(2)}, u32[]{:S(2)}) collective-permute-start(s16[272,128]{1,0:T(8,128)(2,1)S(1)} %get-tuple-element.49), channel_id=1, source_target_pairs={{0,6},{2,4},{4,2},{6,0},{8,14},{10,12},{12,10},{14,8},{1,7},{3,5},... | collective-permute-start | bytes 208904 | tf_op jit(solution)/shard_map/ppermute | solution.py:676
  10.2 4.4 %collective-permute-start.4 = (s16[272,128]{1,0:T(8,128)(2,1)S(1)}, s16[272,128]{1,0:T(8,128)(2,1)S(1)}, u32[]{:S(2)}, u32[]{:S(2)}) collective-permute-start(s16[272,128]{1,0:T(8,128)(2,1)S(1)} %get-tuple-element.50), channel_id=1, source_target_pairs={{0,10},{2,8},{4,14},{6,12},{8,2},{10,0},{12,6},{14,4},{1,11},{3,9}... | collective-permute-start | bytes 208904 | tf_op jit(solution)/shard_map/ppermute | solution.py:676
  14.6 0.6 %collective-permute-start.6 = (s16[272,128]{1,0:T(8,128)(2,1)S(1)}, s16[272,128]{1,0:T(8,128)(2,1)S(1)}, u32[]{:S(2)}, u32[]{:S(2)}) collective-permute-start(s16[272,128]{1,0:T(8,128)(2,1)S(1)} %get-tuple-element.52), channel_id=1, source_target_pairs={{0,8},{2,10},{4,12},{6,14},{8,0},{10,2},{12,4},{14,6},{1,9},{3,11}... | collective-permute-start | bytes 208904 | tf_op jit(solution)/shard_map/ppermute | solution.py:676
  15.2 0.8 %copy-done.3 = bf16[2,4,4096]{2,1,0:T(4,128)(2,1)S(1)} copy-done((bf16[2,4,4096]{2,1,0:T(4,128)(2,1)S(1)}, bf16[2,4,4096]{2,1,0:T(4,128)(2,1)}, u32[]{:S(2)}) %copy-start.3) | copy-done | bytes 65560
  16.1 0.8 %copy-done.4 = bf16[2,4,4096]{2,1,0:T(4,128)(2,1)S(1)} copy-done((bf16[2,4,4096]{2,1,0:T(4,128)(2,1)S(1)}, bf16[2,4,4096]{2,1,0:T(4,128)(2,1)}, u32[]{:S(2)}) %copy-start.4) | copy-done | bytes 65560
  16.9 0.8 %copy-done.5 = f32[4,4096]{1,0:T(4,128)S(1)} copy-done((f32[4,4096]{1,0:T(4,128)S(1)}, f32[4,4096]{1,0:T(4,128)}, u32[]{:S(2)}) %copy-start.5) | copy-done | bytes 65560
  17.7 1.9 %prep.1 = (s32[16]{0:T(128)S(1)}, f32[2,128,128]{2,1,0:T(8,128)S(1)}, f32[2,128,128]{2,1,0:T(8,128)S(1)}, f32[2,128,128]{2,1,0:T(8,128)S(1)}, f32[2,128,128]{2,1...) custom-call(s32[1]{0:T(128)} %bitcast.me_ref, ...), custom_call_target="tpu_custom_call" | custom-call | tf_op jit(solution)/shard_map/prep/pallas_call | solution.py:683
  19.7 0.4 collective-permute-done.6.refs_7_
  20.1 0.6 %pick.1 = (s16[272,128]{1,0:T(8,128)(2,1)S(1)}, s16[272,128]{1,0:T(8,128)(2,1)S(1)}, s16[272,128]{1,0:T(8,128)(2,1)S(1)}, s16[272,128]{1,0:T(8,128)(2,1)S(1)}, s...) custom-call(s32[16]{0:T(128)S(1)} %get-tuple-element.54.info_ref, ...), custom_call_target="tpu_custom_call" | custom-call | tf_op jit(solution)/shard_map/pick/pallas_call | solution.py:703
  20.7 3.4 %collective-permute-start.7 = (s16[272,128]{1,0:T(8,128)(2,1)S(1)}, s16[272,128]{1,0:T(8,128)(2,1)S(1)}, u32[]{:S(2)}, u32[]{:S(2)}) collective-permute-start(s16[272,128]{1,0:T(8,128)(2,1)S(1)} %get-tuple-element.55), channel_id=1, source_target_pairs={{0,12},{2,14},{4,8},{6,10},{8,4},{10,6},{12,0},{14,2},{1,13},{3,15... | collective-permute-start | bytes 208904 | tf_op jit(solution)/shard_map/ppermute | solution.py:676
  24.2 1.5 %collective-permute-start.8 = (s16[272,128]{1,0:T(8,128)(2,1)S(1)}, s16[272,128]{1,0:T(8,128)(2,1)S(1)}, u32[]{:S(2)}, u32[]{:S(2)}) collective-permute-start(s16[272,128]{1,0:T(8,128)(2,1)S(1)} %get-tuple-element.56), channel_id=1, source_target_pairs={{0,2},{2,0},{4,6},{6,4},{8,10},{10,8},{12,14},{14,12},{1,3},{3,1},... | collective-permute-start | bytes 208904 | tf_op jit(solution)/shard_map/ppermute | solution.py:676
  25.7 0.4 %collective-permute-start.9 = (s16[272,128]{1,0:T(8,128)(2,1)S(1)}, s16[272,128]{1,0:T(8,128)(2,1)S(1)}, u32[]{:S(2)}, u32[]{:S(2)}) collective-permute-start(s16[272,128]{1,0:T(8,128)(2,1)S(1)} %get-tuple-element.57), channel_id=1, source_target_pairs={{0,14},{2,12},{4,10},{6,8},{8,6},{10,4},{12,2},{14,0},{1,15},{3,13... | collective-permute-start | bytes 208904 | tf_op jit(solution)/shard_map/ppermute | solution.py:676
  26.1 0.8 %collective-permute-start.10 = (s16[272,128]{1,0:T(8,128)(2,1)S(1)}, s16[272,128]{1,0:T(8,128)(2,1)S(1)}, u32[]{:S(2)}, u32[]{:S(2)}) collective-permute-start(s16[272,128]{1,0:T(8,128)(2,1)S(1)} %get-tuple-element.58), channel_id=1, source_target_pairs={{0,6},{2,4},{4,2},{6,0},{8,14},{10,12},{12,10},{14,8},{1,7},{3,5},... | collective-permute-start | bytes 208904 | tf_op jit(solution)/shard_map/ppermute | solution.py:676
  26.9 4.0 %collective-permute-start.11 = (s16[272,128]{1,0:T(8,128)(2,1)S(1)}, s16[272,128]{1,0:T(8,128)(2,1)S(1)}, u32[]{:S(2)}, u32[]{:S(2)}) collective-permute-start(s16[272,128]{1,0:T(8,128)(2,1)S(1)} %get-tuple-element.59), channel_id=1, source_target_pairs={{0,10},{2,8},{4,14},{6,12},{8,2},{10,0},{12,6},{14,4},{1,11},{3,9}... | collective-permute-start | bytes 208904 | tf_op jit(solution)/shard_map/ppermute | solution.py:676
  31.0 1.0 %collective-permute-start.13 = (s16[272,128]{1,0:T(8,128)(2,1)S(1)}, s16[272,128]{1,0:T(8,128)(2,1)S(1)}, u32[]{:S(2)}, u32[]{:S(2)}) collective-permute-start(s16[272,128]{1,0:T(8,128)(2,1)S(1)} %get-tuple-element.61), channel_id=1, source_target_pairs={{0,8},{2,10},{4,12},{6,14},{8,0},{10,2},{12,4},{14,6},{1,9},{3,11}... | collective-permute-start | bytes 208904 | tf_op jit(solution)/shard_map/ppermute | solution.py:676
  32.0 2.9 %kept.1 = (f32[2,64,4096]{2,1,0:T(8,128)}, f32[4,32,128]{2,1,0:T(8,128)S(1)}, f32[4,128]{1,0:T(4,128)S(1)}) custom-call(s32[16]{0:T(128)S(1)} %get-tuple-element.54.info_ref, f32[2,64,4096]{2,1,0:T(8,128)S(1)} %copy-done, bf16[3,2,4096]{2,1,0:T(2,128)(2,1)S(1)} %bitcast.9, bf16[2,3,2,128]{3,2,1,0:T(2,128)(2,1)S(1)} %copy-done.9, ...), custom_call_target="tpu_custom_call" | custom-call | tf_op jit(solution)/shard_map/kept/pallas_call | solution.py:713
  34.9 0.8 %collective-permute-done.11.refs_5_ = s16[272,128]{1,0:T(8,128)(2,1)S(1)} collective-permute-done((s16[272,128]{1,0:T(8,128)(2,1)S(1)}, s16[272,128]{1,0:T(8,128)(2,1)S(1)}, u32[]{:S(2)}, u32[]{:S(2)}) %collective-permute-start.11) | collective-permute-done | bytes 69664 | tf_op jit(solution)/shard_map/ppermute | solution.py:676
  35.7 0.5 %collective-permute-done.13.refs_7_ = s16[272,128]{1,0:T(8,128)(2,1)S(1)} collective-permute-done((s16[272,128]{1,0:T(8,128)(2,1)S(1)}, s16[272,128]{1,0:T(8,128)(2,1)S(1)}, u32[]{:S(2)}, u32[]{:S(2)}) %collective-permute-start.13) | collective-permute-done | bytes 69664 | tf_op jit(solution)/shard_map/ppermute | solution.py:676
  36.2 1.6 %moved.1 = (f32[4,32,128]{2,1,0:T(8,128)S(1)}, f32[8,128]{1,0:T(8,128)S(1)}, bf16[256,256]{1,0:T(8,128)(2,1)S(1)}, f32[4,2,128]{2,1,0:T(2,128)S(1)}, f32[64,128]{1,0:T(8,128)S(1)}) custom-call(s32[16]{0:T(128)S(1)} %get-tuple-element.54.info_ref, s16[272,128]{1,0:T(8,128)(2,1)S(1)} %get-tuple-element.53.refs_0_, ...), custom_call_target="tpu_custom_call" | custom-call | tf_op jit(solution)/shard_map/moved/pallas_call | solution.py:723
  37.8 2.1 %state.1 = (f32[2,64,4096]{2,1,0:T(8,128)}, f32[2,4,4096]{2,1,0:T(4,128)S(1)}) custom-call(s32[16]{0:T(128)S(1)} %get-tuple-element.54.info_ref, s16[272,128]{1,0:T(8,128)(2,1)S(1)} %get-tuple-element.53.refs_0_, s16[272,128]{1,0:T(8,128)(2,1)S(1)} %collective-permute-done.7.refs_1_, ...), custom_call_target="tpu_custom_call", output_to_operand_aliasing={{0}: (9, {})} | custom-call | tf_op jit(solution)/shard_map/state/pallas_call | solution.py:734
  39.9 1.2 %norm.1 = bf16[2,4,4096]{2,1,0:T(4,128)(2,1)} custom-call(s32[16]{0:T(128)S(1)} %get-tuple-element.54.info_ref, f32[2,4,4096]{2,1,0:T(4,128)S(1)} %get-tuple-element.77.ready_ref, f32[8,128]{1,0:T(8,128)S(1)} %get-tuple-element.78.mine_ref, f32[8,128]{1,0:T(8,128)S(1)} %collective-permute-done.14.theirs_ref), custom_call_target="tpu_custom_call" | custom-call | tf_op jit(solution)/shard_map/norm/pallas_call | solution.py:748
  (43 shorter events, 0.2 us)
Async XLA Ops:
  0.6 31.3 %copy-start.9 = (bf16[2,3,2,128]{3,2,1,0:T(2,128)(2,1)S(1)}, bf16[2,3,2,128]{3,2,1,0:T(2,128)(2,1)}, u32[]{:S(2)}) copy-start(bf16[2,3,2,128]{3,2,1,0:T(2,128)(2,1)} %cb_ref.1) | copy-start | bytes 9220
  0.6 31.3 %copy-start = (f32[2,64,4096]{2,1,0:T(8,128)S(1)}, f32[2,64,4096]{2,1,0:T(8,128)}, u32[]{:S(2)}) copy-start(f32[2,64,4096]{2,1,0:T(8,128)} %state_ref.1) | copy-start | bytes 6291460
  0.7 31.3 %copy-start.1 = (bf16[2,3,4096]{2,0,1:T(2,128)(2,1)S(1)}, bf16[2,3,4096]{2,0,1:T(2,128)(2,1)}, u32[]{:S(2)}) copy-start(bf16[2,3,4096]{2,0,1:T(2,128)(2,1)} %param.20) | copy-start | bytes 147460
  0.7 14.5 %copy-start.6 = (bf16[2,4,2,128]{3,2,1,0:T(2,128)(2,1)S(1)}, bf16[2,4,2,128]{3,2,1,0:T(2,128)(2,1)}, u32[]{:S(2)}) copy-start(bf16[2,4,2,128]{3,2,1,0:T(2,128)(2,1)} %refs_10_.1) | copy-start | bytes 12292
  0.7 14.5 %copy-start.14 = (f32[64]{0:T(128)S(1)}, f32[64]{0:T(128)}, u32[]{:S(2)}) copy-start(f32[64]{0:T(128)} %param.32) | copy-start | bytes 772
  0.7 14.5 %copy-start.13 = (f32[64]{0:T(128)S(1)}, f32[64]{0:T(128)}, u32[]{:S(2)}) copy-start(f32[64]{0:T(128)} %param.31) | copy-start | bytes 772
  0.7 31.2 %copy-start.10 = (f32[2,128]{1,0:T(2,128)S(1)}, f32[2,128]{1,0:T(2,128)}, u32[]{:S(2)}) copy-start(f32[2,128]{1,0:T(2,128)} %refs_18_.1) | copy-start | bytes 3076
  0.7 31.2 %copy-start.8 = (f32[4,2,128]{2,1,0:T(2,128)S(1)}, f32[4,2,128]{2,1,0:T(2,128)}, u32[]{:S(2)}) copy-start(f32[4,2,128]{2,1,0:T(2,128)} %refs_17_.1) | copy-start | bytes 12292
  0.7 31.2 %copy-start.2 = (f32[4096]{0:T(1024)S(1)}, f32[4096]{0:T(1024)}, u32[]{:S(2)}) copy-start(f32[4096]{0:T(1024)} %param.27) | copy-start | bytes 49156
  2.7 11.9 %collective-permute-start = (s16[272,128]{1,0:T(8,128)(2,1)S(1)}, s16[272,128]{1,0:T(8,128)(2,1)S(1)}, u32[]{:S(2)}, u32[]{:S(2)}) collective-permute-start(s16[272,128]{1,0:T(8,128)(2,1)S(1)} %get-tuple-element.46), channel_id=1, source_target_pairs={{0,12},{2,14},{4,8},{6,10},{8,4},{10,6},{12,0},{14,2},{1,13},{3,15... | collective-permute-start | bytes 208904 | tf_op jit(solution)/shard_map/ppermute | solution.py:676
  7.8 6.8 %collective-permute-start.1 = (s16[272,128]{1,0:T(8,128)(2,1)S(1)}, s16[272,128]{1,0:T(8,128)(2,1)S(1)}, u32[]{:S(2)}, u32[]{:S(2)}) collective-permute-start(s16[272,128]{1,0:T(8,128)(2,1)S(1)} %get-tuple-element.47), channel_id=1, source_target_pairs={{0,2},{2,0},{4,6},{6,4},{8,10},{10,8},{12,14},{14,12},{1,3},{3,1},... | collective-permute-start | bytes 208904 | tf_op jit(solution)/shard_map/ppermute | solution.py:676
  9.3 10.4 %collective-permute-start.2 = (s16[272,128]{1,0:T(8,128)(2,1)S(1)}, s16[272,128]{1,0:T(8,128)(2,1)S(1)}, u32[]{:S(2)}, u32[]{:S(2)}) collective-permute-start(s16[272,128]{1,0:T(8,128)(2,1)S(1)} %get-tuple-element.48), channel_id=1, source_target_pairs={{0,14},{2,12},{4,10},{6,8},{8,6},{10,4},{12,2},{14,0},{1,15},{3,13... | collective-permute-start | bytes 208904 | tf_op jit(solution)/shard_map/ppermute | solution.py:676
  9.3 10.4 %collective-permute-start.3 = (s16[272,128]{1,0:T(8,128)(2,1)S(1)}, s16[272,128]{1,0:T(8,128)(2,1)S(1)}, u32[]{:S(2)}, u32[]{:S(2)}) collective-permute-start(s16[272,128]{1,0:T(8,128)(2,1)S(1)} %get-tuple-element.49), channel_id=1, source_target_pairs={{0,6},{2,4},{4,2},{6,0},{8,14},{10,12},{12,10},{14,8},{1,7},{3,5},... | collective-permute-start | bytes 208904 | tf_op jit(solution)/shard_map/ppermute | solution.py:676
  10.2 9.5 %collective-permute-start.4 = (s16[272,128]{1,0:T(8,128)(2,1)S(1)}, s16[272,128]{1,0:T(8,128)(2,1)S(1)}, u32[]{:S(2)}, u32[]{:S(2)}) collective-permute-start(s16[272,128]{1,0:T(8,128)(2,1)S(1)} %get-tuple-element.50), channel_id=1, source_target_pairs={{0,10},{2,8},{4,14},{6,12},{8,2},{10,0},{12,6},{14,4},{1,11},{3,9}... | collective-permute-start | bytes 208904 | tf_op jit(solution)/shard_map/ppermute | solution.py:676
  14.6 5.2 %collective-permute-start.5 = (s16[272,128]{1,0:T(8,128)(2,1)S(1)}, s16[272,128]{1,0:T(8,128)(2,1)S(1)}, u32[]{:S(2)}, u32[]{:S(2)}) collective-permute-start(s16[272,128]{1,0:T(8,128)(2,1)S(1)} %get-tuple-element.51), channel_id=1, source_target_pairs={{0,4},{2,6},{4,0},{6,2},{8,12},{10,14},{12,8},{14,10},{1,5},{3,7},... | collective-permute-start | bytes 208904 | tf_op jit(solution)/shard_map/ppermute | solution.py:676
  14.6 5.5 %collective-permute-start.6 = (s16[272,128]{1,0:T(8,128)(2,1)S(1)}, s16[272,128]{1,0:T(8,128)(2,1)S(1)}, u32[]{:S(2)}, u32[]{:S(2)}) collective-permute-start(s16[272,128]{1,0:T(8,128)(2,1)S(1)} %get-tuple-element.52), channel_id=1, source_target_pairs={{0,8},{2,10},{4,12},{6,14},{8,0},{10,2},{12,4},{14,6},{1,9},{3,11}... | collective-permute-start | bytes 208904 | tf_op jit(solution)/shard_map/ppermute | solution.py:676
  20.7 10.2 %collective-permute-start.7 = (s16[272,128]{1,0:T(8,128)(2,1)S(1)}, s16[272,128]{1,0:T(8,128)(2,1)S(1)}, u32[]{:S(2)}, u32[]{:S(2)}) collective-permute-start(s16[272,128]{1,0:T(8,128)(2,1)S(1)} %get-tuple-element.55), channel_id=1, source_target_pairs={{0,12},{2,14},{4,8},{6,10},{8,4},{10,6},{12,0},{14,2},{1,13},{3,15... | collective-permute-start | bytes 208904 | tf_op jit(solution)/shard_map/ppermute | solution.py:676
  24.2 6.8 %collective-permute-start.8 = (s16[272,128]{1,0:T(8,128)(2,1)S(1)}, s16[272,128]{1,0:T(8,128)(2,1)S(1)}, u32[]{:S(2)}, u32[]{:S(2)}) collective-permute-start(s16[272,128]{1,0:T(8,128)(2,1)S(1)} %get-tuple-element.56), channel_id=1, source_target_pairs={{0,2},{2,0},{4,6},{6,4},{8,10},{10,8},{12,14},{14,12},{1,3},{3,1},... | collective-permute-start | bytes 208904 | tf_op jit(solution)/shard_map/ppermute | solution.py:676
  25.7 9.2 %collective-permute-start.9 = (s16[272,128]{1,0:T(8,128)(2,1)S(1)}, s16[272,128]{1,0:T(8,128)(2,1)S(1)}, u32[]{:S(2)}, u32[]{:S(2)}) collective-permute-start(s16[272,128]{1,0:T(8,128)(2,1)S(1)} %get-tuple-element.57), channel_id=1, source_target_pairs={{0,14},{2,12},{4,10},{6,8},{8,6},{10,4},{12,2},{14,0},{1,15},{3,13... | collective-permute-start | bytes 208904 | tf_op jit(solution)/shard_map/ppermute | solution.py:676
  26.1 8.8 %collective-permute-start.10 = (s16[272,128]{1,0:T(8,128)(2,1)S(1)}, s16[272,128]{1,0:T(8,128)(2,1)S(1)}, u32[]{:S(2)}, u32[]{:S(2)}) collective-permute-start(s16[272,128]{1,0:T(8,128)(2,1)S(1)} %get-tuple-element.58), channel_id=1, source_target_pairs={{0,6},{2,4},{4,2},{6,0},{8,14},{10,12},{12,10},{14,8},{1,7},{3,5},... | collective-permute-start | bytes 208904 | tf_op jit(solution)/shard_map/ppermute | solution.py:676
  26.9 8.8 %collective-permute-start.11 = (s16[272,128]{1,0:T(8,128)(2,1)S(1)}, s16[272,128]{1,0:T(8,128)(2,1)S(1)}, u32[]{:S(2)}, u32[]{:S(2)}) collective-permute-start(s16[272,128]{1,0:T(8,128)(2,1)S(1)} %get-tuple-element.59), channel_id=1, source_target_pairs={{0,10},{2,8},{4,14},{6,12},{8,2},{10,0},{12,6},{14,4},{1,11},{3,9}... | collective-permute-start | bytes 208904 | tf_op jit(solution)/shard_map/ppermute | solution.py:676
  30.9 4.8 %collective-permute-start.12 = (s16[272,128]{1,0:T(8,128)(2,1)S(1)}, s16[272,128]{1,0:T(8,128)(2,1)S(1)}, u32[]{:S(2)}, u32[]{:S(2)}) collective-permute-start(s16[272,128]{1,0:T(8,128)(2,1)S(1)} %get-tuple-element.60), channel_id=1, source_target_pairs={{0,4},{2,6},{4,0},{6,2},{8,12},{10,14},{12,8},{14,10},{1,5},{3,7},... | collective-permute-start | bytes 208904 | tf_op jit(solution)/shard_map/ppermute | solution.py:676
  31.0 5.2 %collective-permute-start.13 = (s16[272,128]{1,0:T(8,128)(2,1)S(1)}, s16[272,128]{1,0:T(8,128)(2,1)S(1)}, u32[]{:S(2)}, u32[]{:S(2)}) collective-permute-start(s16[272,128]{1,0:T(8,128)(2,1)S(1)} %get-tuple-element.61), channel_id=1, source_target_pairs={{0,8},{2,10},{4,12},{6,14},{8,0},{10,2},{12,4},{14,6},{1,9},{3,11}... | collective-permute-start | bytes 208904 | tf_op jit(solution)/shard_map/ppermute | solution.py:676
  37.8 2.1 %collective-permute-start.14 = (f32[8,128]{1,0:T(8,128)S(1)}, f32[8,128]{1,0:T(8,128)S(1)}, u32[]{:S(2)}, u32[]{:S(2)}) collective-permute-start(f32[8,128]{1,0:T(8,128)S(1)} %get-tuple-element.78.mine_ref), channel_id=1, source_target_pairs={{0,1},{1,0},{2,3},{3,2},{4,5},{5,4},{6,7},{7,6},{8,9},{9,8},{10,11... | collective-permute-start | bytes 12296 | tf_op jit(solution)/shard_map/ppermute | solution.py:733
  (6 other events, 37.4 us)

commit v4 on v3

--- a/solution.py
+++ b/solution.py
@@ -13,6 +13,7 @@
 AUX = 16
 BLOCK = 16
 QUAD = 4
+COPIES = 8
 INFO = 8
 REACH = 6.0
 LEVELS = 32767.0
@@ -46,6 +47,16 @@
             rows_ref[at + b : at + b + 1, :] = part
         else:
             rows_ref[pl.ds(at + b, count, stride=blocks), :] = part
+
+
+def copy_rows(src, dst, sems, at, count):
+    run = dst.shape[0] // count
+    copies = []
+    for i in range(count):
+        rows = pl.ds(i * run, run)
+        copies.append(pltpu.make_async_copy(src.at[rows], dst.at[rows], sems.at[at + i]))
+        copies[-1].start()
+    return copies
 
 
 def of_slot(values, slot):
@@ -211,26 +222,23 @@
     return jnp.concatenate(split(spread_ref[...]), 1)
 
 
-def new_state(tile, first, wide, spread, bs, write):
+def new_state(tile, first, wide, spread, bs, place_ref, write):
     steps = len(bs)
     heads = wide.shape[0]
     b_rows = [by_group(b, heads) for b in bs]
-    at = lax.broadcasted_iota(jnp.int32, (2 * LANES, LANES), 0) // P_SIZE
-    to = lax.broadcasted_iota(jnp.int32, (2 * LANES, LANES), 1) % P_SIZE
-    place = to - at
-    for k in range(P_SIZE * P_SIZE // (2 * LANES)):
-        chosen = jnp.where(place == first(2 * k) * (LANES // P_SIZE), 1.0, 0.0)
-        chosen = chosen.astype(jnp.bfloat16)
-        both = jnp.concatenate([chosen, chosen], 1)
-        grown = lax.dot_general(
-            spread, both, (((1,), (1,)), ((), ())), preferred_element_type=jnp.float32
+    for j in range(0, P_SIZE * P_SIZE // LANES, 2):
+        at = pl.ds(pl.multiple_of(first(j) * LANES, LANES), 2 * LANES)
+        grown = jnp.dot(
+            spread,
+            jnp.concatenate([place_ref[:, at]] * (spread.shape[1] // P_SIZE), 0),
+            preferred_element_type=jnp.float32,
         )
         for half in range(2):
-            new = wide * tile(2 * k + half)
+            new = wide * tile(j + half)
             for t in range(steps):
                 piece = grown[t * heads : (t + 1) * heads, half * LANES : (half + 1) * LANES]
                 new = new + piece * b_rows[t]
-            write(2 * k + half, new)
+            write(j + half, new)
 
 
 def against_c(tile, first, cs, perm_ref, rows_ref):
@@ -308,11 +316,11 @@
 
 
 def prep_kernel(
-    me_ref, counts_hbm, plan_hbm, x_ref, z_ref, bc_ref, dt_ref, bias_ref, rate_ref, skip_ref,
-    wx_ref,
-    info_ref, xd_ref, gate_ref, dec_ref, dtd_ref, wide_ref, skipd_ref, wxd_ref, perm_ref, cx_ref,
-    cb_ref,
-    counts_ref, plan_ref, sems,
+    me_ref, counts_hbm, plan_hbm, x_hbm, z_hbm, wx_hbm, state_hbm, bc_ref, dt_ref, bias_ref,
+    rate_ref, skip_ref,
+    info_ref, xd_ref, gate_ref, dec_ref, dtd_ref, wide_ref, skipd_ref, wxd_ref, perm_ref,
+    place_ref, kept_ref, cx_ref, cb_ref,
+    counts_ref, plan_ref, x_ref, z_ref, wx_ref, sems,
 ):
     slots, steps, channels = x_ref.shape
     heads = dt_ref.shape[2]
@@ -320,17 +328,66 @@
     taps = cx_ref.shape[0]
     me = me_ref[0]
     copies = [
-        pltpu.make_async_copy(counts_hbm, counts_ref, sems.at[0]),
-        pltpu.make_async_copy(plan_hbm, plan_ref, sems.at[1]),
+        pltpu.make_async_copy(src, dst, sems.at[i])
+        for i, (src, dst) in enumerate(
+            (
+                (counts_hbm, counts_ref), (plan_hbm, plan_ref), (x_hbm, x_ref), (z_hbm, z_ref),
+                (wx_hbm, wx_ref),
+            )
+        )
     ]
     for copy in copies:
         copy.start()
-    x = [x_ref[s].astype(jnp.float32) for s in range(slots)]
-    for s in range(slots):
-        dense_rows(xd_ref.at[s], 0, x[s])
-        dense_rows(gate_ref.at[s], 0, z_ref[s].astype(jnp.float32))
-    dense_rows(wxd_ref, 0, wx_ref[...])
-    gate_ref[...] = silu(gate_ref[...])
+    copies[0].wait()
+    copies[1].wait()
+    reqs = plan_ref.shape[0]
+    owners = counts_ref.shape[0]
+    for d in range(owners):
+        info_ref[INFO + d] = 0
+
+    def look(r, carry):
+        kept_to, kept_from, has_kept, moved_to, has_moved = carry
+        home, local = r // slots, r % slots
+        goal = plan_ref[r]
+        live = local < counts_ref[home]
+        owner, place = goal // slots, goal % slots
+        mine = live & (owner == me)
+        own = mine & (home == me)
+        into = mine & (home != me)
+
+        @pl.when(live & (owner != home))
+        def _():
+            info_ref[INFO + owner] = home
+
+        return (
+            jnp.where(own, place, kept_to), jnp.where(own, local, kept_from),
+            jnp.where(own, 1, has_kept), jnp.where(into, place, moved_to),
+            jnp.where(into, 1, has_moved),
+        )
+
+    carry = (jnp.int32(0),) * 5
+    if reqs <= 32:
+        for r in range(reqs):
+            carry = look(r, carry)
+    else:
+        carry = lax.fori_loop(0, reqs, look, carry)
+    kept_to, kept_from, has_kept, moved_to, has_moved = carry
+    moved_to = jnp.where(has_moved > 0, moved_to, jnp.where(has_kept > 0, 1 - kept_to, 0))
+    kept_to = 1 - moved_to
+    for i, v in enumerate((kept_to, kept_from, has_kept, moved_to, has_moved, me)):
+        info_ref[i] = v
+    copies += copy_rows(state_hbm.at[kept_from], kept_ref, sems, len(copies), COPIES)
+    shape = perm_ref.shape
+    line = lax.broadcasted_iota(jnp.int32, shape, 0)
+    lane = lax.broadcasted_iota(jnp.int32, shape, 1)
+    span = shape[0] // QUAD
+    p = (line % span // (2 * steps) * QUAD + line // span) * 2 + line % (2 * steps) // steps
+    hit = (lane // LANES == line % steps) & (lane % P_SIZE == p)
+    perm_ref[...] = jnp.where(hit, 1.0, 0.0).astype(jnp.bfloat16)
+    shape = place_ref.shape
+    line = lax.broadcasted_iota(jnp.int32, shape, 0)
+    lane = lax.broadcasted_iota(jnp.int32, shape, 1)
+    place_ref[...] = jnp.where(lane // P_SIZE == line, 1.0, 0.0).astype(jnp.bfloat16)
     rate = jnp.exp(rate_ref[...])
     raw = [dt_ref[s] + bias_ref[...] for s in range(slots)]
     delta = [jnp.maximum(v, 0.0) + jnp.log1p(jnp.exp(-jnp.abs(v))) for v in raw]
@@ -360,51 +417,14 @@
         wide = jnp.sum(jnp.where(head == lane, total, 0.0), axis=1, keepdims=True)
         wide_ref[s] = jnp.broadcast_to(wide, (heads, LANES))
     skipd_ref[...] = out[2 * slots * run :]
-    shape = perm_ref.shape
-    line = lax.broadcasted_iota(jnp.int32, shape, 0)
-    lane = lax.broadcasted_iota(jnp.int32, shape, 1)
-    span = shape[0] // QUAD
-    p = (line % span // (2 * steps) * QUAD + line // span) * 2 + line % (2 * steps) // steps
-    hit = (lane // LANES == line % steps) & (lane % P_SIZE == p)
-    perm_ref[...] = jnp.where(hit, 1.0, 0.0).astype(jnp.bfloat16)
-    for copy in copies:
+    for copy in copies[2:5]:
         copy.wait()
-    reqs = plan_ref.shape[0]
-    owners = counts_ref.shape[0]
-    for d in range(owners):
-        info_ref[INFO + d] = 0
-
-    def look(r, carry):
-        kept_to, kept_from, has_kept, moved_to, has_moved = carry
-        home, local = r // slots, r % slots
-        goal = plan_ref[r]
-        live = local < counts_ref[home]
-        owner, place = goal // slots, goal % slots
-        mine = live & (owner == me)
-        own = mine & (home == me)
-        into = mine & (home != me)
-
-        @pl.when(live & (owner != home))
-        def _():
-            info_ref[INFO + owner] = home
-
-        return (
-            jnp.where(own, place, kept_to), jnp.where(own, local, kept_from),
-            jnp.where(own, 1, has_kept), jnp.where(into, place, moved_to),
-            jnp.where(into, 1, has_moved),
-        )
-
-    carry = (jnp.int32(0),) * 5
-    if reqs <= 32:
-        for r in range(reqs):
-            carry = look(r, carry)
-    else:
-        carry = lax.fori_loop(0, reqs, look, carry)
-    kept_to, kept_from, has_kept, moved_to, has_moved = carry
-    moved_to = jnp.where(has_moved > 0, moved_to, jnp.where(has_kept > 0, 1 - kept_to, 0))
-    kept_to = 1 - moved_to
-    for i, v in enumerate((kept_to, kept_from, has_kept, moved_to, has_moved, me)):
-        info_ref[i] = v
+    x = [x_ref[s].astype(jnp.float32) for s in range(slots)]
+    for s in range(slots):
+        dense_rows(xd_ref.at[s], 0, x[s])
+        dense_rows(gate_ref.at[s], 0, z_ref[s].astype(jnp.float32))
+    dense_rows(wxd_ref, 0, wx_ref[...])
+    gate_ref[...] = silu(gate_ref[...])
     full = [jnp.where(kept_to == s, has_kept, has_moved) > 0 for s in range(slots)]
     for k in range(taps):
         t = steps - taps + k
@@ -413,6 +433,8 @@
         for s in range(slots):
             pairs = bc_ref[s, t].astype(jnp.float32)
             cb_ref[s, k] = jnp.where(full[s], pairs, 0.0).astype(jnp.bfloat16)
+    for copy in copies[5:]:
+        copy.wait()
 
 
 def slot_inputs(slot, steps, x_ref, bc_ref, gate_ref, dec_ref, dt_ref):
@@ -425,8 +447,8 @@
 
 def kept_kernel(
     info_ref, state_ref, cx_ref, cb_ref, x_ref, bc_ref, gate_ref, dec_ref, dt_ref, skip_ref,
-    wx_ref, bx_ref, wb_ref, bb_ref, perm_ref, wide_ref,
-    out_hbm, gated_ref, sums_ref, spread_ref, mixed_ref, turn_ref, rows_ref, new_ref, sem,
+    wx_ref, bx_ref, wb_ref, bb_ref, perm_ref, wide_ref, place_ref,
+    out_hbm, gated_ref, sums_ref, spread_ref, mixed_ref, turn_ref, rows_ref, new_ref, sems,
 ):
     steps = bc_ref.shape[1]
     blocks = bx_ref.shape[0]
@@ -446,20 +468,20 @@
         new_ref[:, j * LANES : (j + 1) * LANES] = jnp.where(full, new, 0.0)
 
     def tile(j):
-        return state_ref[origin, :, j * LANES : (j + 1) * LANES]
+        return state_ref[:, j * LANES : (j + 1) * LANES]
 
     mixed = against_c(tile, lambda j: j, cs, perm_ref, turn_ref)
     gated, sums = gated_steps(
         mixed, None, xs, bs, cs, dec, dts, skip_ref[...], gate, mixed_ref
     )
     spread = spread_x(xs, dec, dts, spread_ref)
-    new_state(tile, lambda j: j, wide_ref[slot], spread, bs, write)
-    copy = pltpu.make_async_copy(new_ref, out_hbm.at[slot], sem)
-    copy.start()
+    new_state(tile, lambda j: j, wide_ref[slot], spread, bs, place_ref, write)
+    copies = copy_rows(new_ref, out_hbm.at[slot], sems, 0, COPIES)
     for t in range(steps):
         gated_ref[t] = gated[t]
     sums_ref[...] = jnp.concatenate(sums, 0)
-    copy.wait()
+    for copy in copies:
+        copy.wait()
 
 
 def piece_tiles(masks, me, got_refs, heads):
@@ -537,14 +559,14 @@
     pieces = len(masks)
     got_refs = refs[:pieces]
     (
-        held_hbm, kept_ref, moved_ref, norm_ref, spread_ref, b_ref, wide_ref,
+        held_hbm, spread_ref, b_ref, wide_ref, place_ref, kept_ref, moved_ref, norm_ref,
         out_hbm, ready_ref, rows_ref, new_ref, sems,
     ) = refs[pieces:]
     del held_hbm
     direct = pieces > 1
-    steps, blocks = kept_ref.shape[:2]
     heads = wide_ref.shape[0]
-    each = (got_refs[0].shape[-2] - AUX) // heads
+    count = P_SIZE * P_SIZE // LANES
+    each = (got_refs[0].shape[-2] - AUX) // heads if direct else count
     slot, full, me = info_ref[3], info_ref[4] > 0, info_ref[5]
     _, tile, first = piece_tiles(masks, me, got_refs, heads)
     copies = []
@@ -552,19 +574,17 @@
     def write(j, new):
         at = pl.ds(pl.multiple_of(first(j) * LANES, LANES), LANES)
         new_ref[:, at] = jnp.where(full, new, 0.0)
-        if direct and j % each == each - 1:
+        if j % each == each - 1:
             span = pl.ds(pl.multiple_of(first(j - each + 1) * LANES, LANES), each * LANES)
             copy = pltpu.make_async_copy(
-                new_ref.at[:, span], out_hbm.at[slot, :, span], sems.at[j // each]
+                new_ref.at[:, span], out_hbm.at[slot, :, span], sems.at[len(copies)]
             )
             copy.start()
             copies.append(copy)
 
-    bs = [b_ref[t] for t in range(steps)]
-    new_state(tile, first, wide_ref[...], spread_ref[...], bs, write)
-    if not direct:
-        copies.append(pltpu.make_async_copy(new_ref, out_hbm.at[slot], sems.at[0]))
-        copies[0].start()
+    bs = [b_ref[t] for t in range(b_ref.shape[0])]
+    new_state(tile, first, wide_ref[...], spread_ref[...], bs, place_ref, write)
+    steps, blocks = kept_ref.shape[:2]
     for which, ref in enumerate((kept_ref, moved_ref)):
         for t in range(steps):
             rows_ref[t * blocks : (t + 1) * blocks, :] = ref[t] * norm_ref[...]
@@ -678,26 +698,30 @@
 
     spread = exchange(payload)
 
-    _, x_late = lax.optimization_barrier((payload[0], x_in))
+    _, me_late = lax.optimization_barrier((payload[0], me))
     rows = (places, steps * blocks, LANES)
-    info, x_dense, gate, dec, dt_dense, wide, skip, wx, perm, new_conv_x, new_conv_bc = call(
-        prep_kernel, "prep", [smem] + [anywhere] * 2 + [vmem] * 8, [smem] + [vmem] * 10,
+    info, x_dense, gate, dec, dt_dense, wide, skip, wx, perm, place, kept_state, *convs = call(
+        prep_kernel, "prep", [smem] + [anywhere] * 6 + [vmem] * 5, [smem] + [vmem] * 12,
         [
             shaped(INFO + owners, dtype=jnp.int32), shaped(*rows), shaped(*rows), shaped(*rows),
             shaped(*rows), shaped(places, heads, LANES), shaped(blocks, LANES),
             shaped((taps + 1) * blocks, LANES),
             shaped(QUAD * P_SIZE, 2 * steps * P_SIZE, dtype=jnp.bfloat16),
+            shaped(P_SIZE, columns, dtype=jnp.bfloat16), shaped(heads, columns),
             shaped(taps, places, channels, dtype=jnp.bfloat16),
             shaped(*conv_bc_state.shape, dtype=jnp.bfloat16),
         ],
         [
             pltpu.SMEM(counts.shape, jnp.int32),
             pltpu.SMEM(move_plan.shape, jnp.int32),
-            pltpu.SemaphoreType.DMA((2,)),
+            pltpu.VMEM(x_in.shape, jnp.bfloat16),
+            pltpu.VMEM(z_in.shape, jnp.bfloat16),
+            pltpu.VMEM(conv_w_x.shape, f32),
+            pltpu.SemaphoreType.DMA((5 + COPIES,)),
         ],
     )(
-        me, *in_hbm(counts, move_plan), x_late, z_in, bc_in, dt_in, dt_bias.reshape(1, -1),
-        a_log.reshape(1, -1), d_skip.reshape(1, -1), conv_w_x,
+        me_late, *in_hbm(counts, move_plan, x_in, z_in, conv_w_x, ssm_state), bc_in, dt_in,
+        dt_bias.reshape(1, -1), a_log.reshape(1, -1), d_skip.reshape(1, -1),
     )
 
     picked = call(
@@ -711,15 +735,15 @@
     common += [conv_b_x.reshape(blocks, LANES), conv_w_bc, conv_b_bc, perm, wide]
     scratch = [pltpu.VMEM((steps * heads, LANES), f32)] * 2 + [pltpu.VMEM((LANES, LANES), f32)]
     held, kept_gated, kept_sums = call(
-        kept_kernel, "kept", [smem] + [vmem] * (3 + len(common)), [anywhere, vmem, vmem],
+        kept_kernel, "kept", [smem] + [vmem] * (4 + len(common)), [anywhere, vmem, vmem],
         [shaped(places, heads, columns), shaped(steps, blocks, LANES), shaped(steps, LANES)],
         scratch
         + [
             pltpu.VMEM((taps * blocks, LANES), f32),
             pltpu.VMEM((heads, columns), f32),
-            pltpu.SemaphoreType.DMA,
+            pltpu.SemaphoreType.DMA((COPIES,)),
         ],
-    )(info, ssm_state, conv_x_taps, conv_bc_state, *common)
+    )(info, kept_state, conv_x_taps, conv_bc_state, *common, place)
     moved_gated, sums, spread_rows, b_steps, wide_scaled = call(
         functools.partial(moved_kernel, masks), "moved",
         [smem] + [vmem] * (pieces + 1 + len(common)), [vmem] * 5,
@@ -733,7 +757,7 @@
     theirs = lax.ppermute(sums, "tp", [(0, 1), (1, 0)])
     new_ssm, ready = call(
         functools.partial(state_kernel, masks), "state",
-        [smem] + [vmem] * pieces + [anywhere] + [vmem] * 6, [anywhere, vmem],
+        [smem] + [vmem] * pieces + [anywhere] + [vmem] * 7, [anywhere, vmem],
         [shaped(places, heads, columns), shaped(places, steps, channels)],
         [
             pltpu.VMEM((steps * blocks, LANES), f32),
@@ -742,14 +766,14 @@
         ],
         input_output_aliases={1 + pieces: 0},
     )(
-        info, *got, held, kept_gated, moved_gated, norm_w.reshape(blocks, LANES), spread_rows,
-        b_steps, wide_scaled,
+        info, *got, held, spread_rows, b_steps, wide_scaled, place, kept_gated, moved_gated,
+        norm_w.reshape(blocks, LANES),
     )
     y_out = call(
         norm_kernel, "norm", [smem] + [vmem] * 3, vmem,
         shaped(places, steps, channels, dtype=jnp.bfloat16),
     )(info, ready, sums, theirs)
-    return (y_out, new_ssm, jnp.transpose(new_conv_x, (1, 0, 2)), new_conv_bc)
+    return (y_out, new_ssm, jnp.transpose(convs[0], (1, 0, 2)), convs[1])
 
 
 def solution(mesh):

time: 41.4 us -> 40.6 us (0.981)
  local copies, waits for them, and re-layouts: 2.57 us -> 0.05 us
  Pallas kernels: 12.2 us -> 13.5 us
  waiting for transfers between devices: 1.71 us -> 2.24 us
    unnamed x30 -> x22, local copies, waits for them, and re-layouts: 2.57 us -> 0.05 us
    pallas_call x2, Pallas kernels: 4.83 us -> 6.24 us  [the longest x1 3.29 us: on_device(): call(prep_kernel, 'prep', [smem] + [anywhere] * 6 + [vmem] * 5, [smem] +...]
    ppermute x14, waiting for transfers between devices: 1.71 us -> 2.24 us  [exchange(): out[i] = lax.ppermute(values[i], 'req', [(o, o ^ k) for o in range(owners)])]
  transfers between devices with their start and end apart: 15 -> 15, of which waited for: 3 -> 4; matrix products, arithmetic and copies ran while one was open for 0% -> 0% of each run, Pallas kernels for 17% -> 20%
where the time goes in v4:
time: 40.6 us; the launch traced here: 40.4 us
  starting transfers between devices  23.7 us (58%)
  Pallas kernels  13.5 us (33%)
  waiting for transfers between devices  2.24 us (6%)
  between operations  0.87 us (2%)
    ppermute x14, starting transfers between devices, exchange(): out[i] = lax.ppermute(values[i], 'req', [(o, o ^ k) for o in range(owners)])  23.7 us
    pallas_call x1, Pallas kernels, on_device(): call(prep_kernel, 'prep', [smem] + [anywhere] * 6 + [vmem] * 5, [smem] +...  3.29 us
    pallas_call x1, Pallas kernels, on_device(): call(kept_kernel, 'kept', [smem] + [vmem] * (4 + len(common)), [anywhere,...  2.95 us
    ppermute x14, waiting for transfers between devices, exchange(): out[i] = lax.ppermute(values[i], 'req', [(o, o ^ k) for o in range(owners)])  2.24 us
    pallas_call x1, Pallas kernels, on_device(): call(functools.partial(state_kernel, masks), 'state', [smem] + [vmem] * p...  2.04 us
    pallas_call x1, Pallas kernels, on_device(): call(functools.partial(pack_kernel, masks), 'pack', [smem] + [anywhere] *...  1.86 us
    pallas_call x1, Pallas kernels, on_device(): call(functools.partial(moved_kernel, masks), 'moved', [smem] + [vmem] * (...  1.56 us
    pallas_call x1, Pallas kernels, on_device(): call(norm_kernel, 'norm', [smem] + [vmem] * 3, vmem, shaped(places, steps...  1.21 us
  transfers between devices with their start and end apart: 15, of which 4 were waited for; matrix products, arithmetic and copies ran while one was open for 0% of the time, Pallas kernels for 20%

profile of v4, /device:TPU:0, one launch (start us, length us, event | category | flops | bytes accessed | tf_op | source)
XLA Modules:
  0.0 40.4 jit_solution(17909566536834576620)
XLA Ops:
  0.7 1.9 %pack.1 = (s16[272,128]{1,0:T(8,128)(2,1)S(1)}, s16[272,128]{1,0:T(8,128)(2,1)S(1)}, s16[272,128]{1,0:T(8,128)(2,1)S(1)}, s16[272,128]{1,0:T(8,128)(2,1)S(1)}, s...) custom-call(s32[1]{0:T(128)} %bitcast.me_ref, ...), custom_call_target="tpu_custom_call" | custom-call | tf_op jit(solution)/shard_map/pack/pallas_call | solution.py:677
  2.6 5.1 %collective-permute-start = (s16[272,128]{1,0:T(8,128)(2,1)S(1)}, s16[272,128]{1,0:T(8,128)(2,1)S(1)}, u32[]{:S(2)}, u32[]{:S(2)}) collective-permute-start(s16[272,128]{1,0:T(8,128)(2,1)S(1)} %get-tuple-element.48), channel_id=1, source_target_pairs={{0,12},{2,14},{4,8},{6,10},{8,4},{10,6},{12,0},{14,2},{1,13},{3,15... | collective-permute-start | bytes 208904 | tf_op jit(solution)/shard_map/ppermute | solution.py:696
  7.7 1.5 %collective-permute-start.1 = (s16[272,128]{1,0:T(8,128)(2,1)S(1)}, s16[272,128]{1,0:T(8,128)(2,1)S(1)}, u32[]{:S(2)}, u32[]{:S(2)}) collective-permute-start(s16[272,128]{1,0:T(8,128)(2,1)S(1)} %get-tuple-element.49), channel_id=1, source_target_pairs={{0,2},{2,0},{4,6},{6,4},{8,10},{10,8},{12,14},{14,12},{1,3},{3,1},... | collective-permute-start | bytes 208904 | tf_op jit(solution)/shard_map/ppermute | solution.py:696
  9.2 0.0 collective-permute-start.2
  9.3 0.8 %collective-permute-start.3 = (s16[272,128]{1,0:T(8,128)(2,1)S(1)}, s16[272,128]{1,0:T(8,128)(2,1)S(1)}, u32[]{:S(2)}, u32[]{:S(2)}) collective-permute-start(s16[272,128]{1,0:T(8,128)(2,1)S(1)} %get-tuple-element.51), channel_id=1, source_target_pairs={{0,6},{2,4},{4,2},{6,0},{8,14},{10,12},{12,10},{14,8},{1,7},{3,5},... | collective-permute-start | bytes 208904 | tf_op jit(solution)/shard_map/ppermute | solution.py:696
  10.1 4.4 %collective-permute-start.4 = (s16[272,128]{1,0:T(8,128)(2,1)S(1)}, s16[272,128]{1,0:T(8,128)(2,1)S(1)}, u32[]{:S(2)}, u32[]{:S(2)}) collective-permute-start(s16[272,128]{1,0:T(8,128)(2,1)S(1)} %get-tuple-element.52), channel_id=1, source_target_pairs={{0,10},{2,8},{4,14},{6,12},{8,2},{10,0},{12,6},{14,4},{1,11},{3,9}... | collective-permute-start | bytes 208904 | tf_op jit(solution)/shard_map/ppermute | solution.py:696
  14.5 0.0 collective-permute-start.5
  14.5 0.6 %collective-permute-start.6 = (s16[272,128]{1,0:T(8,128)(2,1)S(1)}, s16[272,128]{1,0:T(8,128)(2,1)S(1)}, u32[]{:S(2)}, u32[]{:S(2)}) collective-permute-start(s16[272,128]{1,0:T(8,128)(2,1)S(1)} %get-tuple-element.54), channel_id=1, source_target_pairs={{0,8},{2,10},{4,12},{6,14},{8,0},{10,2},{12,4},{14,6},{1,9},{3,11}... | collective-permute-start | bytes 208904 | tf_op jit(solution)/shard_map/ppermute | solution.py:696
  15.1 3.3 %prep.1 = (s32[16]{0:T(128)S(1)}, f32[2,128,128]{2,1,0:T(8,128)S(1)}, f32[2,128,128]{2,1,0:T(8,128)S(1)}, f32[2,128,128]{2,1,0:T(8,128)S(1)}, f32[2,128,128]{2,1...) custom-call(s32[1]{0:T(128)} %bitcast.me_ref, ...), custom_call_target="tpu_custom_call" | custom-call | tf_op jit(solution)/shard_map/prep/pallas_call | solution.py:703
  18.5 0.6 %collective-permute-done.5.refs_6_ = s16[272,128]{1,0:T(8,128)(2,1)S(1)} collective-permute-done((s16[272,128]{1,0:T(8,128)(2,1)S(1)}, s16[272,128]{1,0:T(8,128)(2,1)S(1)}, u32[]{:S(2)}, u32[]{:S(2)}) %collective-permute-start.5) | collective-permute-done | bytes 69664 | tf_op jit(solution)/shard_map/ppermute | solution.py:696
  19.0 1.0 %collective-permute-done.6.refs_7_ = s16[272,128]{1,0:T(8,128)(2,1)S(1)} collective-permute-done((s16[272,128]{1,0:T(8,128)(2,1)S(1)}, s16[272,128]{1,0:T(8,128)(2,1)S(1)}, u32[]{:S(2)}, u32[]{:S(2)}) %collective-permute-start.6) | collective-permute-done | bytes 69664 | tf_op jit(solution)/shard_map/ppermute | solution.py:696
  20.0 0.6 %pick.1 = (s16[272,128]{1,0:T(8,128)(2,1)S(1)}, s16[272,128]{1,0:T(8,128)(2,1)S(1)}, s16[272,128]{1,0:T(8,128)(2,1)S(1)}, s16[272,128]{1,0:T(8,128)(2,1)S(1)}, s...) custom-call(s32[16]{0:T(128)S(1)} %get-tuple-element.56.info_ref, ...), custom_call_target="tpu_custom_call" | custom-call | tf_op jit(solution)/shard_map/pick/pallas_call | solution.py:727
  20.7 2.8 %collective-permute-start.7 = (s16[272,128]{1,0:T(8,128)(2,1)S(1)}, s16[272,128]{1,0:T(8,128)(2,1)S(1)}, u32[]{:S(2)}, u32[]{:S(2)}) collective-permute-start(s16[272,128]{1,0:T(8,128)(2,1)S(1)} %get-tuple-element.57), channel_id=1, source_target_pairs={{0,12},{2,14},{4,8},{6,10},{8,4},{10,6},{12,0},{14,2},{1,13},{3,15... | collective-permute-start | bytes 208904 | tf_op jit(solution)/shard_map/ppermute | solution.py:696
  23.5 1.4 %collective-permute-start.8 = (s16[272,128]{1,0:T(8,128)(2,1)S(1)}, s16[272,128]{1,0:T(8,128)(2,1)S(1)}, u32[]{:S(2)}, u32[]{:S(2)}) collective-permute-start(s16[272,128]{1,0:T(8,128)(2,1)S(1)} %get-tuple-element.58), channel_id=1, source_target_pairs={{0,2},{2,0},{4,6},{6,4},{8,10},{10,8},{12,14},{14,12},{1,3},{3,1},... | collective-permute-start | bytes 208904 | tf_op jit(solution)/shard_map/ppermute | solution.py:696
  24.9 1.2 %collective-permute-start.9 = (s16[272,128]{1,0:T(8,128)(2,1)S(1)}, s16[272,128]{1,0:T(8,128)(2,1)S(1)}, u32[]{:S(2)}, u32[]{:S(2)}) collective-permute-start(s16[272,128]{1,0:T(8,128)(2,1)S(1)} %get-tuple-element.59), channel_id=1, source_target_pairs={{0,14},{2,12},{4,10},{6,8},{8,6},{10,4},{12,2},{14,0},{1,15},{3,13... | collective-permute-start | bytes 208904 | tf_op jit(solution)/shard_map/ppermute | solution.py:696
  26.0 0.8 %collective-permute-start.10 = (s16[272,128]{1,0:T(8,128)(2,1)S(1)}, s16[272,128]{1,0:T(8,128)(2,1)S(1)}, u32[]{:S(2)}, u32[]{:S(2)}) collective-permute-start(s16[272,128]{1,0:T(8,128)(2,1)S(1)} %get-tuple-element.60), channel_id=1, source_target_pairs={{0,6},{2,4},{4,2},{6,0},{8,14},{10,12},{12,10},{14,8},{1,7},{3,5},... | collective-permute-start | bytes 208904 | tf_op jit(solution)/shard_map/ppermute | solution.py:696
  26.8 3.4 %collective-permute-start.11 = (s16[272,128]{1,0:T(8,128)(2,1)S(1)}, s16[272,128]{1,0:T(8,128)(2,1)S(1)}, u32[]{:S(2)}, u32[]{:S(2)}) collective-permute-start(s16[272,128]{1,0:T(8,128)(2,1)S(1)} %get-tuple-element.61), channel_id=1, source_target_pairs={{0,10},{2,8},{4,14},{6,12},{8,2},{10,0},{12,6},{14,4},{1,11},{3,9}... | collective-permute-start | bytes 208904 | tf_op jit(solution)/shard_map/ppermute | solution.py:696
  30.3 1.6 %collective-permute-start.13 = (s16[272,128]{1,0:T(8,128)(2,1)S(1)}, s16[272,128]{1,0:T(8,128)(2,1)S(1)}, u32[]{:S(2)}, u32[]{:S(2)}) collective-permute-start(s16[272,128]{1,0:T(8,128)(2,1)S(1)} %get-tuple-element.63), channel_id=1, source_target_pairs={{0,8},{2,10},{4,12},{6,14},{8,0},{10,2},{12,4},{14,6},{1,9},{3,11}... | collective-permute-start | bytes 208904 | tf_op jit(solution)/shard_map/ppermute | solution.py:696
  31.9 3.0 %kept.1 = (f32[2,64,4096]{2,1,0:T(8,128)}, f32[4,32,128]{2,1,0:T(8,128)S(1)}, f32[4,128]{1,0:T(4,128)S(1)}) custom-call(s32[16]{0:T(128)S(1)} %get-tuple-element.56.info_ref, f32[64,4096]{1,0:T(8,128)S(1)} %get-tuple-element.64.state_ref, bf16[3,2,4096]{2,1,0:T(2,128)(2,1)S(1)} %bitcast.9, bf16[2,3,2,128]{3,2,1,0:T(2,128)(2,1)S(1)} %copy-done.5, ...), custom_call_target="tpu_custom_call" | custom-call | tf_op jit(solution)/shard_map/kept/pallas_call | solution.py:737
  34.9 0.4 %collective-permute-done.11.refs_5_ = s16[272,128]{1,0:T(8,128)(2,1)S(1)} collective-permute-done((s16[272,128]{1,0:T(8,128)(2,1)S(1)}, s16[272,128]{1,0:T(8,128)(2,1)S(1)}, u32[]{:S(2)}, u32[]{:S(2)}) %collective-permute-start.11) | collective-permute-done | bytes 69664 | tf_op jit(solution)/shard_map/ppermute | solution.py:696
  35.3 0.2 collective-permute-done.13.refs_7_
  35.5 1.6 %moved.1 = (f32[4,32,128]{2,1,0:T(8,128)S(1)}, f32[8,128]{1,0:T(8,128)S(1)}, bf16[256,256]{1,0:T(8,128)(2,1)S(1)}, f32[4,2,128]{2,1,0:T(2,128)S(1)}, f32[64,128]{1,0:T(8,128)S(1)}) custom-call(s32[16]{0:T(128)S(1)} %get-tuple-element.56.info_ref, s16[272,128]{1,0:T(8,128)(2,1)S(1)} %get-tuple-element.55.refs_0_, ...), custom_call_target="tpu_custom_call" | custom-call | tf_op jit(solution)/shard_map/moved/pallas_call | solution.py:747
  37.1 2.0 %state.1 = (f32[2,64,4096]{2,1,0:T(8,128)}, f32[2,4,4096]{2,1,0:T(4,128)S(1)}) custom-call(s32[16]{0:T(128)S(1)} %get-tuple-element.56.info_ref, s16[272,128]{1,0:T(8,128)(2,1)S(1)} %get-tuple-element.55.refs_0_, s16[272,128]{1,0:T(8,128)(2,1)S(1)} %collective-permute-done.7.refs_1_, ...), custom_call_target="tpu_custom_call", output_to_operand_aliasing={{0}: (9, {})} | custom-call | tf_op jit(solution)/shard_map/state/pallas_call | solution.py:758
  39.2 1.2 %norm.1 = bf16[2,4,4096]{2,1,0:T(4,128)(2,1)} custom-call(s32[16]{0:T(128)S(1)} %get-tuple-element.56.info_ref, f32[2,4,4096]{2,1,0:T(4,128)S(1)} %get-tuple-element.81.ready_ref, f32[8,128]{1,0:T(8,128)S(1)} %get-tuple-element.82.mine_ref, f32[8,128]{1,0:T(8,128)S(1)} %collective-permute-done.14.theirs_ref), custom_call_target="tpu_custom_call" | custom-call | tf_op jit(solution)/shard_map/norm/pallas_call | solution.py:772
  (35 shorter events, 0.1 us)
Async XLA Ops:
  0.6 14.5 %copy-start.2 = (bf16[2,4,2,128]{3,2,1,0:T(2,128)(2,1)S(1)}, bf16[2,4,2,128]{3,2,1,0:T(2,128)(2,1)}, u32[]{:S(2)}) copy-start(bf16[2,4,2,128]{3,2,1,0:T(2,128)(2,1)} %refs_10_.1) | copy-start | bytes 12292
  0.6 14.5 %copy-start.10 = (f32[64]{0:T(128)S(1)}, f32[64]{0:T(128)}, u32[]{:S(2)}) copy-start(f32[64]{0:T(128)} %param.32) | copy-start | bytes 772
  0.7 14.5 %copy-start.9 = (f32[64]{0:T(128)S(1)}, f32[64]{0:T(128)}, u32[]{:S(2)}) copy-start(f32[64]{0:T(128)} %param.31) | copy-start | bytes 772
  0.7 31.2 %copy-start = (bf16[2,3,4096]{2,0,1:T(2,128)(2,1)S(1)}, bf16[2,3,4096]{2,0,1:T(2,128)(2,1)}, u32[]{:S(2)}) copy-start(bf16[2,3,4096]{2,0,1:T(2,128)(2,1)} %param.20) | copy-start | bytes 147460
  0.7 31.2 %copy-start.1 = (f32[4096]{0:T(1024)S(1)}, f32[4096]{0:T(1024)}, u32[]{:S(2)}) copy-start(f32[4096]{0:T(1024)} %param.27) | copy-start | bytes 49156
  0.7 31.2 %copy-start.4 = (f32[4,2,128]{2,1,0:T(2,128)S(1)}, f32[4,2,128]{2,1,0:T(2,128)}, u32[]{:S(2)}) copy-start(f32[4,2,128]{2,1,0:T(2,128)} %refs_17_.1) | copy-start | bytes 12292
  0.7 31.2 %copy-start.5 = (bf16[2,3,2,128]{3,2,1,0:T(2,128)(2,1)S(1)}, bf16[2,3,2,128]{3,2,1,0:T(2,128)(2,1)}, u32[]{:S(2)}) copy-start(bf16[2,3,2,128]{3,2,1,0:T(2,128)(2,1)} %cb_ref.1) | copy-start | bytes 9220
  0.7 31.2 %copy-start.7 = (f32[2,128]{1,0:T(2,128)S(1)}, f32[2,128]{1,0:T(2,128)}, u32[]{:S(2)}) copy-start(f32[2,128]{1,0:T(2,128)} %refs_18_.1) | copy-start | bytes 3076
  2.6 11.9 %collective-permute-start = (s16[272,128]{1,0:T(8,128)(2,1)S(1)}, s16[272,128]{1,0:T(8,128)(2,1)S(1)}, u32[]{:S(2)}, u32[]{:S(2)}) collective-permute-start(s16[272,128]{1,0:T(8,128)(2,1)S(1)} %get-tuple-element.48), channel_id=1, source_target_pairs={{0,12},{2,14},{4,8},{6,10},{8,4},{10,6},{12,0},{14,2},{1,13},{3,15... | collective-permute-start | bytes 208904 | tf_op jit(solution)/shard_map/ppermute | solution.py:696
  7.7 6.8 %collective-permute-start.1 = (s16[272,128]{1,0:T(8,128)(2,1)S(1)}, s16[272,128]{1,0:T(8,128)(2,1)S(1)}, u32[]{:S(2)}, u32[]{:S(2)}) collective-permute-start(s16[272,128]{1,0:T(8,128)(2,1)S(1)} %get-tuple-element.49), channel_id=1, source_target_pairs={{0,2},{2,0},{4,6},{6,4},{8,10},{10,8},{12,14},{14,12},{1,3},{3,1},... | collective-permute-start | bytes 208904 | tf_op jit(solution)/shard_map/ppermute | solution.py:696
  9.2 9.2 %collective-permute-start.2 = (s16[272,128]{1,0:T(8,128)(2,1)S(1)}, s16[272,128]{1,0:T(8,128)(2,1)S(1)}, u32[]{:S(2)}, u32[]{:S(2)}) collective-permute-start(s16[272,128]{1,0:T(8,128)(2,1)S(1)} %get-tuple-element.50), channel_id=1, source_target_pairs={{0,14},{2,12},{4,10},{6,8},{8,6},{10,4},{12,2},{14,0},{1,15},{3,13... | collective-permute-start | bytes 208904 | tf_op jit(solution)/shard_map/ppermute | solution.py:696
  9.3 9.2 %collective-permute-start.3 = (s16[272,128]{1,0:T(8,128)(2,1)S(1)}, s16[272,128]{1,0:T(8,128)(2,1)S(1)}, u32[]{:S(2)}, u32[]{:S(2)}) collective-permute-start(s16[272,128]{1,0:T(8,128)(2,1)S(1)} %get-tuple-element.51), channel_id=1, source_target_pairs={{0,6},{2,4},{4,2},{6,0},{8,14},{10,12},{12,10},{14,8},{1,7},{3,5},... | collective-permute-start | bytes 208904 | tf_op jit(solution)/shard_map/ppermute | solution.py:696
  10.1 8.4 %collective-permute-start.4 = (s16[272,128]{1,0:T(8,128)(2,1)S(1)}, s16[272,128]{1,0:T(8,128)(2,1)S(1)}, u32[]{:S(2)}, u32[]{:S(2)}) collective-permute-start(s16[272,128]{1,0:T(8,128)(2,1)S(1)} %get-tuple-element.52), channel_id=1, source_target_pairs={{0,10},{2,8},{4,14},{6,12},{8,2},{10,0},{12,6},{14,4},{1,11},{3,9}... | collective-permute-start | bytes 208904 | tf_op jit(solution)/shard_map/ppermute | solution.py:696
  14.5 4.6 %collective-permute-start.5 = (s16[272,128]{1,0:T(8,128)(2,1)S(1)}, s16[272,128]{1,0:T(8,128)(2,1)S(1)}, u32[]{:S(2)}, u32[]{:S(2)}) collective-permute-start(s16[272,128]{1,0:T(8,128)(2,1)S(1)} %get-tuple-element.53), channel_id=1, source_target_pairs={{0,4},{2,6},{4,0},{6,2},{8,12},{10,14},{12,8},{14,10},{1,5},{3,7},... | collective-permute-start | bytes 208904 | tf_op jit(solution)/shard_map/ppermute | solution.py:696
  14.5 5.5 %collective-permute-start.6 = (s16[272,128]{1,0:T(8,128)(2,1)S(1)}, s16[272,128]{1,0:T(8,128)(2,1)S(1)}, u32[]{:S(2)}, u32[]{:S(2)}) collective-permute-start(s16[272,128]{1,0:T(8,128)(2,1)S(1)} %get-tuple-element.54), channel_id=1, source_target_pairs={{0,8},{2,10},{4,12},{6,14},{8,0},{10,2},{12,4},{14,6},{1,9},{3,11}... | collective-permute-start | bytes 208904 | tf_op jit(solution)/shard_map/ppermute | solution.py:696
  20.7 16.5 %copy-start.3 = (f32[4096]{0:T(1024)S(1)}, f32[4096]{0:T(1024)}, u32[]{:S(2)}) copy-start(f32[4096]{0:T(1024)} %param.33) | copy-start | bytes 49156
  20.7 9.6 %collective-permute-start.7 = (s16[272,128]{1,0:T(8,128)(2,1)S(1)}, s16[272,128]{1,0:T(8,128)(2,1)S(1)}, u32[]{:S(2)}, u32[]{:S(2)}) collective-permute-start(s16[272,128]{1,0:T(8,128)(2,1)S(1)} %get-tuple-element.57), channel_id=1, source_target_pairs={{0,12},{2,14},{4,8},{6,10},{8,4},{10,6},{12,0},{14,2},{1,13},{3,15... | collective-permute-start | bytes 208904 | tf_op jit(solution)/shard_map/ppermute | solution.py:696
  23.5 6.8 %collective-permute-start.8 = (s16[272,128]{1,0:T(8,128)(2,1)S(1)}, s16[272,128]{1,0:T(8,128)(2,1)S(1)}, u32[]{:S(2)}, u32[]{:S(2)}) collective-permute-start(s16[272,128]{1,0:T(8,128)(2,1)S(1)} %get-tuple-element.58), channel_id=1, source_target_pairs={{0,2},{2,0},{4,6},{6,4},{8,10},{10,8},{12,14},{14,12},{1,3},{3,1},... | collective-permute-start | bytes 208904 | tf_op jit(solution)/shard_map/ppermute | solution.py:696
  24.9 10.0 %collective-permute-start.9 = (s16[272,128]{1,0:T(8,128)(2,1)S(1)}, s16[272,128]{1,0:T(8,128)(2,1)S(1)}, u32[]{:S(2)}, u32[]{:S(2)}) collective-permute-start(s16[272,128]{1,0:T(8,128)(2,1)S(1)} %get-tuple-element.59), channel_id=1, source_target_pairs={{0,14},{2,12},{4,10},{6,8},{8,6},{10,4},{12,2},{14,0},{1,15},{3,13... | collective-permute-start | bytes 208904 | tf_op jit(solution)/shard_map/ppermute | solution.py:696
  26.0 8.9 %collective-permute-start.10 = (s16[272,128]{1,0:T(8,128)(2,1)S(1)}, s16[272,128]{1,0:T(8,128)(2,1)S(1)}, u32[]{:S(2)}, u32[]{:S(2)}) collective-permute-start(s16[272,128]{1,0:T(8,128)(2,1)S(1)} %get-tuple-element.60), channel_id=1, source_target_pairs={{0,6},{2,4},{4,2},{6,0},{8,14},{10,12},{12,10},{14,8},{1,7},{3,5},... | collective-permute-start | bytes 208904 | tf_op jit(solution)/shard_map/ppermute | solution.py:696
  26.8 8.5 %collective-permute-start.11 = (s16[272,128]{1,0:T(8,128)(2,1)S(1)}, s16[272,128]{1,0:T(8,128)(2,1)S(1)}, u32[]{:S(2)}, u32[]{:S(2)}) collective-permute-start(s16[272,128]{1,0:T(8,128)(2,1)S(1)} %get-tuple-element.61), channel_id=1, source_target_pairs={{0,10},{2,8},{4,14},{6,12},{8,2},{10,0},{12,6},{14,4},{1,11},{3,9}... | collective-permute-start | bytes 208904 | tf_op jit(solution)/shard_map/ppermute | solution.py:696
  30.3 5.1 %collective-permute-start.12 = (s16[272,128]{1,0:T(8,128)(2,1)S(1)}, s16[272,128]{1,0:T(8,128)(2,1)S(1)}, u32[]{:S(2)}, u32[]{:S(2)}) collective-permute-start(s16[272,128]{1,0:T(8,128)(2,1)S(1)} %get-tuple-element.62), channel_id=1, source_target_pairs={{0,4},{2,6},{4,0},{6,2},{8,12},{10,14},{12,8},{14,10},{1,5},{3,7},... | collective-permute-start | bytes 208904 | tf_op jit(solution)/shard_map/ppermute | solution.py:696
  30.3 5.3 %collective-permute-start.13 = (s16[272,128]{1,0:T(8,128)(2,1)S(1)}, s16[272,128]{1,0:T(8,128)(2,1)S(1)}, u32[]{:S(2)}, u32[]{:S(2)}) collective-permute-start(s16[272,128]{1,0:T(8,128)(2,1)S(1)} %get-tuple-element.63), channel_id=1, source_target_pairs={{0,8},{2,10},{4,12},{6,14},{8,0},{10,2},{12,4},{14,6},{1,9},{3,11}... | collective-permute-start | bytes 208904 | tf_op jit(solution)/shard_map/ppermute | solution.py:696
  37.1 2.1 %collective-permute-start.14 = (f32[8,128]{1,0:T(8,128)S(1)}, f32[8,128]{1,0:T(8,128)S(1)}, u32[]{:S(2)}, u32[]{:S(2)}) collective-permute-start(f32[8,128]{1,0:T(8,128)S(1)} %get-tuple-element.82.mine_ref), channel_id=1, source_target_pairs={{0,1},{1,0},{2,3},{3,2},{4,5},{5,4},{6,7},{7,6},{8,9},{9,8},{10,11... | collective-permute-start | bytes 12296 | tf_op jit(solution)/shard_map/ppermute | solution.py:757
  (2 other events, 28.9 us)

commit v5 on v4

--- a/solution.py
+++ b/solution.py
@@ -559,28 +559,15 @@
     pieces = len(masks)
     got_refs = refs[:pieces]
     (
-        held_hbm, spread_ref, b_ref, wide_ref, place_ref, kept_ref, moved_ref, norm_ref,
-        out_hbm, ready_ref, rows_ref, new_ref, sems,
+        spread_ref, b_ref, wide_ref, place_ref, kept_ref, moved_ref, norm_ref,
+        new_ref, ready_ref, rows_ref,
     ) = refs[pieces:]
-    del held_hbm
-    direct = pieces > 1
-    heads = wide_ref.shape[0]
-    count = P_SIZE * P_SIZE // LANES
-    each = (got_refs[0].shape[-2] - AUX) // heads if direct else count
-    slot, full, me = info_ref[3], info_ref[4] > 0, info_ref[5]
-    _, tile, first = piece_tiles(masks, me, got_refs, heads)
-    copies = []
+    full, me = info_ref[4] > 0, info_ref[5]
+    _, tile, first = piece_tiles(masks, me, got_refs, wide_ref.shape[0])
 
     def write(j, new):
         at = pl.ds(pl.multiple_of(first(j) * LANES, LANES), LANES)
         new_ref[:, at] = jnp.where(full, new, 0.0)
-        if j % each == each - 1:
-            span = pl.ds(pl.multiple_of(first(j - each + 1) * LANES, LANES), each * LANES)
-            copy = pltpu.make_async_copy(
-                new_ref.at[:, span], out_hbm.at[slot, :, span], sems.at[len(copies)]
-            )
-            copy.start()
-            copies.append(copy)
 
     bs = [b_ref[t] for t in range(b_ref.shape[0])]
     new_state(tile, first, wide_ref[...], spread_ref[...], bs, place_ref, write)
@@ -592,11 +579,13 @@
             ready_ref[which, :, b * LANES : (b + 1) * LANES] = rows_ref[
                 pl.ds(b, steps, stride=blocks), :
             ]
-    for copy in copies:
-        copy.wait()
-
-
-def norm_kernel(info_ref, ready_ref, mine_ref, theirs_ref, out_ref):
+
+
+def norm_kernel(
+    info_ref, held_hbm, new_ref, ready_ref, mine_ref, theirs_ref, out_hbm, y_hbm, y_ref, sems
+):
+    del held_hbm
+    copies = copy_rows(new_ref, out_hbm.at[info_ref[3]], sems, 0, COPIES)
     steps = ready_ref.shape[1]
     factor = lax.rsqrt((mine_ref[...] + theirs_ref[...]) * (1.0 / (H * P_SIZE)) + 1e-05)
     for which in range(ready_ref.shape[0]):
@@ -604,7 +593,11 @@
         rows = factor[which * steps : (which + 1) * steps]
         for b in range(0, ready_ref.shape[2], LANES):
             values = jnp.where(full, ready_ref[which, :, b : b + LANES] * rows, 0.0)
-            out_ref[info_ref[3 * which], :, b : b + LANES] = values.astype(jnp.bfloat16)
+            y_ref[info_ref[3 * which], :, b : b + LANES] = values.astype(jnp.bfloat16)
+    copies.append(pltpu.make_async_copy(y_ref, y_hbm, sems.at[COPIES]))
+    copies[-1].start()
+    for copy in copies:
+        copy.wait()
 
 
 def partner_masks(owners):
@@ -698,7 +691,15 @@
 
     spread = exchange(payload)
 
-    _, me_late = lax.optimization_barrier((payload[0], me))
+    (
+        _, me_late, cx_late, cb_late, bc_late, dt_late, bias_late, rate_late, skip_late,
+        bx_late, wb_late, bb_late, norm_late,
+    ) = lax.optimization_barrier(
+        (
+            payload[0], me, conv_x_taps, conv_bc_state, bc_in, dt_in, dt_bias, a_log, d_skip,
+            conv_b_x, conv_w_bc, conv_b_bc, norm_w,
+        )
+    )
     rows = (places, steps * blocks, LANES)
     info, x_dense, gate, dec, dt_dense, wide, skip, wx, perm, place, kept_state, *convs = call(
         prep_kernel, "prep", [smem] + [anywhere] * 6 + [vmem] * 5, [smem] + [vmem] * 12,
@@ -720,8 +721,8 @@
             pltpu.SemaphoreType.DMA((5 + COPIES,)),
         ],
     )(
-        me_late, *in_hbm(counts, move_plan, x_in, z_in, conv_w_x, ssm_state), bc_in, dt_in,
-        dt_bias.reshape(1, -1), a_log.reshape(1, -1), d_skip.reshape(1, -1),
+        me_late, *in_hbm(counts, move_plan, x_in, z_in, conv_w_x, ssm_state), bc_late,
+        dt_late, bias_late.reshape(1, -1), rate_late.reshape(1, -1), skip_late.reshape(1, -1),
     )
 
     picked = call(
@@ -731,8 +732,8 @@
     got = exchange(picked)
 
     _, info = lax.optimization_barrier((picked[0], info))
-    common = [x_dense, bc_in, gate, dec, dt_dense, skip, wx]
-    common += [conv_b_x.reshape(blocks, LANES), conv_w_bc, conv_b_bc, perm, wide]
+    common = [x_dense, bc_late, gate, dec, dt_dense, skip, wx]
+    common += [bx_late.reshape(blocks, LANES), wb_late, bb_late, perm, wide]
     scratch = [pltpu.VMEM((steps * heads, LANES), f32)] * 2 + [pltpu.VMEM((LANES, LANES), f32)]
     held, kept_gated, kept_sums = call(
         kept_kernel, "kept", [smem] + [vmem] * (4 + len(common)), [anywhere, vmem, vmem],
@@ -743,7 +744,7 @@
             pltpu.VMEM((heads, columns), f32),
             pltpu.SemaphoreType.DMA((COPIES,)),
         ],
-    )(info, kept_state, conv_x_taps, conv_bc_state, *common, place)
+    )(info, kept_state, cx_late, cb_late, *common, place)
     moved_gated, sums, spread_rows, b_steps, wide_scaled = call(
         functools.partial(moved_kernel, masks), "moved",
         [smem] + [vmem] * (pieces + 1 + len(common)), [vmem] * 5,
@@ -755,24 +756,27 @@
         scratch + [pltpu.VMEM((max(aux_rows, pieces * AUX), LANES), f32)],
     )(info, *got, kept_sums, *common)
     theirs = lax.ppermute(sums, "tp", [(0, 1), (1, 0)])
-    new_ssm, ready = call(
+    new, ready = call(
         functools.partial(state_kernel, masks), "state",
-        [smem] + [vmem] * pieces + [anywhere] + [vmem] * 7, [anywhere, vmem],
-        [shaped(places, heads, columns), shaped(places, steps, channels)],
+        [smem] + [vmem] * (pieces + 7), [vmem] * 2,
+        [shaped(heads, columns), shaped(places, steps, channels)],
+        [pltpu.VMEM((steps * blocks, LANES), f32)],
+    )(
+        info, *got, spread_rows, b_steps, wide_scaled, place, kept_gated, moved_gated,
+        norm_late.reshape(blocks, LANES),
+    )
+    new_ssm, y_out = call(
+        norm_kernel, "norm", [smem, anywhere] + [vmem] * 4, [anywhere, anywhere],
         [
-            pltpu.VMEM((steps * blocks, LANES), f32),
-            pltpu.VMEM((heads, columns), f32),
-            pltpu.SemaphoreType.DMA((pieces,)),
+            shaped(places, heads, columns),
+            shaped(places, steps, channels, dtype=jnp.bfloat16),
         ],
-        input_output_aliases={1 + pieces: 0},
-    )(
-        info, *got, held, spread_rows, b_steps, wide_scaled, place, kept_gated, moved_gated,
-        norm_w.reshape(blocks, LANES),
-    )
-    y_out = call(
-        norm_kernel, "norm", [smem] + [vmem] * 3, vmem,
-        shaped(places, steps, channels, dtype=jnp.bfloat16),
-    )(info, ready, sums, theirs)
+        [
+            pltpu.VMEM((places, steps, channels), jnp.bfloat16),
+            pltpu.SemaphoreType.DMA((COPIES + 1,)),
+        ],
+        input_output_aliases={1: 0},
+    )(info, held, new, ready, sums, theirs)
     return (y_out, new_ssm, jnp.transpose(convs[0], (1, 0, 2)), convs[1])
 
 

time: 40.6 us -> 40.3 us (level)
  transfers between devices with their start and end apart: 15 -> 15, of which waited for: 4 -> 4; matrix products, arithmetic and copies ran while one was open for 0% -> 0% of each run, Pallas kernels for 20% -> 19%
where the time goes in v5:
time: 40.3 us; the launch traced here: 40.1 us
  starting transfers between devices  23.7 us (59%)
  Pallas kernels  13.2 us (33%)
  waiting for transfers between devices  2.25 us (6%)
  between operations  0.87 us (2%)
    ppermute x14, starting transfers between devices, exchange(): out[i] = lax.ppermute(values[i], 'req', [(o, o ^ k) for o in range(owners)])  23.7 us
    pallas_call x1, Pallas kernels, on_device(): call(prep_kernel, 'prep', [smem] + [anywhere] * 6 + [vmem] * 5, [smem] +...  3.29 us
    pallas_call x1, Pallas kernels, on_device(): call(kept_kernel, 'kept', [smem] + [vmem] * (4 + len(common)), [anywhere,...  2.94 us
    ppermute x14, waiting for transfers between devices, exchange(): out[i] = lax.ppermute(values[i], 'req', [(o, o ^ k) for o in range(owners)])  2.24 us
    pallas_call x1, Pallas kernels, on_device(): call(functools.partial(pack_kernel, masks), 'pack', [smem] + [anywhere] *...  1.86 us
    pallas_call x1, Pallas kernels, on_device(): call(norm_kernel, 'norm', [smem, anywhere] + [vmem] * 4, [anywhere, anywh...  1.6 us
    pallas_call x1, Pallas kernels, on_device(): call(functools.partial(moved_kernel, masks), 'moved', [smem] + [vmem] * (...  1.55 us
    pallas_call x1, Pallas kernels, on_device(): call(functools.partial(state_kernel, masks), 'state', [smem] + [vmem] * (...  1.35 us
  transfers between devices with their start and end apart: 15, of which 4 were waited for; matrix products, arithmetic and copies ran while one was open for 0% of the time, Pallas kernels for 19%

profile of v5, /device:TPU:0, one launch (start us, length us, event | category | flops | bytes accessed | tf_op | source)
XLA Modules:
  0.0 40.1 jit_solution(883901561308316386)
XLA Ops:
  0.7 1.9 %pack.1 = (s16[272,128]{1,0:T(8,128)(2,1)S(1)}, s16[272,128]{1,0:T(8,128)(2,1)S(1)}, s16[272,128]{1,0:T(8,128)(2,1)S(1)}, s16[272,128]{1,0:T(8,128)(2,1)S(1)}, s...) custom-call(s32[1]{0:T(128)} %bitcast.me_ref, ...), custom_call_target="tpu_custom_call" | custom-call | tf_op jit(solution)/shard_map/pack/pallas_call | solution.py:670
  2.6 5.1 %collective-permute-start = (s16[272,128]{1,0:T(8,128)(2,1)S(1)}, s16[272,128]{1,0:T(8,128)(2,1)S(1)}, u32[]{:S(2)}, u32[]{:S(2)}) collective-permute-start(s16[272,128]{1,0:T(8,128)(2,1)S(1)} %get-tuple-element.66), channel_id=1, source_target_pairs={{0,12},{2,14},{4,8},{6,10},{8,4},{10,6},{12,0},{14,2},{1,13},{3,15... | collective-permute-start | bytes 208904 | tf_op jit(solution)/shard_map/ppermute | solution.py:689
  7.7 1.5 %collective-permute-start.1 = (s16[272,128]{1,0:T(8,128)(2,1)S(1)}, s16[272,128]{1,0:T(8,128)(2,1)S(1)}, u32[]{:S(2)}, u32[]{:S(2)}) collective-permute-start(s16[272,128]{1,0:T(8,128)(2,1)S(1)} %get-tuple-element.67), channel_id=1, source_target_pairs={{0,2},{2,0},{4,6},{6,4},{8,10},{10,8},{12,14},{14,12},{1,3},{3,1},... | collective-permute-start | bytes 208904 | tf_op jit(solution)/shard_map/ppermute | solution.py:689
  9.2 0.0 collective-permute-start.2
  9.3 0.8 %collective-permute-start.3 = (s16[272,128]{1,0:T(8,128)(2,1)S(1)}, s16[272,128]{1,0:T(8,128)(2,1)S(1)}, u32[]{:S(2)}, u32[]{:S(2)}) collective-permute-start(s16[272,128]{1,0:T(8,128)(2,1)S(1)} %get-tuple-element.69), channel_id=1, source_target_pairs={{0,6},{2,4},{4,2},{6,0},{8,14},{10,12},{12,10},{14,8},{1,7},{3,5},... | collective-permute-start | bytes 208904 | tf_op jit(solution)/shard_map/ppermute | solution.py:689
  10.1 4.4 %collective-permute-start.4 = (s16[272,128]{1,0:T(8,128)(2,1)S(1)}, s16[272,128]{1,0:T(8,128)(2,1)S(1)}, u32[]{:S(2)}, u32[]{:S(2)}) collective-permute-start(s16[272,128]{1,0:T(8,128)(2,1)S(1)} %get-tuple-element.70), channel_id=1, source_target_pairs={{0,10},{2,8},{4,14},{6,12},{8,2},{10,0},{12,6},{14,4},{1,11},{3,9}... | collective-permute-start | bytes 208904 | tf_op jit(solution)/shard_map/ppermute | solution.py:689
  14.5 0.0 collective-permute-start.5
  14.5 0.6 %collective-permute-start.6 = (s16[272,128]{1,0:T(8,128)(2,1)S(1)}, s16[272,128]{1,0:T(8,128)(2,1)S(1)}, u32[]{:S(2)}, u32[]{:S(2)}) collective-permute-start(s16[272,128]{1,0:T(8,128)(2,1)S(1)} %get-tuple-element.72), channel_id=1, source_target_pairs={{0,8},{2,10},{4,12},{6,14},{8,0},{10,2},{12,4},{14,6},{1,9},{3,11}... | collective-permute-start | bytes 208904 | tf_op jit(solution)/shard_map/ppermute | solution.py:689
  15.1 3.3 %prep.1 = (s32[16]{0:T(128)S(1)}, f32[2,128,128]{2,1,0:T(8,128)S(1)}, f32[2,128,128]{2,1,0:T(8,128)S(1)}, f32[2,128,128]{2,1,0:T(8,128)S(1)}, f32[2,128,128]{2,1...) custom-call(s32[1]{0:T(128)} %bitcast.me_ref, ...), custom_call_target="tpu_custom_call" | custom-call | tf_op jit(solution)/shard_map/prep/pallas_call | solution.py:704
  18.5 0.6 %collective-permute-done.5.refs_6_ = s16[272,128]{1,0:T(8,128)(2,1)S(1)} collective-permute-done((s16[272,128]{1,0:T(8,128)(2,1)S(1)}, s16[272,128]{1,0:T(8,128)(2,1)S(1)}, u32[]{:S(2)}, u32[]{:S(2)}) %collective-permute-start.5) | collective-permute-done | bytes 69664 | tf_op jit(solution)/shard_map/ppermute | solution.py:689
  19.0 1.0 %collective-permute-done.6.refs_7_ = s16[272,128]{1,0:T(8,128)(2,1)S(1)} collective-permute-done((s16[272,128]{1,0:T(8,128)(2,1)S(1)}, s16[272,128]{1,0:T(8,128)(2,1)S(1)}, u32[]{:S(2)}, u32[]{:S(2)}) %collective-permute-start.6) | collective-permute-done | bytes 69664 | tf_op jit(solution)/shard_map/ppermute | solution.py:689
  20.0 0.6 %pick.1 = (s16[272,128]{1,0:T(8,128)(2,1)S(1)}, s16[272,128]{1,0:T(8,128)(2,1)S(1)}, s16[272,128]{1,0:T(8,128)(2,1)S(1)}, s16[272,128]{1,0:T(8,128)(2,1)S(1)}, s...) custom-call(s32[16]{0:T(128)S(1)} %get-tuple-element.74.info_ref, ...), custom_call_target="tpu_custom_call" | custom-call | tf_op jit(solution)/shard_map/pick/pallas_call | solution.py:728
  20.7 2.8 %collective-permute-start.7 = (s16[272,128]{1,0:T(8,128)(2,1)S(1)}, s16[272,128]{1,0:T(8,128)(2,1)S(1)}, u32[]{:S(2)}, u32[]{:S(2)}) collective-permute-start(s16[272,128]{1,0:T(8,128)(2,1)S(1)} %get-tuple-element.91), channel_id=1, source_target_pairs={{0,12},{2,14},{4,8},{6,10},{8,4},{10,6},{12,0},{14,2},{1,13},{3,15... | collective-permute-start | bytes 208904 | tf_op jit(solution)/shard_map/ppermute | solution.py:689
  23.5 1.4 %collective-permute-start.8 = (s16[272,128]{1,0:T(8,128)(2,1)S(1)}, s16[272,128]{1,0:T(8,128)(2,1)S(1)}, u32[]{:S(2)}, u32[]{:S(2)}) collective-permute-start(s16[272,128]{1,0:T(8,128)(2,1)S(1)} %get-tuple-element.92), channel_id=1, source_target_pairs={{0,2},{2,0},{4,6},{6,4},{8,10},{10,8},{12,14},{14,12},{1,3},{3,1},... | collective-permute-start | bytes 208904 | tf_op jit(solution)/shard_map/ppermute | solution.py:689
  24.9 1.2 %collective-permute-start.9 = (s16[272,128]{1,0:T(8,128)(2,1)S(1)}, s16[272,128]{1,0:T(8,128)(2,1)S(1)}, u32[]{:S(2)}, u32[]{:S(2)}) collective-permute-start(s16[272,128]{1,0:T(8,128)(2,1)S(1)} %get-tuple-element.93), channel_id=1, source_target_pairs={{0,14},{2,12},{4,10},{6,8},{8,6},{10,4},{12,2},{14,0},{1,15},{3,13... | collective-permute-start | bytes 208904 | tf_op jit(solution)/shard_map/ppermute | solution.py:689
  26.0 0.8 %collective-permute-start.10 = (s16[272,128]{1,0:T(8,128)(2,1)S(1)}, s16[272,128]{1,0:T(8,128)(2,1)S(1)}, u32[]{:S(2)}, u32[]{:S(2)}) collective-permute-start(s16[272,128]{1,0:T(8,128)(2,1)S(1)} %get-tuple-element.94), channel_id=1, source_target_pairs={{0,6},{2,4},{4,2},{6,0},{8,14},{10,12},{12,10},{14,8},{1,7},{3,5},... | collective-permute-start | bytes 208904 | tf_op jit(solution)/shard_map/ppermute | solution.py:689
  26.8 3.4 %collective-permute-start.11 = (s16[272,128]{1,0:T(8,128)(2,1)S(1)}, s16[272,128]{1,0:T(8,128)(2,1)S(1)}, u32[]{:S(2)}, u32[]{:S(2)}) collective-permute-start(s16[272,128]{1,0:T(8,128)(2,1)S(1)} %get-tuple-element.95), channel_id=1, source_target_pairs={{0,10},{2,8},{4,14},{6,12},{8,2},{10,0},{12,6},{14,4},{1,11},{3,9}... | collective-permute-start | bytes 208904 | tf_op jit(solution)/shard_map/ppermute | solution.py:689
  30.3 1.6 %collective-permute-start.13 = (s16[272,128]{1,0:T(8,128)(2,1)S(1)}, s16[272,128]{1,0:T(8,128)(2,1)S(1)}, u32[]{:S(2)}, u32[]{:S(2)}) collective-permute-start(s16[272,128]{1,0:T(8,128)(2,1)S(1)} %get-tuple-element.97), channel_id=1, source_target_pairs={{0,8},{2,10},{4,12},{6,14},{8,0},{10,2},{12,4},{14,6},{1,9},{3,11}... | collective-permute-start | bytes 208904 | tf_op jit(solution)/shard_map/ppermute | solution.py:689
  31.9 2.9 %kept.1 = (f32[2,64,4096]{2,1,0:T(8,128)}, f32[4,32,128]{2,1,0:T(8,128)S(1)}, f32[4,128]{1,0:T(4,128)S(1)}) custom-call(s32[16]{0:T(128)S(1)} %get-tuple-element.74.info_ref, f32[64,4096]{1,0:T(8,128)S(1)} %get-tuple-element.75.state_ref, bf16[3,2,4096]{2,1,0:T(2,128)(2,1)S(1)} %bitcast.9, bf16[2,3,2,128]{3,2,1,0:T(2,128)(2,1)S(1)} %copy-done.5, ...), custom_call_target="tpu_custom_call" | custom-call | tf_op jit(solution)/shard_map/kept/pallas_call | solution.py:738
  34.9 0.5 %collective-permute-done.11.refs_5_ = s16[272,128]{1,0:T(8,128)(2,1)S(1)} collective-permute-done((s16[272,128]{1,0:T(8,128)(2,1)S(1)}, s16[272,128]{1,0:T(8,128)(2,1)S(1)}, u32[]{:S(2)}, u32[]{:S(2)}) %collective-permute-start.11) | collective-permute-done | bytes 69664 | tf_op jit(solution)/shard_map/ppermute | solution.py:689
  35.3 0.2 collective-permute-done.13.refs_7_
  35.5 1.6 %moved.1 = (f32[4,32,128]{2,1,0:T(8,128)S(1)}, f32[8,128]{1,0:T(8,128)S(1)}, bf16[256,256]{1,0:T(8,128)(2,1)S(1)}, f32[4,2,128]{2,1,0:T(2,128)S(1)}, f32[64,128]{1,0:T(8,128)S(1)}) custom-call(s32[16]{0:T(128)S(1)} %get-tuple-element.74.info_ref, s16[272,128]{1,0:T(8,128)(2,1)S(1)} %get-tuple-element.73.refs_0_, ...), custom_call_target="tpu_custom_call" | custom-call | tf_op jit(solution)/shard_map/moved/pallas_call | solution.py:748
  37.1 1.4 %state.1 = (f32[64,4096]{1,0:T(8,128)S(1)}, f32[2,4,4096]{2,1,0:T(4,128)S(1)}) custom-call(s32[16]{0:T(128)S(1)} %get-tuple-element.74.info_ref, s16[272,128]{1,0:T(8,128)(2,1)S(1)} %get-tuple-element.73.refs_0_, s16[272,128]{1,0:T(8,128)(2,1)S(1)} %collective-permute-done.7.refs_1_, s16[272,128]{1,0:T(8,128)(2,1)S(1)} %collective-permute-done.8.refs_2_, ...), custom_call_target="tpu_custom_call" | custom-call | tf_op jit(solution)/shard_map/state/pallas_call | solution.py:759
  38.5 1.6 %norm.1 = (f32[2,64,4096]{2,1,0:T(8,128)}, bf16[2,4,4096]{2,1,0:T(4,128)(2,1)}) custom-call(s32[16]{0:T(128)S(1)} %get-tuple-element.74.info_ref, f32[2,64,4096]{2,1,0:T(8,128)} %get-tuple-element.90.held_hbm, f32[64,4096]{1,0:T(8,128)S(1)} %get-tuple-element.105.new_ref, ...), custom_call_target="tpu_custom_call", output_to_operand_aliasing={{0}: (1, {})} | custom-call | tf_op jit(solution)/shard_map/norm/pallas_call | solution.py:768
  (35 shorter events, 0.1 us)
Async XLA Ops:
  0.6 14.5 %copy-start.10 = (f32[64]{0:T(128)S(1)}, f32[64]{0:T(128)}, u32[]{:S(2)}) copy-start(f32[64]{0:T(128)} %param.32) | copy-start | bytes 772
  0.6 14.5 %copy-start.9 = (f32[64]{0:T(128)S(1)}, f32[64]{0:T(128)}, u32[]{:S(2)}) copy-start(f32[64]{0:T(128)} %param.31) | copy-start | bytes 772
  0.7 14.5 %copy-start.8 = (f32[64]{0:T(128)S(1)}, f32[64]{0:T(128)}, u32[]{:S(2)}) copy-start(f32[64]{0:T(128)} %param.30) | copy-start | bytes 772
  0.7 31.2 %copy-start = (bf16[2,3,4096]{2,0,1:T(2,128)(2,1)S(1)}, bf16[2,3,4096]{2,0,1:T(2,128)(2,1)}, u32[]{:S(2)}) copy-start(bf16[2,3,4096]{2,0,1:T(2,128)(2,1)} %param.20) | copy-start | bytes 147460
  0.7 31.2 %copy-start.1 = (f32[4096]{0:T(1024)S(1)}, f32[4096]{0:T(1024)}, u32[]{:S(2)}) copy-start(f32[4096]{0:T(1024)} %param.27) | copy-start | bytes 49156
  0.7 31.2 %copy-start.4 = (f32[4,2,128]{2,1,0:T(2,128)S(1)}, f32[4,2,128]{2,1,0:T(2,128)}, u32[]{:S(2)}) copy-start(f32[4,2,128]{2,1,0:T(2,128)} %refs_17_) | copy-start | bytes 12292
  0.7 31.2 %copy-start.5 = (bf16[2,3,2,128]{3,2,1,0:T(2,128)(2,1)S(1)}, bf16[2,3,2,128]{3,2,1,0:T(2,128)(2,1)}, u32[]{:S(2)}) copy-start(bf16[2,3,2,128]{3,2,1,0:T(2,128)(2,1)} %cb_ref) | copy-start | bytes 9220
  0.7 31.2 %copy-start.7 = (f32[2,128]{1,0:T(2,128)S(1)}, f32[2,128]{1,0:T(2,128)}, u32[]{:S(2)}) copy-start(f32[2,128]{1,0:T(2,128)} %refs_18_) | copy-start | bytes 3076
  2.6 11.9 %collective-permute-start = (s16[272,128]{1,0:T(8,128)(2,1)S(1)}, s16[272,128]{1,0:T(8,128)(2,1)S(1)}, u32[]{:S(2)}, u32[]{:S(2)}) collective-permute-start(s16[272,128]{1,0:T(8,128)(2,1)S(1)} %get-tuple-element.66), channel_id=1, source_target_pairs={{0,12},{2,14},{4,8},{6,10},{8,4},{10,6},{12,0},{14,2},{1,13},{3,15... | collective-permute-start | bytes 208904 | tf_op jit(solution)/shard_map/ppermute | solution.py:689
  7.7 6.8 %collective-permute-start.1 = (s16[272,128]{1,0:T(8,128)(2,1)S(1)}, s16[272,128]{1,0:T(8,128)(2,1)S(1)}, u32[]{:S(2)}, u32[]{:S(2)}) collective-permute-start(s16[272,128]{1,0:T(8,128)(2,1)S(1)} %get-tuple-element.67), channel_id=1, source_target_pairs={{0,2},{2,0},{4,6},{6,4},{8,10},{10,8},{12,14},{14,12},{1,3},{3,1},... | collective-permute-start | bytes 208904 | tf_op jit(solution)/shard_map/ppermute | solution.py:689
  9.2 9.2 %collective-permute-start.2 = (s16[272,128]{1,0:T(8,128)(2,1)S(1)}, s16[272,128]{1,0:T(8,128)(2,1)S(1)}, u32[]{:S(2)}, u32[]{:S(2)}) collective-permute-start(s16[272,128]{1,0:T(8,128)(2,1)S(1)} %get-tuple-element.68), channel_id=1, source_target_pairs={{0,14},{2,12},{4,10},{6,8},{8,6},{10,4},{12,2},{14,0},{1,15},{3,13... | collective-permute-start | bytes 208904 | tf_op jit(solution)/shard_map/ppermute | solution.py:689
  9.3 9.2 %collective-permute-start.3 = (s16[272,128]{1,0:T(8,128)(2,1)S(1)}, s16[272,128]{1,0:T(8,128)(2,1)S(1)}, u32[]{:S(2)}, u32[]{:S(2)}) collective-permute-start(s16[272,128]{1,0:T(8,128)(2,1)S(1)} %get-tuple-element.69), channel_id=1, source_target_pairs={{0,6},{2,4},{4,2},{6,0},{8,14},{10,12},{12,10},{14,8},{1,7},{3,5},... | collective-permute-start | bytes 208904 | tf_op jit(solution)/shard_map/ppermute | solution.py:689
  10.1 8.4 %collective-permute-start.4 = (s16[272,128]{1,0:T(8,128)(2,1)S(1)}, s16[272,128]{1,0:T(8,128)(2,1)S(1)}, u32[]{:S(2)}, u32[]{:S(2)}) collective-permute-start(s16[272,128]{1,0:T(8,128)(2,1)S(1)} %get-tuple-element.70), channel_id=1, source_target_pairs={{0,10},{2,8},{4,14},{6,12},{8,2},{10,0},{12,6},{14,4},{1,11},{3,9}... | collective-permute-start | bytes 208904 | tf_op jit(solution)/shard_map/ppermute | solution.py:689
  14.5 4.6 %collective-permute-start.5 = (s16[272,128]{1,0:T(8,128)(2,1)S(1)}, s16[272,128]{1,0:T(8,128)(2,1)S(1)}, u32[]{:S(2)}, u32[]{:S(2)}) collective-permute-start(s16[272,128]{1,0:T(8,128)(2,1)S(1)} %get-tuple-element.71), channel_id=1, source_target_pairs={{0,4},{2,6},{4,0},{6,2},{8,12},{10,14},{12,8},{14,10},{1,5},{3,7},... | collective-permute-start | bytes 208904 | tf_op jit(solution)/shard_map/ppermute | solution.py:689
  14.5 5.5 %collective-permute-start.6 = (s16[272,128]{1,0:T(8,128)(2,1)S(1)}, s16[272,128]{1,0:T(8,128)(2,1)S(1)}, u32[]{:S(2)}, u32[]{:S(2)}) collective-permute-start(s16[272,128]{1,0:T(8,128)(2,1)S(1)} %get-tuple-element.72), channel_id=1, source_target_pairs={{0,8},{2,10},{4,12},{6,14},{8,0},{10,2},{12,4},{14,6},{1,9},{3,11}... | collective-permute-start | bytes 208904 | tf_op jit(solution)/shard_map/ppermute | solution.py:689
  20.7 16.5 %copy-start.3 = (f32[4096]{0:T(1024)S(1)}, f32[4096]{0:T(1024)}, u32[]{:S(2)}) copy-start(f32[4096]{0:T(1024)} %param.33) | copy-start | bytes 49156
  20.7 9.6 %collective-permute-start.7 = (s16[272,128]{1,0:T(8,128)(2,1)S(1)}, s16[272,128]{1,0:T(8,128)(2,1)S(1)}, u32[]{:S(2)}, u32[]{:S(2)}) collective-permute-start(s16[272,128]{1,0:T(8,128)(2,1)S(1)} %get-tuple-element.91), channel_id=1, source_target_pairs={{0,12},{2,14},{4,8},{6,10},{8,4},{10,6},{12,0},{14,2},{1,13},{3,15... | collective-permute-start | bytes 208904 | tf_op jit(solution)/shard_map/ppermute | solution.py:689
  23.5 6.8 %collective-permute-start.8 = (s16[272,128]{1,0:T(8,128)(2,1)S(1)}, s16[272,128]{1,0:T(8,128)(2,1)S(1)}, u32[]{:S(2)}, u32[]{:S(2)}) collective-permute-start(s16[272,128]{1,0:T(8,128)(2,1)S(1)} %get-tuple-element.92), channel_id=1, source_target_pairs={{0,2},{2,0},{4,6},{6,4},{8,10},{10,8},{12,14},{14,12},{1,3},{3,1},... | collective-permute-start | bytes 208904 | tf_op jit(solution)/shard_map/ppermute | solution.py:689
  24.9 10.0 %collective-permute-start.9 = (s16[272,128]{1,0:T(8,128)(2,1)S(1)}, s16[272,128]{1,0:T(8,128)(2,1)S(1)}, u32[]{:S(2)}, u32[]{:S(2)}) collective-permute-start(s16[272,128]{1,0:T(8,128)(2,1)S(1)} %get-tuple-element.93), channel_id=1, source_target_pairs={{0,14},{2,12},{4,10},{6,8},{8,6},{10,4},{12,2},{14,0},{1,15},{3,13... | collective-permute-start | bytes 208904 | tf_op jit(solution)/shard_map/ppermute | solution.py:689
  26.0 8.8 %collective-permute-start.10 = (s16[272,128]{1,0:T(8,128)(2,1)S(1)}, s16[272,128]{1,0:T(8,128)(2,1)S(1)}, u32[]{:S(2)}, u32[]{:S(2)}) collective-permute-start(s16[272,128]{1,0:T(8,128)(2,1)S(1)} %get-tuple-element.94), channel_id=1, source_target_pairs={{0,6},{2,4},{4,2},{6,0},{8,14},{10,12},{12,10},{14,8},{1,7},{3,5},... | collective-permute-start | bytes 208904 | tf_op jit(solution)/shard_map/ppermute | solution.py:689
  26.8 8.5 %collective-permute-start.11 = (s16[272,128]{1,0:T(8,128)(2,1)S(1)}, s16[272,128]{1,0:T(8,128)(2,1)S(1)}, u32[]{:S(2)}, u32[]{:S(2)}) collective-permute-start(s16[272,128]{1,0:T(8,128)(2,1)S(1)} %get-tuple-element.95), channel_id=1, source_target_pairs={{0,10},{2,8},{4,14},{6,12},{8,2},{10,0},{12,6},{14,4},{1,11},{3,9}... | collective-permute-start | bytes 208904 | tf_op jit(solution)/shard_map/ppermute | solution.py:689
  30.3 5.1 %collective-permute-start.12 = (s16[272,128]{1,0:T(8,128)(2,1)S(1)}, s16[272,128]{1,0:T(8,128)(2,1)S(1)}, u32[]{:S(2)}, u32[]{:S(2)}) collective-permute-start(s16[272,128]{1,0:T(8,128)(2,1)S(1)} %get-tuple-element.96), channel_id=1, source_target_pairs={{0,4},{2,6},{4,0},{6,2},{8,12},{10,14},{12,8},{14,10},{1,5},{3,7},... | collective-permute-start | bytes 208904 | tf_op jit(solution)/shard_map/ppermute | solution.py:689
  30.3 5.3 %collective-permute-start.13 = (s16[272,128]{1,0:T(8,128)(2,1)S(1)}, s16[272,128]{1,0:T(8,128)(2,1)S(1)}, u32[]{:S(2)}, u32[]{:S(2)}) collective-permute-start(s16[272,128]{1,0:T(8,128)(2,1)S(1)} %get-tuple-element.97), channel_id=1, source_target_pairs={{0,8},{2,10},{4,12},{6,14},{8,0},{10,2},{12,4},{14,6},{1,9},{3,11}... | collective-permute-start | bytes 208904 | tf_op jit(solution)/shard_map/ppermute | solution.py:689
  37.1 1.4 %collective-permute-start.14 = (f32[8,128]{1,0:T(8,128)S(1)}, f32[8,128]{1,0:T(8,128)S(1)}, u32[]{:S(2)}, u32[]{:S(2)}) collective-permute-start(f32[8,128]{1,0:T(8,128)S(1)} %get-tuple-element.107.mine_ref), channel_id=1, source_target_pairs={{0,1},{1,0},{2,3},{3,2},{4,5},{5,4},{6,7},{7,6},{8,9},{9,8},{10,11... | collective-permute-start | bytes 12296 | tf_op jit(solution)/shard_map/ppermute | solution.py:758
  (2 other events, 28.9 us)

commit v6 on v5

--- a/solution.py
+++ b/solution.py
@@ -63,8 +63,8 @@
     return jnp.where(slot == 0, values[0], values[1])
 
 
-def pack_kernel(masks, me_ref, counts_hbm, plan_hbm, state_hbm, cx_hbm, cb_hbm, *refs):
-    *out_refs, counts_ref, plan_ref, state_ref, cx_ref, cb_ref, rows_ref, sems = refs
+def pack_kernel(masks, me_ref, counts_hbm, plan_hbm, state_hbm, cx_ref, cb_ref, *refs):
+    *out_refs, counts_ref, plan_ref, state_ref, rows_ref, sems = refs
     direct = len(out_refs) > 1
     slots, heads, columns = state_ref.shape
     owners = len(out_refs) if direct else out_refs[0].shape[0]
@@ -75,7 +75,7 @@
     small = [
         pltpu.make_async_copy(src, dst, sems.at[i])
         for i, (src, dst) in enumerate(
-            ((counts_hbm, counts_ref), (plan_hbm, plan_ref), (cx_hbm, cx_ref), (cb_hbm, cb_ref))
+            ((counts_hbm, counts_ref), (plan_hbm, plan_ref))
         )
     ]
     for copy in small:
@@ -92,8 +92,6 @@
     small[0].wait()
     small[1].wait()
     slot = moving_slot(counts_ref, plan_ref, me, slots)
-    small[2].wait()
-    small[3].wait()
     taps, _, channels = cx_ref.shape
     groups = cb_ref.shape[2]
     blocks = channels // LANES
@@ -316,11 +314,11 @@
 
 
 def prep_kernel(
-    me_ref, counts_hbm, plan_hbm, x_hbm, z_hbm, wx_hbm, state_hbm, bc_ref, dt_ref, bias_ref,
+    me_ref, counts_hbm, plan_hbm, wx_hbm, state_hbm, x_ref, z_ref, bc_ref, dt_ref, bias_ref,
     rate_ref, skip_ref,
     info_ref, xd_ref, gate_ref, dec_ref, dtd_ref, wide_ref, skipd_ref, wxd_ref, perm_ref,
     place_ref, kept_ref, cx_ref, cb_ref,
-    counts_ref, plan_ref, x_ref, z_ref, wx_ref, sems,
+    counts_ref, plan_ref, wx_ref, sems,
 ):
     slots, steps, channels = x_ref.shape
     heads = dt_ref.shape[2]
@@ -331,8 +329,7 @@
         pltpu.make_async_copy(src, dst, sems.at[i])
         for i, (src, dst) in enumerate(
             (
-                (counts_hbm, counts_ref), (plan_hbm, plan_ref), (x_hbm, x_ref), (z_hbm, z_ref),
-                (wx_hbm, wx_ref),
+                (counts_hbm, counts_ref), (plan_hbm, plan_ref), (wx_hbm, wx_ref),
             )
         )
     ]
@@ -417,7 +414,7 @@
         wide = jnp.sum(jnp.where(head == lane, total, 0.0), axis=1, keepdims=True)
         wide_ref[s] = jnp.broadcast_to(wide, (heads, LANES))
     skipd_ref[...] = out[2 * slots * run :]
-    for copy in copies[2:5]:
+    for copy in copies[2:3]:
         copy.wait()
     x = [x_ref[s].astype(jnp.float32) for s in range(slots)]
     for s in range(slots):
@@ -433,7 +430,7 @@
         for s in range(slots):
             pairs = bc_ref[s, t].astype(jnp.float32)
             cb_ref[s, k] = jnp.where(full[s], pairs, 0.0).astype(jnp.bfloat16)
-    for copy in copies[5:]:
+    for copy in copies[3:]:
         copy.wait()
 
 
@@ -582,7 +579,7 @@
 
 
 def norm_kernel(
-    info_ref, held_hbm, new_ref, ready_ref, mine_ref, theirs_ref, out_hbm, y_hbm, y_ref, sems
+    info_ref, held_hbm, new_ref, ready_ref, mine_ref, theirs_ref, out_hbm, y_ref, sems
 ):
     del held_hbm
     copies = copy_rows(new_ref, out_hbm.at[info_ref[3]], sems, 0, COPIES)
@@ -594,8 +591,6 @@
         for b in range(0, ready_ref.shape[2], LANES):
             values = jnp.where(full, ready_ref[which, :, b : b + LANES] * rows, 0.0)
             y_ref[info_ref[3 * which], :, b : b + LANES] = values.astype(jnp.bfloat16)
-    copies.append(pltpu.make_async_copy(y_ref, y_hbm, sems.at[COPIES]))
-    copies[-1].start()
     for copy in copies:
         copy.wait()
 
@@ -668,17 +663,15 @@
     piece = (share + AUX, LANES) if direct else (owners, share + AUX, LANES)
     sent = [shaped(*piece, dtype=jnp.int16)] * pieces
     payload = call(
-        functools.partial(pack_kernel, masks), "pack", [smem] + [anywhere] * 5, [vmem] * pieces, sent,
+        functools.partial(pack_kernel, masks), "pack", [smem] + [anywhere] * 3 + [vmem] * 2, [vmem] * pieces, sent,
         [
             pltpu.SMEM(counts.shape, jnp.int32),
             pltpu.SMEM(move_plan.shape, jnp.int32),
             pltpu.VMEM(ssm_state.shape, f32),
-            pltpu.VMEM(conv_x_taps.shape, jnp.bfloat16),
-            pltpu.VMEM(conv_bc_state.shape, jnp.bfloat16),
             pltpu.VMEM((max(aux_rows, pieces * AUX), LANES), f32),
-            pltpu.SemaphoreType.DMA((4 + slots * heads // BLOCK,)),
+            pltpu.SemaphoreType.DMA((2 + slots * heads // BLOCK,)),
         ],
-    )(me, *in_hbm(counts, move_plan, ssm_state, conv_x_taps, conv_bc_state))
+    )(me, *in_hbm(counts, move_plan, ssm_state), conv_x_taps, conv_bc_state)
 
     def exchange(values):
         if not direct:
@@ -693,16 +686,16 @@
 
     (
         _, me_late, cx_late, cb_late, bc_late, dt_late, bias_late, rate_late, skip_late,
-        bx_late, wb_late, bb_late, norm_late,
+        bx_late, wb_late, bb_late, norm_late, x_late, z_late,
     ) = lax.optimization_barrier(
         (
             payload[0], me, conv_x_taps, conv_bc_state, bc_in, dt_in, dt_bias, a_log, d_skip,
-            conv_b_x, conv_w_bc, conv_b_bc, norm_w,
+            conv_b_x, conv_w_bc, conv_b_bc, norm_w, x_in, z_in,
         )
     )
     rows = (places, steps * blocks, LANES)
     info, x_dense, gate, dec, dt_dense, wide, skip, wx, perm, place, kept_state, *convs = call(
-        prep_kernel, "prep", [smem] + [anywhere] * 6 + [vmem] * 5, [smem] + [vmem] * 12,
+        prep_kernel, "prep", [smem] + [anywhere] * 4 + [vmem] * 7, [smem] + [vmem] * 12,
         [
             shaped(INFO + owners, dtype=jnp.int32), shaped(*rows), shaped(*rows), shaped(*rows),
             shaped(*rows), shaped(places, heads, LANES), shaped(blocks, LANES),
@@ -715,13 +708,11 @@
         [
             pltpu.SMEM(counts.shape, jnp.int32),
             pltpu.SMEM(move_plan.shape, jnp.int32),
-            pltpu.VMEM(x_in.shape, jnp.bfloat16),
-            pltpu.VMEM(z_in.shape, jnp.bfloat16),
             pltpu.VMEM(conv_w_x.shape, f32),
-            pltpu.SemaphoreType.DMA((5 + COPIES,)),
+            pltpu.SemaphoreType.DMA((3 + COPIES,)),
         ],
     )(
-        me_late, *in_hbm(counts, move_plan, x_in, z_in, conv_w_x, ssm_state), bc_late,
+        me_late, *in_hbm(counts, move_plan, conv_w_x, ssm_state), x_late, z_late, bc_late,
         dt_late, bias_late.reshape(1, -1), rate_late.reshape(1, -1), skip_late.reshape(1, -1),
     )
 
@@ -766,15 +757,12 @@
         norm_late.reshape(blocks, LANES),
     )
     new_ssm, y_out = call(
-        norm_kernel, "norm", [smem, anywhere] + [vmem] * 4, [anywhere, anywhere],
+        norm_kernel, "norm", [smem, anywhere] + [vmem] * 4, [anywhere, vmem],
         [
             shaped(places, heads, columns),
             shaped(places, steps, channels, dtype=jnp.bfloat16),
         ],
-        [
-            pltpu.VMEM((places, steps, channels), jnp.bfloat16),
-            pltpu.SemaphoreType.DMA((COPIES + 1,)),
-        ],
+        [pltpu.SemaphoreType.DMA((COPIES,))],
         input_output_aliases={1: 0},
     )(info, held, new, ready, sums, theirs)
     return (y_out, new_ssm, jnp.transpose(convs[0], (1, 0, 2)), convs[1])

time: 40.3 us -> 42.5 us (1.055)
  local copies, waits for them, and re-layouts: 0.05 us -> 1.55 us
  Pallas kernels: 13.2 us -> 13.8 us
    unnamed x22 -> x30, local copies, waits for them, and re-layouts: 0.05 us -> 1.55 us
    pallas_call x2, Pallas kernels: 4.89 us -> 5.47 us  [the longest x1 3.27 us: on_device(): call(prep_kernel, 'prep', [smem] + [anywhere] * 4 + [vmem] * 7, [smem] +...]
  transfers between devices with their start and end apart: 15 -> 15, of which waited for: 4 -> 4; matrix products, arithmetic and copies ran while one was open for 0% -> 0% of each run, Pallas kernels for 19% -> 18%
where the time goes in v6:
time: 42.5 us; the launch traced here: 42.2 us
  starting transfers between devices  23.7 us (56%)
  Pallas kernels  13.8 us (32%)
  waiting for transfers between devices  2.25 us (5%)
  local copies, waits for them, and re-layouts  1.55 us (4%)
  between operations  0.88 us (2%)
    ppermute x14, starting transfers between devices, exchange(): out[i] = lax.ppermute(values[i], 'req', [(o, o ^ k) for o in range(owners)])  23.7 us
    pallas_call x1, Pallas kernels, on_device(): call(prep_kernel, 'prep', [smem] + [anywhere] * 4 + [vmem] * 7, [smem] +...  3.27 us
    pallas_call x1, Pallas kernels, on_device(): call(kept_kernel, 'kept', [smem] + [vmem] * (4 + len(common)), [anywhere,...  2.95 us
    ppermute x14, waiting for transfers between devices, exchange(): out[i] = lax.ppermute(values[i], 'req', [(o, o ^ k) for o in range(owners)])  2.24 us
    pallas_call x1, Pallas kernels, on_device(): call(norm_kernel, 'norm', [smem, anywhere] + [vmem] * 4, [anywhere, vmem]...  2.2 us
    pallas_call x1, Pallas kernels, on_device(): call(functools.partial(pack_kernel, masks), 'pack', [smem] + [anywhere] *...  1.84 us
    pallas_call x1, Pallas kernels, on_device(): call(functools.partial(moved_kernel, masks), 'moved', [smem] + [vmem] * (...  1.56 us
    unnamed x30, local copies, waits for them, and re-layouts  1.55 us
  transfers between devices with their start and end apart: 15, of which 4 were waited for; matrix products, arithmetic and copies ran while one was open for 0% of the time, Pallas kernels for 18%

profile of v6, /device:TPU:0, one launch (start us, length us, event | category | flops | bytes accessed | tf_op | source)
XLA Modules:
  0.0 42.2 jit_solution(1325812385058440010)
XLA Ops:
  0.7 0.8 %copy-done = bf16[2,3,4096]{2,0,1:T(2,128)(2,1)S(1)} copy-done((bf16[2,3,4096]{2,0,1:T(2,128)(2,1)S(1)}, bf16[2,3,4096]{2,0,1:T(2,128)(2,1)}, u32[]{:S(2)}) %copy-start) | copy-done | bytes 49176
  1.5 0.7 %copy-done.8 = bf16[2,3,2,128]{3,2,1,0:T(2,128)(2,1)S(1)} copy-done((bf16[2,3,2,128]{3,2,1,0:T(2,128)(2,1)S(1)}, bf16[2,3,2,128]{3,2,1,0:T(2,128)(2,1)}, u32[]{:S(2)}) %copy-start.8) | copy-done | bytes 3096
  2.2 1.8 %pack.1 = (s16[272,128]{1,0:T(8,128)(2,1)S(1)}, s16[272,128]{1,0:T(8,128)(2,1)S(1)}, s16[272,128]{1,0:T(8,128)(2,1)S(1)}, s16[272,128]{1,0:T(8,128)(2,1)S(1)}, s...) custom-call(s32[1]{0:T(128)} %bitcast.me_ref, ...), custom_call_target="tpu_custom_call" | custom-call | tf_op jit(solution)/shard_map/pack/pallas_call | solution.py:665
  4.1 5.1 %collective-permute-start = (s16[272,128]{1,0:T(8,128)(2,1)S(1)}, s16[272,128]{1,0:T(8,128)(2,1)S(1)}, u32[]{:S(2)}, u32[]{:S(2)}) collective-permute-start(s16[272,128]{1,0:T(8,128)(2,1)S(1)} %get-tuple-element.70), channel_id=1, source_target_pairs={{0,12},{2,14},{4,8},{6,10},{8,4},{10,6},{12,0},{14,2},{1,13},{3,15... | collective-permute-start | bytes 208904 | tf_op jit(solution)/shard_map/ppermute | solution.py:682
  9.2 1.5 %collective-permute-start.1 = (s16[272,128]{1,0:T(8,128)(2,1)S(1)}, s16[272,128]{1,0:T(8,128)(2,1)S(1)}, u32[]{:S(2)}, u32[]{:S(2)}) collective-permute-start(s16[272,128]{1,0:T(8,128)(2,1)S(1)} %get-tuple-element.71), channel_id=1, source_target_pairs={{0,2},{2,0},{4,6},{6,4},{8,10},{10,8},{12,14},{14,12},{1,3},{3,1},... | collective-permute-start | bytes 208904 | tf_op jit(solution)/shard_map/ppermute | solution.py:682
  10.7 0.8 %collective-permute-start.3 = (s16[272,128]{1,0:T(8,128)(2,1)S(1)}, s16[272,128]{1,0:T(8,128)(2,1)S(1)}, u32[]{:S(2)}, u32[]{:S(2)}) collective-permute-start(s16[272,128]{1,0:T(8,128)(2,1)S(1)} %get-tuple-element.73), channel_id=1, source_target_pairs={{0,6},{2,4},{4,2},{6,0},{8,14},{10,12},{12,10},{14,8},{1,7},{3,5},... | collective-permute-start | bytes 208904 | tf_op jit(solution)/shard_map/ppermute | solution.py:682
  11.6 4.4 %collective-permute-start.4 = (s16[272,128]{1,0:T(8,128)(2,1)S(1)}, s16[272,128]{1,0:T(8,128)(2,1)S(1)}, u32[]{:S(2)}, u32[]{:S(2)}) collective-permute-start(s16[272,128]{1,0:T(8,128)(2,1)S(1)} %get-tuple-element.74), channel_id=1, source_target_pairs={{0,10},{2,8},{4,14},{6,12},{8,2},{10,0},{12,6},{14,4},{1,11},{3,9}... | collective-permute-start | bytes 208904 | tf_op jit(solution)/shard_map/ppermute | solution.py:682
  16.0 0.6 %collective-permute-start.6 = (s16[272,128]{1,0:T(8,128)(2,1)S(1)}, s16[272,128]{1,0:T(8,128)(2,1)S(1)}, u32[]{:S(2)}, u32[]{:S(2)}) collective-permute-start(s16[272,128]{1,0:T(8,128)(2,1)S(1)} %get-tuple-element.76), channel_id=1, source_target_pairs={{0,8},{2,10},{4,12},{6,14},{8,0},{10,2},{12,4},{14,6},{1,9},{3,11}... | collective-permute-start | bytes 208904 | tf_op jit(solution)/shard_map/ppermute | solution.py:682
  16.7 3.3 %prep.1 = (s32[16]{0:T(128)S(1)}, f32[2,128,128]{2,1,0:T(8,128)S(1)}, f32[2,128,128]{2,1,0:T(8,128)S(1)}, f32[2,128,128]{2,1,0:T(8,128)S(1)}, f32[2,128,128]{2,1...) custom-call(s32[1]{0:T(128)} %bitcast.me_ref, ...), custom_call_target="tpu_custom_call" | custom-call | tf_op jit(solution)/shard_map/prep/pallas_call | solution.py:697
  20.0 0.6 %collective-permute-done.5.refs_6_ = s16[272,128]{1,0:T(8,128)(2,1)S(1)} collective-permute-done((s16[272,128]{1,0:T(8,128)(2,1)S(1)}, s16[272,128]{1,0:T(8,128)(2,1)S(1)}, u32[]{:S(2)}, u32[]{:S(2)}) %collective-permute-start.5) | collective-permute-done | bytes 69664 | tf_op jit(solution)/shard_map/ppermute | solution.py:682
  20.5 1.0 %collective-permute-done.6.refs_7_ = s16[272,128]{1,0:T(8,128)(2,1)S(1)} collective-permute-done((s16[272,128]{1,0:T(8,128)(2,1)S(1)}, s16[272,128]{1,0:T(8,128)(2,1)S(1)}, u32[]{:S(2)}, u32[]{:S(2)}) %collective-permute-start.6) | collective-permute-done | bytes 69664 | tf_op jit(solution)/shard_map/ppermute | solution.py:682
  21.5 0.6 %pick.1 = (s16[272,128]{1,0:T(8,128)(2,1)S(1)}, s16[272,128]{1,0:T(8,128)(2,1)S(1)}, s16[272,128]{1,0:T(8,128)(2,1)S(1)}, s16[272,128]{1,0:T(8,128)(2,1)S(1)}, s...) custom-call(s32[16]{0:T(128)S(1)} %get-tuple-element.78.info_ref, ...), custom_call_target="tpu_custom_call" | custom-call | tf_op jit(solution)/shard_map/pick/pallas_call | solution.py:719
  22.2 2.8 %collective-permute-start.7 = (s16[272,128]{1,0:T(8,128)(2,1)S(1)}, s16[272,128]{1,0:T(8,128)(2,1)S(1)}, u32[]{:S(2)}, u32[]{:S(2)}) collective-permute-start(s16[272,128]{1,0:T(8,128)(2,1)S(1)} %get-tuple-element.95), channel_id=1, source_target_pairs={{0,12},{2,14},{4,8},{6,10},{8,4},{10,6},{12,0},{14,2},{1,13},{3,15... | collective-permute-start | bytes 208904 | tf_op jit(solution)/shard_map/ppermute | solution.py:682
  25.0 1.4 %collective-permute-start.8 = (s16[272,128]{1,0:T(8,128)(2,1)S(1)}, s16[272,128]{1,0:T(8,128)(2,1)S(1)}, u32[]{:S(2)}, u32[]{:S(2)}) collective-permute-start(s16[272,128]{1,0:T(8,128)(2,1)S(1)} %get-tuple-element.96), channel_id=1, source_target_pairs={{0,2},{2,0},{4,6},{6,4},{8,10},{10,8},{12,14},{14,12},{1,3},{3,1},... | collective-permute-start | bytes 208904 | tf_op jit(solution)/shard_map/ppermute | solution.py:682
  26.3 1.2 %collective-permute-start.9 = (s16[272,128]{1,0:T(8,128)(2,1)S(1)}, s16[272,128]{1,0:T(8,128)(2,1)S(1)}, u32[]{:S(2)}, u32[]{:S(2)}) collective-permute-start(s16[272,128]{1,0:T(8,128)(2,1)S(1)} %get-tuple-element.97), channel_id=1, source_target_pairs={{0,14},{2,12},{4,10},{6,8},{8,6},{10,4},{12,2},{14,0},{1,15},{3,13... | collective-permute-start | bytes 208904 | tf_op jit(solution)/shard_map/ppermute | solution.py:682
  27.5 0.8 %collective-permute-start.10 = (s16[272,128]{1,0:T(8,128)(2,1)S(1)}, s16[272,128]{1,0:T(8,128)(2,1)S(1)}, u32[]{:S(2)}, u32[]{:S(2)}) collective-permute-start(s16[272,128]{1,0:T(8,128)(2,1)S(1)} %get-tuple-element.98), channel_id=1, source_target_pairs={{0,6},{2,4},{4,2},{6,0},{8,14},{10,12},{12,10},{14,8},{1,7},{3,5},... | collective-permute-start | bytes 208904 | tf_op jit(solution)/shard_map/ppermute | solution.py:682
  28.3 3.4 %collective-permute-start.11 = (s16[272,128]{1,0:T(8,128)(2,1)S(1)}, s16[272,128]{1,0:T(8,128)(2,1)S(1)}, u32[]{:S(2)}, u32[]{:S(2)}) collective-permute-start(s16[272,128]{1,0:T(8,128)(2,1)S(1)} %get-tuple-element.99), channel_id=1, source_target_pairs={{0,10},{2,8},{4,14},{6,12},{8,2},{10,0},{12,6},{14,4},{1,11},{3,9}... | collective-permute-start | bytes 208904 | tf_op jit(solution)/shard_map/ppermute | solution.py:682
  31.8 1.6 %collective-permute-start.13 = (s16[272,128]{1,0:T(8,128)(2,1)S(1)}, s16[272,128]{1,0:T(8,128)(2,1)S(1)}, u32[]{:S(2)}, u32[]{:S(2)}) collective-permute-start(s16[272,128]{1,0:T(8,128)(2,1)S(1)} %get-tuple-element.101), channel_id=1, source_target_pairs={{0,8},{2,10},{4,12},{6,14},{8,0},{10,2},{12,4},{14,6},{1,9},{3,11}... | collective-permute-start | bytes 208904 | tf_op jit(solution)/shard_map/ppermute | solution.py:682
  33.4 2.9 %kept.1 = (f32[2,64,4096]{2,1,0:T(8,128)}, f32[4,32,128]{2,1,0:T(8,128)S(1)}, f32[4,128]{1,0:T(4,128)S(1)}) custom-call(s32[16]{0:T(128)S(1)} %get-tuple-element.78.info_ref, f32[64,4096]{1,0:T(8,128)S(1)} %get-tuple-element.79.state_ref, bf16[3,2,4096]{2,1,0:T(2,128)(2,1)S(1)} %bitcast.9, bf16[2,3,2,128]{3,2,1,0:T(2,128)(2,1)S(1)} %copy-done.9, ...), custom_call_target="tpu_custom_call" | custom-call | tf_op jit(solution)/shard_map/kept/pallas_call | solution.py:729
  36.4 0.5 %collective-permute-done.11.refs_5_ = s16[272,128]{1,0:T(8,128)(2,1)S(1)} collective-permute-done((s16[272,128]{1,0:T(8,128)(2,1)S(1)}, s16[272,128]{1,0:T(8,128)(2,1)S(1)}, u32[]{:S(2)}, u32[]{:S(2)}) %collective-permute-start.11) | collective-permute-done | bytes 69664 | tf_op jit(solution)/shard_map/ppermute | solution.py:682
  36.8 0.2 collective-permute-done.13.refs_7_
  37.0 1.6 %moved.1 = (f32[4,32,128]{2,1,0:T(8,128)S(1)}, f32[8,128]{1,0:T(8,128)S(1)}, bf16[256,256]{1,0:T(8,128)(2,1)S(1)}, f32[4,2,128]{2,1,0:T(2,128)S(1)}, f32[64,128]{1,0:T(8,128)S(1)}) custom-call(s32[16]{0:T(128)S(1)} %get-tuple-element.78.info_ref, s16[272,128]{1,0:T(8,128)(2,1)S(1)} %get-tuple-element.77.refs_0_, ...), custom_call_target="tpu_custom_call" | custom-call | tf_op jit(solution)/shard_map/moved/pallas_call | solution.py:739
  38.6 1.3 %state.1 = (f32[64,4096]{1,0:T(8,128)S(1)}, f32[2,4,4096]{2,1,0:T(4,128)S(1)}) custom-call(s32[16]{0:T(128)S(1)} %get-tuple-element.78.info_ref, s16[272,128]{1,0:T(8,128)(2,1)S(1)} %get-tuple-element.77.refs_0_, s16[272,128]{1,0:T(8,128)(2,1)S(1)} %collective-permute-done.7.refs_1_, s16[272,128]{1,0:T(8,128)(2,1)S(1)} %collective-permute-done.8.refs_2_, ...), custom_call_target="tpu_custom_call" | custom-call | tf_op jit(solution)/shard_map/state/pallas_call | solution.py:750
  40.0 2.2 %norm.1 = (f32[2,64,4096]{2,1,0:T(8,128)}, bf16[2,4,4096]{2,1,0:T(4,128)(2,1)}) custom-call(s32[16]{0:T(128)S(1)} %get-tuple-element.78.info_ref, f32[2,64,4096]{2,1,0:T(8,128)} %get-tuple-element.94.held_hbm, f32[64,4096]{1,0:T(8,128)S(1)} %get-tuple-element.109.new_ref, ...), custom_call_target="tpu_custom_call", output_to_operand_aliasing={{0}: (1, {})} | custom-call | tf_op jit(solution)/shard_map/norm/pallas_call | solution.py:759
  (43 shorter events, 0.2 us)
Async XLA Ops:
  0.6 16.0 %copy-start.14 = (f32[64]{0:T(128)S(1)}, f32[64]{0:T(128)}, u32[]{:S(2)}) copy-start(f32[64]{0:T(128)} %param.32) | copy-start | bytes 772
  0.6 16.0 %copy-start.13 = (f32[64]{0:T(128)S(1)}, f32[64]{0:T(128)}, u32[]{:S(2)}) copy-start(f32[64]{0:T(128)} %param.31) | copy-start | bytes 772
  0.7 16.0 %copy-start.12 = (f32[64]{0:T(128)S(1)}, f32[64]{0:T(128)}, u32[]{:S(2)}) copy-start(f32[64]{0:T(128)} %param.30) | copy-start | bytes 772
  2.2 31.2 %copy-start.1 = (bf16[2,3,4096]{2,0,1:T(2,128)(2,1)S(1)}, bf16[2,3,4096]{2,0,1:T(2,128)(2,1)}, u32[]{:S(2)}) copy-start(bf16[2,3,4096]{2,0,1:T(2,128)(2,1)} %param.20) | copy-start | bytes 147460
  2.2 31.2 %copy-start.2 = (f32[4096]{0:T(1024)S(1)}, f32[4096]{0:T(1024)}, u32[]{:S(2)}) copy-start(f32[4096]{0:T(1024)} %param.27) | copy-start | bytes 49156
  2.2 31.2 %copy-start.7 = (f32[4,2,128]{2,1,0:T(2,128)S(1)}, f32[4,2,128]{2,1,0:T(2,128)}, u32[]{:S(2)}) copy-start(f32[4,2,128]{2,1,0:T(2,128)} %refs_17_) | copy-start | bytes 12292
  2.2 31.2 %copy-start.9 = (bf16[2,3,2,128]{3,2,1,0:T(2,128)(2,1)S(1)}, bf16[2,3,2,128]{3,2,1,0:T(2,128)(2,1)}, u32[]{:S(2)}) copy-start(bf16[2,3,2,128]{3,2,1,0:T(2,128)(2,1)} %cb_ref.2) | copy-start | bytes 9220
  2.2 31.2 %copy-start.11 = (f32[2,128]{1,0:T(2,128)S(1)}, f32[2,128]{1,0:T(2,128)}, u32[]{:S(2)}) copy-start(f32[2,128]{1,0:T(2,128)} %refs_18_) | copy-start | bytes 3076
  4.1 11.9 %collective-permute-start = (s16[272,128]{1,0:T(8,128)(2,1)S(1)}, s16[272,128]{1,0:T(8,128)(2,1)S(1)}, u32[]{:S(2)}, u32[]{:S(2)}) collective-permute-start(s16[272,128]{1,0:T(8,128)(2,1)S(1)} %get-tuple-element.70), channel_id=1, source_target_pairs={{0,12},{2,14},{4,8},{6,10},{8,4},{10,6},{12,0},{14,2},{1,13},{3,15... | collective-permute-start | bytes 208904 | tf_op jit(solution)/shard_map/ppermute | solution.py:682
  9.2 6.8 %collective-permute-start.1 = (s16[272,128]{1,0:T(8,128)(2,1)S(1)}, s16[272,128]{1,0:T(8,128)(2,1)S(1)}, u32[]{:S(2)}, u32[]{:S(2)}) collective-permute-start(s16[272,128]{1,0:T(8,128)(2,1)S(1)} %get-tuple-element.71), channel_id=1, source_target_pairs={{0,2},{2,0},{4,6},{6,4},{8,10},{10,8},{12,14},{14,12},{1,3},{3,1},... | collective-permute-start | bytes 208904 | tf_op jit(solution)/shard_map/ppermute | solution.py:682
  10.7 9.2 %collective-permute-start.2 = (s16[272,128]{1,0:T(8,128)(2,1)S(1)}, s16[272,128]{1,0:T(8,128)(2,1)S(1)}, u32[]{:S(2)}, u32[]{:S(2)}) collective-permute-start(s16[272,128]{1,0:T(8,128)(2,1)S(1)} %get-tuple-element.72), channel_id=1, source_target_pairs={{0,14},{2,12},{4,10},{6,8},{8,6},{10,4},{12,2},{14,0},{1,15},{3,13... | collective-permute-start | bytes 208904 | tf_op jit(solution)/shard_map/ppermute | solution.py:682
  10.7 9.2 %collective-permute-start.3 = (s16[272,128]{1,0:T(8,128)(2,1)S(1)}, s16[272,128]{1,0:T(8,128)(2,1)S(1)}, u32[]{:S(2)}, u32[]{:S(2)}) collective-permute-start(s16[272,128]{1,0:T(8,128)(2,1)S(1)} %get-tuple-element.73), channel_id=1, source_target_pairs={{0,6},{2,4},{4,2},{6,0},{8,14},{10,12},{12,10},{14,8},{1,7},{3,5},... | collective-permute-start | bytes 208904 | tf_op jit(solution)/shard_map/ppermute | solution.py:682
  11.6 8.3 %collective-permute-start.4 = (s16[272,128]{1,0:T(8,128)(2,1)S(1)}, s16[272,128]{1,0:T(8,128)(2,1)S(1)}, u32[]{:S(2)}, u32[]{:S(2)}) collective-permute-start(s16[272,128]{1,0:T(8,128)(2,1)S(1)} %get-tuple-element.74), channel_id=1, source_target_pairs={{0,10},{2,8},{4,14},{6,12},{8,2},{10,0},{12,6},{14,4},{1,11},{3,9}... | collective-permute-start | bytes 208904 | tf_op jit(solution)/shard_map/ppermute | solution.py:682
  16.0 4.6 %collective-permute-start.5 = (s16[272,128]{1,0:T(8,128)(2,1)S(1)}, s16[272,128]{1,0:T(8,128)(2,1)S(1)}, u32[]{:S(2)}, u32[]{:S(2)}) collective-permute-start(s16[272,128]{1,0:T(8,128)(2,1)S(1)} %get-tuple-element.75), channel_id=1, source_target_pairs={{0,4},{2,6},{4,0},{6,2},{8,12},{10,14},{12,8},{14,10},{1,5},{3,7},... | collective-permute-start | bytes 208904 | tf_op jit(solution)/shard_map/ppermute | solution.py:682
  16.0 5.5 %collective-permute-start.6 = (s16[272,128]{1,0:T(8,128)(2,1)S(1)}, s16[272,128]{1,0:T(8,128)(2,1)S(1)}, u32[]{:S(2)}, u32[]{:S(2)}) collective-permute-start(s16[272,128]{1,0:T(8,128)(2,1)S(1)} %get-tuple-element.76), channel_id=1, source_target_pairs={{0,8},{2,10},{4,12},{6,14},{8,0},{10,2},{12,4},{14,6},{1,9},{3,11}... | collective-permute-start | bytes 208904 | tf_op jit(solution)/shard_map/ppermute | solution.py:682
  22.1 16.5 %copy-start.6 = (f32[4096]{0:T(1024)S(1)}, f32[4096]{0:T(1024)}, u32[]{:S(2)}) copy-start(f32[4096]{0:T(1024)} %param.33) | copy-start | bytes 49156
  22.2 9.6 %collective-permute-start.7 = (s16[272,128]{1,0:T(8,128)(2,1)S(1)}, s16[272,128]{1,0:T(8,128)(2,1)S(1)}, u32[]{:S(2)}, u32[]{:S(2)}) collective-permute-start(s16[272,128]{1,0:T(8,128)(2,1)S(1)} %get-tuple-element.95), channel_id=1, source_target_pairs={{0,12},{2,14},{4,8},{6,10},{8,4},{10,6},{12,0},{14,2},{1,13},{3,15... | collective-permute-start | bytes 208904 | tf_op jit(solution)/shard_map/ppermute | solution.py:682
  25.0 6.8 %collective-permute-start.8 = (s16[272,128]{1,0:T(8,128)(2,1)S(1)}, s16[272,128]{1,0:T(8,128)(2,1)S(1)}, u32[]{:S(2)}, u32[]{:S(2)}) collective-permute-start(s16[272,128]{1,0:T(8,128)(2,1)S(1)} %get-tuple-element.96), channel_id=1, source_target_pairs={{0,2},{2,0},{4,6},{6,4},{8,10},{10,8},{12,14},{14,12},{1,3},{3,1},... | collective-permute-start | bytes 208904 | tf_op jit(solution)/shard_map/ppermute | solution.py:682
  26.3 10.0 %collective-permute-start.9 = (s16[272,128]{1,0:T(8,128)(2,1)S(1)}, s16[272,128]{1,0:T(8,128)(2,1)S(1)}, u32[]{:S(2)}, u32[]{:S(2)}) collective-permute-start(s16[272,128]{1,0:T(8,128)(2,1)S(1)} %get-tuple-element.97), channel_id=1, source_target_pairs={{0,14},{2,12},{4,10},{6,8},{8,6},{10,4},{12,2},{14,0},{1,15},{3,13... | collective-permute-start | bytes 208904 | tf_op jit(solution)/shard_map/ppermute | solution.py:682
  27.5 8.8 %collective-permute-start.10 = (s16[272,128]{1,0:T(8,128)(2,1)S(1)}, s16[272,128]{1,0:T(8,128)(2,1)S(1)}, u32[]{:S(2)}, u32[]{:S(2)}) collective-permute-start(s16[272,128]{1,0:T(8,128)(2,1)S(1)} %get-tuple-element.98), channel_id=1, source_target_pairs={{0,6},{2,4},{4,2},{6,0},{8,14},{10,12},{12,10},{14,8},{1,7},{3,5},... | collective-permute-start | bytes 208904 | tf_op jit(solution)/shard_map/ppermute | solution.py:682
  28.3 8.5 %collective-permute-start.11 = (s16[272,128]{1,0:T(8,128)(2,1)S(1)}, s16[272,128]{1,0:T(8,128)(2,1)S(1)}, u32[]{:S(2)}, u32[]{:S(2)}) collective-permute-start(s16[272,128]{1,0:T(8,128)(2,1)S(1)} %get-tuple-element.99), channel_id=1, source_target_pairs={{0,10},{2,8},{4,14},{6,12},{8,2},{10,0},{12,6},{14,4},{1,11},{3,9}... | collective-permute-start | bytes 208904 | tf_op jit(solution)/shard_map/ppermute | solution.py:682
  31.7 5.1 %collective-permute-start.12 = (s16[272,128]{1,0:T(8,128)(2,1)S(1)}, s16[272,128]{1,0:T(8,128)(2,1)S(1)}, u32[]{:S(2)}, u32[]{:S(2)}) collective-permute-start(s16[272,128]{1,0:T(8,128)(2,1)S(1)} %get-tuple-element.100), channel_id=1, source_target_pairs={{0,4},{2,6},{4,0},{6,2},{8,12},{10,14},{12,8},{14,10},{1,5},{3,7},... | collective-permute-start | bytes 208904 | tf_op jit(solution)/shard_map/ppermute | solution.py:682
  31.8 5.3 %collective-permute-start.13 = (s16[272,128]{1,0:T(8,128)(2,1)S(1)}, s16[272,128]{1,0:T(8,128)(2,1)S(1)}, u32[]{:S(2)}, u32[]{:S(2)}) collective-permute-start(s16[272,128]{1,0:T(8,128)(2,1)S(1)} %get-tuple-element.101), channel_id=1, source_target_pairs={{0,8},{2,10},{4,12},{6,14},{8,0},{10,2},{12,4},{14,6},{1,9},{3,11}... | collective-permute-start | bytes 208904 | tf_op jit(solution)/shard_map/ppermute | solution.py:682
  38.6 1.4 %collective-permute-start.14 = (f32[8,128]{1,0:T(8,128)S(1)}, f32[8,128]{1,0:T(8,128)S(1)}, u32[]{:S(2)}, u32[]{:S(2)}) collective-permute-start(f32[8,128]{1,0:T(8,128)S(1)} %get-tuple-element.111.mine_ref), channel_id=1, source_target_pairs={{0,1},{1,0},{2,3},{3,2},{4,5},{5,4},{6,7},{7,6},{8,9},{9,8},{10,11... | collective-permute-start | bytes 12296 | tf_op jit(solution)/shard_map/ppermute | solution.py:749
  (6 other events, 62.3 us)

commit v7 on v5

--- a/solution.py
+++ b/solution.py
@@ -11,7 +11,7 @@
 P_SIZE = 64
 LANES = 128
 AUX = 16
-BLOCK = 16
+BLOCK = 32
 QUAD = 4
 COPIES = 8
 INFO = 8
@@ -276,15 +276,11 @@
     values = jnp.concatenate(
         [jnp.concatenate(low_group, 1), jnp.concatenate(high_group, 1)], 0
     )
-    high = values.astype(jnp.bfloat16)
-    rest = values - high.astype(jnp.float32)
-    middle = rest.astype(jnp.bfloat16)
-    low = (rest - middle.astype(jnp.float32)).astype(jnp.bfloat16)
     heads = values.shape[0]
     out = jnp.dot(
-        jnp.concatenate([high, middle, low], 0), perm_ref[...], preferred_element_type=jnp.float32
-    )
-    return out[:heads] + out[heads : 2 * heads] + out[2 * heads :]
+        jnp.concatenate(split(values), 0), perm_ref[...], preferred_element_type=jnp.float32
+    )
+    return out[:heads] + out[heads:]
 
 
 def gated_steps(mixed, scale, xs, bs, cs, dec, dts, skip, gate, mixed_ref):
@@ -445,10 +441,19 @@
     ]
 
 
+def make_ready(gated, norm_ref, rows_ref, ready_ref):
+    blocks = norm_ref.shape[0]
+    steps = len(gated)
+    for t in range(steps):
+        rows_ref[t * blocks : (t + 1) * blocks, :] = gated[t] * norm_ref[...]
+    for b in range(blocks):
+        ready_ref[:, b * LANES : (b + 1) * LANES] = rows_ref[pl.ds(b, steps, stride=blocks), :]
+
+
 def kept_kernel(
     info_ref, state_ref, cx_ref, cb_ref, x_ref, bc_ref, gate_ref, dec_ref, dt_ref, skip_ref,
-    wx_ref, bx_ref, wb_ref, bb_ref, perm_ref, wide_ref, place_ref,
-    out_hbm, gated_ref, sums_ref, spread_ref, mixed_ref, turn_ref, rows_ref, new_ref, sems,
+    wx_ref, bx_ref, wb_ref, bb_ref, perm_ref, wide_ref, place_ref, norm_ref,
+    out_hbm, ready_ref, sums_ref, spread_ref, mixed_ref, turn_ref, rows_ref, new_ref, sems,
 ):
     steps = bc_ref.shape[1]
     blocks = bx_ref.shape[0]
@@ -477,8 +482,7 @@
     spread = spread_x(xs, dec, dts, spread_ref)
     new_state(tile, lambda j: j, wide_ref[slot], spread, bs, place_ref, write)
     copies = copy_rows(new_ref, out_hbm.at[slot], sems, 0, COPIES)
-    for t in range(steps):
-        gated_ref[t] = gated[t]
+    make_ready(gated, norm_ref, mixed_ref, ready_ref)
     sums_ref[...] = jnp.concatenate(sums, 0)
     for copy in copies:
         copy.wait()
@@ -559,7 +563,7 @@
     pieces = len(masks)
     got_refs = refs[:pieces]
     (
-        spread_ref, b_ref, wide_ref, place_ref, kept_ref, moved_ref, norm_ref,
+        spread_ref, b_ref, wide_ref, place_ref, moved_ref, norm_ref,
         new_ref, ready_ref, rows_ref,
     ) = refs[pieces:]
     full, me = info_ref[4] > 0, info_ref[5]
@@ -571,28 +575,22 @@
 
     bs = [b_ref[t] for t in range(b_ref.shape[0])]
     new_state(tile, first, wide_ref[...], spread_ref[...], bs, place_ref, write)
-    steps, blocks = kept_ref.shape[:2]
-    for which, ref in enumerate((kept_ref, moved_ref)):
-        for t in range(steps):
-            rows_ref[t * blocks : (t + 1) * blocks, :] = ref[t] * norm_ref[...]
-        for b in range(blocks):
-            ready_ref[which, :, b * LANES : (b + 1) * LANES] = rows_ref[
-                pl.ds(b, steps, stride=blocks), :
-            ]
+    gated = [moved_ref[t] for t in range(moved_ref.shape[0])]
+    make_ready(gated, norm_ref, rows_ref, ready_ref)
 
 
 def norm_kernel(
-    info_ref, held_hbm, new_ref, ready_ref, mine_ref, theirs_ref, out_hbm, y_hbm, y_ref, sems
+    info_ref, held_hbm, new_ref, kept_ref, moved_ref, mine_ref, theirs_ref, out_hbm, y_hbm, y_ref, sems
 ):
     del held_hbm
     copies = copy_rows(new_ref, out_hbm.at[info_ref[3]], sems, 0, COPIES)
-    steps = ready_ref.shape[1]
+    steps, channels = kept_ref.shape
     factor = lax.rsqrt((mine_ref[...] + theirs_ref[...]) * (1.0 / (H * P_SIZE)) + 1e-05)
-    for which in range(ready_ref.shape[0]):
+    for which, ready_ref in enumerate((kept_ref, moved_ref)):
         full = info_ref[2 + 2 * which] > 0
         rows = factor[which * steps : (which + 1) * steps]
-        for b in range(0, ready_ref.shape[2], LANES):
-            values = jnp.where(full, ready_ref[which, :, b : b + LANES] * rows, 0.0)
+        for b in range(0, channels, LANES):
+            values = jnp.where(full, ready_ref[:, b : b + LANES] * rows, 0.0)
             y_ref[info_ref[3 * which], :, b : b + LANES] = values.astype(jnp.bfloat16)
     copies.append(pltpu.make_async_copy(y_ref, y_hbm, sems.at[COPIES]))
     copies[-1].start()
@@ -735,16 +733,17 @@
     common = [x_dense, bc_late, gate, dec, dt_dense, skip, wx]
     common += [bx_late.reshape(blocks, LANES), wb_late, bb_late, perm, wide]
     scratch = [pltpu.VMEM((steps * heads, LANES), f32)] * 2 + [pltpu.VMEM((LANES, LANES), f32)]
-    held, kept_gated, kept_sums = call(
-        kept_kernel, "kept", [smem] + [vmem] * (4 + len(common)), [anywhere, vmem, vmem],
-        [shaped(places, heads, columns), shaped(steps, blocks, LANES), shaped(steps, LANES)],
+    norm_rows = norm_late.reshape(blocks, LANES)
+    held, kept_ready, kept_sums = call(
+        kept_kernel, "kept", [smem] + [vmem] * (5 + len(common)), [anywhere, vmem, vmem],
+        [shaped(places, heads, columns), shaped(steps, channels), shaped(steps, LANES)],
         scratch
         + [
             pltpu.VMEM((taps * blocks, LANES), f32),
             pltpu.VMEM((heads, columns), f32),
             pltpu.SemaphoreType.DMA((COPIES,)),
         ],
-    )(info, kept_state, cx_late, cb_late, *common, place)
+    )(info, kept_state, cx_late, cb_late, *common, place, norm_rows)
     moved_gated, sums, spread_rows, b_steps, wide_scaled = call(
         functools.partial(moved_kernel, masks), "moved",
         [smem] + [vmem] * (pieces + 1 + len(common)), [vmem] * 5,
@@ -756,17 +755,16 @@
         scratch + [pltpu.VMEM((max(aux_rows, pieces * AUX), LANES), f32)],
     )(info, *got, kept_sums, *common)
     theirs = lax.ppermute(sums, "tp", [(0, 1), (1, 0)])
-    new, ready = call(
+    new, moved_ready = call(
         functools.partial(state_kernel, masks), "state",
-        [smem] + [vmem] * (pieces + 7), [vmem] * 2,
-        [shaped(heads, columns), shaped(places, steps, channels)],
+        [smem] + [vmem] * (pieces + 6), [vmem] * 2,
+        [shaped(heads, columns), shaped(steps, channels)],
         [pltpu.VMEM((steps * blocks, LANES), f32)],
     )(
-        info, *got, spread_rows, b_steps, wide_scaled, place, kept_gated, moved_gated,
-        norm_late.reshape(blocks, LANES),
+        info, *got, spread_rows, b_steps, wide_scaled, place, moved_gated, norm_rows
     )
     new_ssm, y_out = call(
-        norm_kernel, "norm", [smem, anywhere] + [vmem] * 4, [anywhere, anywhere],
+        norm_kernel, "norm", [smem, anywhere] + [vmem] * 5, [anywhere, anywhere],
         [
             shaped(places, heads, columns),
             shaped(places, steps, channels, dtype=jnp.bfloat16),
@@ -776,7 +774,7 @@
             pltpu.SemaphoreType.DMA((COPIES + 1,)),
         ],
         input_output_aliases={1: 0},
-    )(info, held, new, ready, sums, theirs)
+    )(info, held, new, kept_ready, moved_ready, sums, theirs)
     return (y_out, new_ssm, jnp.transpose(convs[0], (1, 0, 2)), convs[1])
 
 

time: 40.3 us -> 40.3 us (level)
  no operation moved by 1% of the time
where the time goes in v7:
time: 40.3 us; the launch traced here: 40 us
  starting transfers between devices  23.7 us (59%)
  Pallas kernels  13.2 us (33%)
  waiting for transfers between devices  2.2 us (5%)
  between operations  0.87 us (2%)
    ppermute x14, starting transfers between devices, exchange(): out[i] = lax.ppermute(values[i], 'req', [(o, o ^ k) for o in range(owners)])  23.7 us
    pallas_call x1, Pallas kernels, on_device(): call(prep_kernel, 'prep', [smem] + [anywhere] * 6 + [vmem] * 5, [smem] +...  3.29 us
    pallas_call x1, Pallas kernels, on_device(): call(kept_kernel, 'kept', [smem] + [vmem] * (5 + len(common)), [anywhere,...  2.98 us
    ppermute x14, waiting for transfers between devices, exchange(): out[i] = lax.ppermute(values[i], 'req', [(o, o ^ k) for o in range(owners)])  2.2 us
    pallas_call x1, Pallas kernels, on_device(): call(functools.partial(pack_kernel, masks), 'pack', [smem] + [anywhere] *...  1.89 us
    pallas_call x1, Pallas kernels, on_device(): call(norm_kernel, 'norm', [smem, anywhere] + [vmem] * 5, [anywhere, anywh...  1.6 us
    pallas_call x1, Pallas kernels, on_device(): call(functools.partial(moved_kernel, masks), 'moved', [smem] + [vmem] * (...  1.53 us
    pallas_call x1, Pallas kernels, on_device(): call(functools.partial(state_kernel, masks), 'state', [smem] + [vmem] * (...  1.31 us
  transfers between devices with their start and end apart: 15, of which 4 were waited for; matrix products, arithmetic and copies ran while one was open for 0% of the time, Pallas kernels for 19%

profile of v7, /device:TPU:0, one launch (start us, length us, event | category | flops | bytes accessed | tf_op | source)
XLA Modules:
  0.0 40.0 jit_solution(14239339509538481065)
XLA Ops:
  0.7 1.9 %pack.1 = (s16[272,128]{1,0:T(8,128)(2,1)S(1)}, s16[272,128]{1,0:T(8,128)(2,1)S(1)}, s16[272,128]{1,0:T(8,128)(2,1)S(1)}, s16[272,128]{1,0:T(8,128)(2,1)S(1)}, s...) custom-call(s32[1]{0:T(128)} %bitcast.me_ref, ...), custom_call_target="tpu_custom_call" | custom-call | tf_op jit(solution)/shard_map/pack/pallas_call | solution.py:668
  2.6 5.1 %collective-permute-start = (s16[272,128]{1,0:T(8,128)(2,1)S(1)}, s16[272,128]{1,0:T(8,128)(2,1)S(1)}, u32[]{:S(2)}, u32[]{:S(2)}) collective-permute-start(s16[272,128]{1,0:T(8,128)(2,1)S(1)} %get-tuple-element.66), channel_id=1, source_target_pairs={{0,12},{2,14},{4,8},{6,10},{8,4},{10,6},{12,0},{14,2},{1,13},{3,15... | collective-permute-start | bytes 208904 | tf_op jit(solution)/shard_map/ppermute | solution.py:687
  7.8 1.5 %collective-permute-start.1 = (s16[272,128]{1,0:T(8,128)(2,1)S(1)}, s16[272,128]{1,0:T(8,128)(2,1)S(1)}, u32[]{:S(2)}, u32[]{:S(2)}) collective-permute-start(s16[272,128]{1,0:T(8,128)(2,1)S(1)} %get-tuple-element.67), channel_id=1, source_target_pairs={{0,2},{2,0},{4,6},{6,4},{8,10},{10,8},{12,14},{14,12},{1,3},{3,1},... | collective-permute-start | bytes 208904 | tf_op jit(solution)/shard_map/ppermute | solution.py:687
  9.2 0.0 collective-permute-start.2
  9.3 0.9 %collective-permute-start.3 = (s16[272,128]{1,0:T(8,128)(2,1)S(1)}, s16[272,128]{1,0:T(8,128)(2,1)S(1)}, u32[]{:S(2)}, u32[]{:S(2)}) collective-permute-start(s16[272,128]{1,0:T(8,128)(2,1)S(1)} %get-tuple-element.69), channel_id=1, source_target_pairs={{0,6},{2,4},{4,2},{6,0},{8,14},{10,12},{12,10},{14,8},{1,7},{3,5},... | collective-permute-start | bytes 208904 | tf_op jit(solution)/shard_map/ppermute | solution.py:687
  10.2 4.4 %collective-permute-start.4 = (s16[272,128]{1,0:T(8,128)(2,1)S(1)}, s16[272,128]{1,0:T(8,128)(2,1)S(1)}, u32[]{:S(2)}, u32[]{:S(2)}) collective-permute-start(s16[272,128]{1,0:T(8,128)(2,1)S(1)} %get-tuple-element.70), channel_id=1, source_target_pairs={{0,10},{2,8},{4,14},{6,12},{8,2},{10,0},{12,6},{14,4},{1,11},{3,9}... | collective-permute-start | bytes 208904 | tf_op jit(solution)/shard_map/ppermute | solution.py:687
  14.5 0.0 collective-permute-start.5
  14.5 0.6 %collective-permute-start.6 = (s16[272,128]{1,0:T(8,128)(2,1)S(1)}, s16[272,128]{1,0:T(8,128)(2,1)S(1)}, u32[]{:S(2)}, u32[]{:S(2)}) collective-permute-start(s16[272,128]{1,0:T(8,128)(2,1)S(1)} %get-tuple-element.72), channel_id=1, source_target_pairs={{0,8},{2,10},{4,12},{6,14},{8,0},{10,2},{12,4},{14,6},{1,9},{3,11}... | collective-permute-start | bytes 208904 | tf_op jit(solution)/shard_map/ppermute | solution.py:687
  15.2 3.3 %prep.1 = (s32[16]{0:T(128)S(1)}, f32[2,128,128]{2,1,0:T(8,128)S(1)}, f32[2,128,128]{2,1,0:T(8,128)S(1)}, f32[2,128,128]{2,1,0:T(8,128)S(1)}, f32[2,128,128]{2,1...) custom-call(s32[1]{0:T(128)} %bitcast.me_ref, ...), custom_call_target="tpu_custom_call" | custom-call | tf_op jit(solution)/shard_map/prep/pallas_call | solution.py:702
  18.5 0.6 %collective-permute-done.5.refs_6_ = s16[272,128]{1,0:T(8,128)(2,1)S(1)} collective-permute-done((s16[272,128]{1,0:T(8,128)(2,1)S(1)}, s16[272,128]{1,0:T(8,128)(2,1)S(1)}, u32[]{:S(2)}, u32[]{:S(2)}) %collective-permute-start.5) | collective-permute-done | bytes 69664 | tf_op jit(solution)/shard_map/ppermute | solution.py:687
  19.1 1.0 %collective-permute-done.6.refs_7_ = s16[272,128]{1,0:T(8,128)(2,1)S(1)} collective-permute-done((s16[272,128]{1,0:T(8,128)(2,1)S(1)}, s16[272,128]{1,0:T(8,128)(2,1)S(1)}, u32[]{:S(2)}, u32[]{:S(2)}) %collective-permute-start.6) | collective-permute-done | bytes 69664 | tf_op jit(solution)/shard_map/ppermute | solution.py:687
  20.1 0.6 %pick.1 = (s16[272,128]{1,0:T(8,128)(2,1)S(1)}, s16[272,128]{1,0:T(8,128)(2,1)S(1)}, s16[272,128]{1,0:T(8,128)(2,1)S(1)}, s16[272,128]{1,0:T(8,128)(2,1)S(1)}, s...) custom-call(s32[16]{0:T(128)S(1)} %get-tuple-element.74.info_ref, ...), custom_call_target="tpu_custom_call" | custom-call | tf_op jit(solution)/shard_map/pick/pallas_call | solution.py:726
  20.7 2.8 %collective-permute-start.7 = (s16[272,128]{1,0:T(8,128)(2,1)S(1)}, s16[272,128]{1,0:T(8,128)(2,1)S(1)}, u32[]{:S(2)}, u32[]{:S(2)}) collective-permute-start(s16[272,128]{1,0:T(8,128)(2,1)S(1)} %get-tuple-element.92), channel_id=1, source_target_pairs={{0,12},{2,14},{4,8},{6,10},{8,4},{10,6},{12,0},{14,2},{1,13},{3,15... | collective-permute-start | bytes 208904 | tf_op jit(solution)/shard_map/ppermute | solution.py:687
  23.5 1.4 %collective-permute-start.8 = (s16[272,128]{1,0:T(8,128)(2,1)S(1)}, s16[272,128]{1,0:T(8,128)(2,1)S(1)}, u32[]{:S(2)}, u32[]{:S(2)}) collective-permute-start(s16[272,128]{1,0:T(8,128)(2,1)S(1)} %get-tuple-element.93), channel_id=1, source_target_pairs={{0,2},{2,0},{4,6},{6,4},{8,10},{10,8},{12,14},{14,12},{1,3},{3,1},... | collective-permute-start | bytes 208904 | tf_op jit(solution)/shard_map/ppermute | solution.py:687
  24.9 1.2 %collective-permute-start.9 = (s16[272,128]{1,0:T(8,128)(2,1)S(1)}, s16[272,128]{1,0:T(8,128)(2,1)S(1)}, u32[]{:S(2)}, u32[]{:S(2)}) collective-permute-start(s16[272,128]{1,0:T(8,128)(2,1)S(1)} %get-tuple-element.94), channel_id=1, source_target_pairs={{0,14},{2,12},{4,10},{6,8},{8,6},{10,4},{12,2},{14,0},{1,15},{3,13... | collective-permute-start | bytes 208904 | tf_op jit(solution)/shard_map/ppermute | solution.py:687
  26.0 0.8 %collective-permute-start.10 = (s16[272,128]{1,0:T(8,128)(2,1)S(1)}, s16[272,128]{1,0:T(8,128)(2,1)S(1)}, u32[]{:S(2)}, u32[]{:S(2)}) collective-permute-start(s16[272,128]{1,0:T(8,128)(2,1)S(1)} %get-tuple-element.95), channel_id=1, source_target_pairs={{0,6},{2,4},{4,2},{6,0},{8,14},{10,12},{12,10},{14,8},{1,7},{3,5},... | collective-permute-start | bytes 208904 | tf_op jit(solution)/shard_map/ppermute | solution.py:687
  26.9 3.4 %collective-permute-start.11 = (s16[272,128]{1,0:T(8,128)(2,1)S(1)}, s16[272,128]{1,0:T(8,128)(2,1)S(1)}, u32[]{:S(2)}, u32[]{:S(2)}) collective-permute-start(s16[272,128]{1,0:T(8,128)(2,1)S(1)} %get-tuple-element.96), channel_id=1, source_target_pairs={{0,10},{2,8},{4,14},{6,12},{8,2},{10,0},{12,6},{14,4},{1,11},{3,9}... | collective-permute-start | bytes 208904 | tf_op jit(solution)/shard_map/ppermute | solution.py:687
  30.3 1.6 %collective-permute-start.13 = (s16[272,128]{1,0:T(8,128)(2,1)S(1)}, s16[272,128]{1,0:T(8,128)(2,1)S(1)}, u32[]{:S(2)}, u32[]{:S(2)}) collective-permute-start(s16[272,128]{1,0:T(8,128)(2,1)S(1)} %get-tuple-element.98), channel_id=1, source_target_pairs={{0,8},{2,10},{4,12},{6,14},{8,0},{10,2},{12,4},{14,6},{1,9},{3,11}... | collective-permute-start | bytes 208904 | tf_op jit(solution)/shard_map/ppermute | solution.py:687
  31.9 3.0 %kept.1 = (f32[2,64,4096]{2,1,0:T(8,128)}, f32[4,4096]{1,0:T(4,128)S(1)}, f32[4,128]{1,0:T(4,128)S(1)}) custom-call(s32[16]{0:T(128)S(1)} %get-tuple-element.74.info_ref, f32[64,4096]{1,0:T(8,128)S(1)} %get-tuple-element.75.state_ref, bf16[3,2,4096]{2,1,0:T(2,128)(2,1)S(1)} %bitcast.9, bf16[2,3,2,128]{3,2,1,0:T(2,128)(2,1)S(1)} %copy-done.5, ...), custom_call_target="tpu_custom_call" | custom-call | tf_op jit(solution)/shard_map/kept/pallas_call | solution.py:737
  34.9 0.4 %collective-permute-done.11.refs_5_ = s16[272,128]{1,0:T(8,128)(2,1)S(1)} collective-permute-done((s16[272,128]{1,0:T(8,128)(2,1)S(1)}, s16[272,128]{1,0:T(8,128)(2,1)S(1)}, u32[]{:S(2)}, u32[]{:S(2)}) %collective-permute-start.11) | collective-permute-done | bytes 69664 | tf_op jit(solution)/shard_map/ppermute | solution.py:687
  35.4 0.2 collective-permute-done.13.refs_7_
  35.6 1.5 %moved.1 = (f32[4,32,128]{2,1,0:T(8,128)S(1)}, f32[8,128]{1,0:T(8,128)S(1)}, bf16[256,256]{1,0:T(8,128)(2,1)S(1)}, f32[4,2,128]{2,1,0:T(2,128)S(1)}, f32[64,128]{1,0:T(8,128)S(1)}) custom-call(s32[16]{0:T(128)S(1)} %get-tuple-element.74.info_ref, s16[272,128]{1,0:T(8,128)(2,1)S(1)} %get-tuple-element.73.refs_0_, ...), custom_call_target="tpu_custom_call" | custom-call | tf_op jit(solution)/shard_map/moved/pallas_call | solution.py:747
  37.1 1.3 %state.1 = (f32[64,4096]{1,0:T(8,128)S(1)}, f32[4,4096]{1,0:T(4,128)S(1)}) custom-call(s32[16]{0:T(128)S(1)} %get-tuple-element.74.info_ref, s16[272,128]{1,0:T(8,128)(2,1)S(1)} %get-tuple-element.73.refs_0_, s16[272,128]{1,0:T(8,128)(2,1)S(1)} %collective-permute-done.7.refs_1_, s16[272,128]{1,0:T(8,128)(2,1)S(1)} %collective-permute-done.8.refs_2_, ...), custom_call_target="tpu_custom_call" | custom-call | tf_op jit(solution)/shard_map/state/pallas_call | solution.py:758
  38.4 1.6 %norm.1 = (f32[2,64,4096]{2,1,0:T(8,128)}, bf16[2,4,4096]{2,1,0:T(4,128)(2,1)}) custom-call(s32[16]{0:T(128)S(1)} %get-tuple-element.74.info_ref, f32[2,64,4096]{2,1,0:T(8,128)} %get-tuple-element.91.held_hbm, f32[64,4096]{1,0:T(8,128)S(1)} %get-tuple-element.104.new_ref, ...), custom_call_target="tpu_custom_call", output_to_operand_aliasing={{0}: (1, {})} | custom-call | tf_op jit(solution)/shard_map/norm/pallas_call | solution.py:766
  (35 shorter events, 0.1 us)
Async XLA Ops:
  0.6 14.5 %copy-start.10 = (f32[64]{0:T(128)S(1)}, f32[64]{0:T(128)}, u32[]{:S(2)}) copy-start(f32[64]{0:T(128)} %param.32) | copy-start | bytes 772
  0.6 14.5 %copy-start.9 = (f32[64]{0:T(128)S(1)}, f32[64]{0:T(128)}, u32[]{:S(2)}) copy-start(f32[64]{0:T(128)} %param.31) | copy-start | bytes 772
  0.7 14.5 %copy-start.8 = (f32[64]{0:T(128)S(1)}, f32[64]{0:T(128)}, u32[]{:S(2)}) copy-start(f32[64]{0:T(128)} %param.30) | copy-start | bytes 772
  0.7 31.2 %copy-start = (bf16[2,3,4096]{2,0,1:T(2,128)(2,1)S(1)}, bf16[2,3,4096]{2,0,1:T(2,128)(2,1)}, u32[]{:S(2)}) copy-start(bf16[2,3,4096]{2,0,1:T(2,128)(2,1)} %param.20) | copy-start | bytes 147460
  0.7 31.2 %copy-start.1 = (f32[4096]{0:T(1024)S(1)}, f32[4096]{0:T(1024)}, u32[]{:S(2)}) copy-start(f32[4096]{0:T(1024)} %param.27) | copy-start | bytes 49156
  0.7 31.2 %copy-start.2 = (f32[4096]{0:T(1024)S(1)}, f32[4096]{0:T(1024)}, u32[]{:S(2)}) copy-start(f32[4096]{0:T(1024)} %param.33) | copy-start | bytes 49156
  0.7 31.2 %copy-start.4 = (f32[4,2,128]{2,1,0:T(2,128)S(1)}, f32[4,2,128]{2,1,0:T(2,128)}, u32[]{:S(2)}) copy-start(f32[4,2,128]{2,1,0:T(2,128)} %refs_17_) | copy-start | bytes 12292
  0.7 31.2 %copy-start.5 = (bf16[2,3,2,128]{3,2,1,0:T(2,128)(2,1)S(1)}, bf16[2,3,2,128]{3,2,1,0:T(2,128)(2,1)}, u32[]{:S(2)}) copy-start(bf16[2,3,2,128]{3,2,1,0:T(2,128)(2,1)} %cb_ref) | copy-start | bytes 9220
  0.7 31.2 %copy-start.7 = (f32[2,128]{1,0:T(2,128)S(1)}, f32[2,128]{1,0:T(2,128)}, u32[]{:S(2)}) copy-start(f32[2,128]{1,0:T(2,128)} %refs_18_) | copy-start | bytes 3076
  2.6 11.9 %collective-permute-start = (s16[272,128]{1,0:T(8,128)(2,1)S(1)}, s16[272,128]{1,0:T(8,128)(2,1)S(1)}, u32[]{:S(2)}, u32[]{:S(2)}) collective-permute-start(s16[272,128]{1,0:T(8,128)(2,1)S(1)} %get-tuple-element.66), channel_id=1, source_target_pairs={{0,12},{2,14},{4,8},{6,10},{8,4},{10,6},{12,0},{14,2},{1,13},{3,15... | collective-permute-start | bytes 208904 | tf_op jit(solution)/shard_map/ppermute | solution.py:687
  7.8 6.8 %collective-permute-start.1 = (s16[272,128]{1,0:T(8,128)(2,1)S(1)}, s16[272,128]{1,0:T(8,128)(2,1)S(1)}, u32[]{:S(2)}, u32[]{:S(2)}) collective-permute-start(s16[272,128]{1,0:T(8,128)(2,1)S(1)} %get-tuple-element.67), channel_id=1, source_target_pairs={{0,2},{2,0},{4,6},{6,4},{8,10},{10,8},{12,14},{14,12},{1,3},{3,1},... | collective-permute-start | bytes 208904 | tf_op jit(solution)/shard_map/ppermute | solution.py:687
  9.2 9.2 %collective-permute-start.2 = (s16[272,128]{1,0:T(8,128)(2,1)S(1)}, s16[272,128]{1,0:T(8,128)(2,1)S(1)}, u32[]{:S(2)}, u32[]{:S(2)}) collective-permute-start(s16[272,128]{1,0:T(8,128)(2,1)S(1)} %get-tuple-element.68), channel_id=1, source_target_pairs={{0,14},{2,12},{4,10},{6,8},{8,6},{10,4},{12,2},{14,0},{1,15},{3,13... | collective-permute-start | bytes 208904 | tf_op jit(solution)/shard_map/ppermute | solution.py:687
  9.3 9.2 %collective-permute-start.3 = (s16[272,128]{1,0:T(8,128)(2,1)S(1)}, s16[272,128]{1,0:T(8,128)(2,1)S(1)}, u32[]{:S(2)}, u32[]{:S(2)}) collective-permute-start(s16[272,128]{1,0:T(8,128)(2,1)S(1)} %get-tuple-element.69), channel_id=1, source_target_pairs={{0,6},{2,4},{4,2},{6,0},{8,14},{10,12},{12,10},{14,8},{1,7},{3,5},... | collective-permute-start | bytes 208904 | tf_op jit(solution)/shard_map/ppermute | solution.py:687
  10.2 8.4 %collective-permute-start.4 = (s16[272,128]{1,0:T(8,128)(2,1)S(1)}, s16[272,128]{1,0:T(8,128)(2,1)S(1)}, u32[]{:S(2)}, u32[]{:S(2)}) collective-permute-start(s16[272,128]{1,0:T(8,128)(2,1)S(1)} %get-tuple-element.70), channel_id=1, source_target_pairs={{0,10},{2,8},{4,14},{6,12},{8,2},{10,0},{12,6},{14,4},{1,11},{3,9}... | collective-permute-start | bytes 208904 | tf_op jit(solution)/shard_map/ppermute | solution.py:687
  14.5 4.6 %collective-permute-start.5 = (s16[272,128]{1,0:T(8,128)(2,1)S(1)}, s16[272,128]{1,0:T(8,128)(2,1)S(1)}, u32[]{:S(2)}, u32[]{:S(2)}) collective-permute-start(s16[272,128]{1,0:T(8,128)(2,1)S(1)} %get-tuple-element.71), channel_id=1, source_target_pairs={{0,4},{2,6},{4,0},{6,2},{8,12},{10,14},{12,8},{14,10},{1,5},{3,7},... | collective-permute-start | bytes 208904 | tf_op jit(solution)/shard_map/ppermute | solution.py:687
  14.5 5.5 %collective-permute-start.6 = (s16[272,128]{1,0:T(8,128)(2,1)S(1)}, s16[272,128]{1,0:T(8,128)(2,1)S(1)}, u32[]{:S(2)}, u32[]{:S(2)}) collective-permute-start(s16[272,128]{1,0:T(8,128)(2,1)S(1)} %get-tuple-element.72), channel_id=1, source_target_pairs={{0,8},{2,10},{4,12},{6,14},{8,0},{10,2},{12,4},{14,6},{1,9},{3,11}... | collective-permute-start | bytes 208904 | tf_op jit(solution)/shard_map/ppermute | solution.py:687
  20.7 9.6 %collective-permute-start.7 = (s16[272,128]{1,0:T(8,128)(2,1)S(1)}, s16[272,128]{1,0:T(8,128)(2,1)S(1)}, u32[]{:S(2)}, u32[]{:S(2)}) collective-permute-start(s16[272,128]{1,0:T(8,128)(2,1)S(1)} %get-tuple-element.92), channel_id=1, source_target_pairs={{0,12},{2,14},{4,8},{6,10},{8,4},{10,6},{12,0},{14,2},{1,13},{3,15... | collective-permute-start | bytes 208904 | tf_op jit(solution)/shard_map/ppermute | solution.py:687
  23.5 6.8 %collective-permute-start.8 = (s16[272,128]{1,0:T(8,128)(2,1)S(1)}, s16[272,128]{1,0:T(8,128)(2,1)S(1)}, u32[]{:S(2)}, u32[]{:S(2)}) collective-permute-start(s16[272,128]{1,0:T(8,128)(2,1)S(1)} %get-tuple-element.93), channel_id=1, source_target_pairs={{0,2},{2,0},{4,6},{6,4},{8,10},{10,8},{12,14},{14,12},{1,3},{3,1},... | collective-permute-start | bytes 208904 | tf_op jit(solution)/shard_map/ppermute | solution.py:687
  24.9 10.0 %collective-permute-start.9 = (s16[272,128]{1,0:T(8,128)(2,1)S(1)}, s16[272,128]{1,0:T(8,128)(2,1)S(1)}, u32[]{:S(2)}, u32[]{:S(2)}) collective-permute-start(s16[272,128]{1,0:T(8,128)(2,1)S(1)} %get-tuple-element.94), channel_id=1, source_target_pairs={{0,14},{2,12},{4,10},{6,8},{8,6},{10,4},{12,2},{14,0},{1,15},{3,13... | collective-permute-start | bytes 208904 | tf_op jit(solution)/shard_map/ppermute | solution.py:687
  26.0 8.9 %collective-permute-start.10 = (s16[272,128]{1,0:T(8,128)(2,1)S(1)}, s16[272,128]{1,0:T(8,128)(2,1)S(1)}, u32[]{:S(2)}, u32[]{:S(2)}) collective-permute-start(s16[272,128]{1,0:T(8,128)(2,1)S(1)} %get-tuple-element.95), channel_id=1, source_target_pairs={{0,6},{2,4},{4,2},{6,0},{8,14},{10,12},{12,10},{14,8},{1,7},{3,5},... | collective-permute-start | bytes 208904 | tf_op jit(solution)/shard_map/ppermute | solution.py:687
  26.9 8.5 %collective-permute-start.11 = (s16[272,128]{1,0:T(8,128)(2,1)S(1)}, s16[272,128]{1,0:T(8,128)(2,1)S(1)}, u32[]{:S(2)}, u32[]{:S(2)}) collective-permute-start(s16[272,128]{1,0:T(8,128)(2,1)S(1)} %get-tuple-element.96), channel_id=1, source_target_pairs={{0,10},{2,8},{4,14},{6,12},{8,2},{10,0},{12,6},{14,4},{1,11},{3,9}... | collective-permute-start | bytes 208904 | tf_op jit(solution)/shard_map/ppermute | solution.py:687
  30.3 5.1 %collective-permute-start.12 = (s16[272,128]{1,0:T(8,128)(2,1)S(1)}, s16[272,128]{1,0:T(8,128)(2,1)S(1)}, u32[]{:S(2)}, u32[]{:S(2)}) collective-permute-start(s16[272,128]{1,0:T(8,128)(2,1)S(1)} %get-tuple-element.97), channel_id=1, source_target_pairs={{0,4},{2,6},{4,0},{6,2},{8,12},{10,14},{12,8},{14,10},{1,5},{3,7},... | collective-permute-start | bytes 208904 | tf_op jit(solution)/shard_map/ppermute | solution.py:687
  30.3 5.3 %collective-permute-start.13 = (s16[272,128]{1,0:T(8,128)(2,1)S(1)}, s16[272,128]{1,0:T(8,128)(2,1)S(1)}, u32[]{:S(2)}, u32[]{:S(2)}) collective-permute-start(s16[272,128]{1,0:T(8,128)(2,1)S(1)} %get-tuple-element.98), channel_id=1, source_target_pairs={{0,8},{2,10},{4,12},{6,14},{8,0},{10,2},{12,4},{14,6},{1,9},{3,11}... | collective-permute-start | bytes 208904 | tf_op jit(solution)/shard_map/ppermute | solution.py:687
  37.1 1.3 %collective-permute-start.14 = (f32[8,128]{1,0:T(8,128)S(1)}, f32[8,128]{1,0:T(8,128)S(1)}, u32[]{:S(2)}, u32[]{:S(2)}) collective-permute-start(f32[8,128]{1,0:T(8,128)S(1)} %get-tuple-element.107.mine_ref), channel_id=1, source_target_pairs={{0,1},{1,0},{2,3},{3,2},{4,5},{5,4},{6,7},{7,6},{8,9},{9,8},{10,11... | collective-permute-start | bytes 12296 | tf_op jit(solution)/shard_map/ppermute | solution.py:757
  (2 other events, 29.0 us)
